TPU v7x, 256 devices: a whole 4x4x8 slice. The times are simulated.
256 devices in a mesh: dp: 2 (over z_hi), seq: 16 (over x, y), fsdp: 8 (over z_lo, core).
Axes of the slice: x: 4, y: 4, z: 8 (z_hi: 2, z_lo: 4; z = z_hi * 4 + z_lo), core: 2. Of those that a mesh axis runs over, the one named last changes fastest.
Arguments:
- video: bfloat16 [16, 32, 128, 3072], P(('dp', 'fsdp'), 'seq'), may hold values from -6 to 6
- norm_gain: float32 [3072], replicated, may hold values from 0.5 to 1.5
- w_query: bfloat16 [3072, 1536], P(None, ('dp', 'fsdp')), may hold values from -0.109375 to 0.109375
- w_key: bfloat16 [3072, 1536], P(None, ('dp', 'fsdp')), may hold values from -0.109375 to 0.109375
- w_value: bfloat16 [3072, 1536], P(None, ('dp', 'fsdp')), may hold values from -0.109375 to 0.109375
- query_gain: float32 [128], replicated, may hold values from 0.1 to 1.9
- key_gain: float32 [128], replicated, may hold values from 0.1 to 1.9
Outputs:
- attended: bfloat16 [16, 32, 128, 1536], P(('dp', 'fsdp'), 'seq')
All inputs are finite; a program needn't handle non-finite values.
Results may differ from a plain program's by a relative error of at most 0.0089.
Values may be sent and summed in bfloat16 or wider, within the bound.
No kernel may reach another device: no remote copies, remote signals or barrier semaphores. Data moves between devices by JAX's collectives and lax.ppermute only.
A program may use at most 128 MiB of HBM per device.

v0:
```python
import jax
import jax.numpy as jnp
from jax import lax
from jax.sharding import PartitionSpec as P


def layer_normed(tokens, gain):
    values = tokens.astype(jnp.float32)
    average = jnp.mean(values, axis=-1, keepdims=True)
    centred = values - average
    spread = jnp.mean(centred * centred, axis=-1, keepdims=True)
    return (centred / jnp.sqrt(spread + 1e-06) * gain).astype(jnp.bfloat16)


def head_normed(rows, gain, head_dim):
    shaped = rows.astype(jnp.float32).reshape(
        rows.shape[:-1] + (rows.shape[-1] // head_dim, head_dim)
    )
    square = jnp.mean(shaped * shaped, axis=-1, keepdims=True)
    return shaped / jnp.sqrt(square + 1e-06) * gain


def attend(query_rows, key_rows, value_rows, query_gain, key_gain):
    head_dim = query_gain.shape[0]
    query_unit = head_normed(query_rows, query_gain, head_dim)
    key_unit = head_normed(key_rows, key_gain, head_dim)
    values_split = value_rows.astype(jnp.float32).reshape(query_unit.shape)
    scores = jnp.einsum(
        "vfphd,vgphd->vphfg", query_unit, key_unit, precision=lax.Precision.HIGHEST
    ) / jnp.sqrt(jnp.float32(head_dim))
    weights = jnp.exp(scores)
    probs = (weights / jnp.sum(weights, axis=-1, keepdims=True)).astype(jnp.bfloat16)
    output = jnp.einsum(
        "vphfg,vgphd->vfphd",
        probs.astype(jnp.float32),
        values_split,
        precision=lax.Precision.HIGHEST,
    )
    return output.reshape(query_rows.shape).astype(jnp.bfloat16)


def project(rows, w_query, w_key, w_value):
    flat = rows.reshape(-1, rows.shape[-1])

    def apply_columns(columns):
        return jnp.dot(flat, columns, preferred_element_type=jnp.float32).astype(jnp.bfloat16)

    query_rows = apply_columns(lax.all_gather(w_query, ("dp", "fsdp"), axis=1, tiled=True))
    key_rows = apply_columns(lax.all_gather(w_key, ("dp", "fsdp"), axis=1, tiled=True))
    value_rows = apply_columns(lax.all_gather(w_value, ("dp", "fsdp"), axis=1, tiled=True))
    shape_out = rows.shape[:-1] + (query_rows.shape[-1],)
    return (
        query_rows.reshape(shape_out),
        key_rows.reshape(shape_out),
        value_rows.reshape(shape_out),
    )


def shards(video, norm_gain, w_query, w_key, w_value, query_gain, key_gain):
    normed = layer_normed(video, norm_gain)
    query_local, key_local, value_local = project(normed, w_query, w_key, w_value)
    query_rows, key_rows, value_rows = (
        lax.all_to_all(query_local, "seq", split_axis=2, concat_axis=1, tiled=True),
        lax.all_to_all(key_local, "seq", split_axis=2, concat_axis=1, tiled=True),
        lax.all_to_all(value_local, "seq", split_axis=2, concat_axis=1, tiled=True),
    )
    output = attend(query_rows, key_rows, value_rows, query_gain, key_gain)
    return lax.all_to_all(output, "seq", split_axis=1, concat_axis=2, tiled=True)


def solution(mesh):
    in_specs = (
        P(("dp", "fsdp"), "seq", None, None),
        P(),
        P(None, ("dp", "fsdp")),
        P(None, ("dp", "fsdp")),
        P(None, ("dp", "fsdp")),
        P(),
        P(),
    )
    out_specs = P(("dp", "fsdp"), "seq", None, None)
    return jax.shard_map(shards, mesh=mesh, in_specs=in_specs, out_specs=out_specs, check_vma=False)
```

profile of v0, /device:TPU:8, one launch (start us, length us, event | category | flops | bytes accessed | tf_op | source)
XLA Modules:
  0.0 273.3 jit_solution(4331483067266405836)
XLA Ops:
  6.5 0.0 copy-start
  6.5 0.0 all-gather.6.cloned.1.call-start
  6.5 0.7 all-gather.6.cloned.1.call-update
  7.3 0.0 all-gather.8.cloned.1.call-start
  7.3 0.7 all-gather.8.cloned.1.call-update
  8.0 0.0 all-gather.4.cloned.1.call-start
  8.1 0.7 all-gather.4.cloned.1.call-update
  8.7 0.0 copy-done
  8.8 0.0 copy-start.4
  8.8 0.3 convert_reduce_fusion
  9.1 0.6 fusion.2
  9.6 0.0 copy-done.4
  9.6 0.7 fusion.4
  10.4 62.6 %all-gather.6.cloned.1.call-done = bf16[3072,1536]{0,1:T(8,128)(2,1)} async-done(((bf16[3072,96]{0,1:T(8,128)(2,1)}), bf16[3072,1536]{0,1:T(8,128)(2,1)}) %all-gather.6.cloned.1.call-update) | async-done | bytes 9437200 | tf_op jit(solution)/shard_map/all_gather | solution.py:48
  73.0 6.4 %convolution_convert_fusion.1 = bf16[256,1536]{1,0:T(8,128)(2,1)S(1)} fusion(bf16[256,3072]{1,0:T(8,128)(2,1)S(1)} %bitcast.59, bf16[3072,1536]{0,1:T(8,128)(2,1)} %all-gather.6.cloned.1.call-done), kind=kOutput, calls=%fused_computation.8 | convolution fusion | flops 2416312320 | bytes 11796480 | tf_op jit(solution)/shard_map/dot_general | solution.py:46
  79.3 1.7 copy.66
  81.0 7.3 %all-to-all-start.1 = ((bf16[1,2,128,1536]{3,1,0,2:T(2,128)(2,1)}), bf16[1,2,128,1536]{3,1,0,2:T(2,128)(2,1)S(1)}, u32[]{:S(2)}, u32[]{:S(2)}) async-start(bf16[1,2,128,1536]{3,1,0,2:T(2,128)(2,1)} %copy.66), calls=%async_computation.1 | async-start | bytes 1572864 | tf_op jit(solution)/shard_map/all_to_all | solution.py:63
  88.3 45.9 %all-gather.8.cloned.1.call-done = bf16[3072,1536]{0,1:T(8,128)(2,1)} async-done(((bf16[3072,96]{0,1:T(8,128)(2,1)}), bf16[3072,1536]{0,1:T(8,128)(2,1)}) %all-gather.8.cloned.1.call-update) | async-done | bytes 9437200 | tf_op jit(solution)/shard_map/all_gather | solution.py:49
  134.2 6.3 %convolution_convert_fusion = bf16[256,1536]{1,0:T(8,128)(2,1)S(1)} fusion(bf16[256,3072]{1,0:T(8,128)(2,1)S(1)} %bitcast.60, bf16[3072,1536]{0,1:T(8,128)(2,1)} %all-gather.8.cloned.1.call-done), kind=kOutput, calls=%fused_computation.7 | convolution fusion | flops 2416312320 | bytes 11796480 | tf_op jit(solution)/shard_map/dot_general | solution.py:46
  140.5 1.7 copy.72
  142.2 53.3 %all-gather.4.cloned.1.call-done = bf16[3072,1536]{0,1:T(8,128)(2,1)} async-done(((bf16[3072,96]{0,1:T(8,128)(2,1)}), bf16[3072,1536]{0,1:T(8,128)(2,1)}) %all-gather.4.cloned.1.call-update) | async-done | bytes 9437200 | tf_op jit(solution)/shard_map/all_gather | solution.py:50
  195.5 6.3 %convolution_convert_fusion.2 = bf16[256,1536]{1,0:T(8,128)(2,1)S(1)} fusion(bf16[256,3072]{1,0:T(8,128)(2,1)S(1)} %bitcast.61, bf16[3072,1536]{0,1:T(8,128)(2,1)} %all-gather.4.cloned.1.call-done), kind=kOutput, calls=%fused_computation.9 | convolution fusion | flops 2416312320 | bytes 11796480 | tf_op jit(solution)/shard_map/dot_general | solution.py:46
  201.8 1.7 copy.63
  203.5 0.0 all-to-all-done.1
  203.5 7.3 %all-to-all-start.2 = ((bf16[1,2,128,1536]{3,1,0,2:T(2,128)(2,1)}), bf16[1,2,128,1536]{3,1,0,2:T(2,128)(2,1)S(1)}, u32[]{:S(2)}, u32[]{:S(2)}) async-start(bf16[1,2,128,1536]{3,1,0,2:T(2,128)(2,1)} %copy.72), calls=%async_computation.2 | async-start | bytes 1572864 | tf_op jit(solution)/shard_map/all_to_all | solution.py:64
  210.7 0.2 fusion.5
  211.0 0.1 copy.69
  211.1 0.5 reduce_sum.47
  211.6 0.1 copy.70
  211.7 0.2 copy.71
  211.9 12.5 %all-to-all-done.2 = bf16[1,2,128,1536]{3,1,0,2:T(2,128)(2,1)S(1)} async-done(((bf16[1,2,128,1536]{3,1,0,2:T(2,128)(2,1)}), bf16[1,2,128,1536]{3,1,0,2:T(2,128)(2,1)S(1)}, u32[]{:S(2)}, u32[]{:S(2)}) %all-to-all-start.2) | async-done | bytes 786464 | tf_op jit(solution)/shard_map/all_to_all | solution.py:64
  224.4 5.5 %all-to-all-start = ((bf16[1,2,128,1536]{3,1,0,2:T(2,128)(2,1)}), bf16[1,2,128,1536]{3,1,0,2:T(2,128)(2,1)}, u32[]{:S(2)}, u32[]{:S(2)}) async-start(bf16[1,2,128,1536]{3,1,0,2:T(2,128)(2,1)} %copy.63), calls=%async_computation | async-start | bytes 1572864 | tf_op jit(solution)/shard_map/all_to_all | solution.py:65
  229.9 0.2 fusion.6
  230.1 0.1 copy.75
  230.3 1.2 reduce_sum.48
  231.4 1.1 copy.76
  232.5 0.2 convert_bitcast_fusion
  232.8 0.9 copy.77
  233.6 1.3 copy.74
  234.9 0.2 convert_bitcast_fusion.1
  235.1 0.1 copy.68
  235.2 0.0 copy-start.1
  235.3 0.0 copy-start.5
  235.3 0.0 copy-start.6
  235.3 6.1 %all-to-all-done = bf16[1,2,128,1536]{3,1,0,2:T(2,128)(2,1)} async-done(((bf16[1,2,128,1536]{3,1,0,2:T(2,128)(2,1)}), bf16[1,2,128,1536]{3,1,0,2:T(2,128)(2,1)}, u32[]{:S(2)}, u32[]{:S(2)}) %all-to-all-start) | async-done | bytes 786464 | tf_op jit(solution)/shard_map/all_to_all | solution.py:65
  241.4 0.0 copy-start.2
  241.4 1.3 copy.105
  242.7 1.0 copy.65
  243.6 0.0 copy-done.1
  243.6 0.0 copy-done.5
  243.7 0.0 copy-done.6
  243.7 0.0 copy-done.2
  243.7 1.1 divide_multiply_fusion
  244.8 0.0 copy-start.3
  244.8 4.3 %multiply_exponential_fusion = f32[8,12,32,32]{2,3,1,0:T(8,128)S(1)} fusion(f32[32,8,12,128]{3,1,2,0:T(8,128)S(1)} %get-tuple-element.5, f32[32,8,12,128]{3,1,2,0:T(8,128)S(1)} %get-tuple-element.6), kind=kOutput, calls=%fused_computation.20 | convolution fusion | flops 151093248 | bytes 3538944 | tf_op jit(solution)/shard_map/vfphd,vgphd->vphfg/dot_general | solution.py:28
  249.1 0.0 copy-done.3
  249.1 0.7 fusion.14
  249.8 0.5 copy.104
  250.3 15.6 %all_to_all.51 = bf16[1,32,8,1536]{3,2,0,1:T(8,128)(2,1)S(1)} all-to-all(bf16[1,32,8,1536]{3,2,0,1:T(8,128)(2,1)S(1)} %bitcast.57), channel_id=1, replica_groups=mesh['dp'=2,'seq'=16,'fsdp'=8] {'seq'}, dimensions={1} | all-to-all | bytes 1572864 | tf_op jit(solution)/shard_map/all_to_all | solution.py:68
  265.9 0.9 copy.103
  (4 shorter events, 0.1 us)
Async XLA Ops:
  6.5 2.2 copy-start
  6.5 66.4 %all-gather.6.cloned.1.call-start = ((), (), s32[]{:S(2)}) async-start(), calls=%async_computation.5 | async-start | bytes 10027008 | tf_op jit(solution)/shard_map/all_gather | solution.py:48
  7.3 127.0 %all-gather.8.cloned.1.call-start = ((), (), s32[]{:S(2)}) async-start(), calls=%async_computation.6 | async-start | bytes 10027008 | tf_op jit(solution)/shard_map/all_gather | solution.py:49
  8.0 187.5 %all-gather.4.cloned.1.call-start = ((), (), s32[]{:S(2)}) async-start(), calls=%async_computation.4 | async-start | bytes 10027008 | tf_op jit(solution)/shard_map/all_gather | solution.py:50
  8.8 0.9 copy-start.4
  81.0 122.5 %all-to-all-start.1 = ((bf16[1,2,128,1536]{3,1,0,2:T(2,128)(2,1)}), bf16[1,2,128,1536]{3,1,0,2:T(2,128)(2,1)S(1)}, u32[]{:S(2)}, u32[]{:S(2)}) async-start(bf16[1,2,128,1536]{3,1,0,2:T(2,128)(2,1)} %copy.66), calls=%async_computation.1 | async-start | bytes 1572864 | tf_op jit(solution)/shard_map/all_to_all | solution.py:63
  203.5 20.9 %all-to-all-start.2 = ((bf16[1,2,128,1536]{3,1,0,2:T(2,128)(2,1)}), bf16[1,2,128,1536]{3,1,0,2:T(2,128)(2,1)S(1)}, u32[]{:S(2)}, u32[]{:S(2)}) async-start(bf16[1,2,128,1536]{3,1,0,2:T(2,128)(2,1)} %copy.72), calls=%async_computation.2 | async-start | bytes 1572864 | tf_op jit(solution)/shard_map/all_to_all | solution.py:64
  224.4 17.0 %all-to-all-start = ((bf16[1,2,128,1536]{3,1,0,2:T(2,128)(2,1)}), bf16[1,2,128,1536]{3,1,0,2:T(2,128)(2,1)}, u32[]{:S(2)}, u32[]{:S(2)}) async-start(bf16[1,2,128,1536]{3,1,0,2:T(2,128)(2,1)} %copy.63), calls=%async_computation | async-start | bytes 1572864 | tf_op jit(solution)/shard_map/all_to_all | solution.py:65
  235.2 8.4 %copy-start.1 = (f32[1,16,2,8,1536]{4,3,2,1,0:T(8,128)S(1)}, f32[1,16,2,8,1536]{4,3,2,1,0:T(8,128)}, u32[]{:S(2)}) copy-start(f32[1,16,2,8,1536]{4,3,2,1,0:T(8,128)} %copy.74) | copy-start | bytes 4718596
  235.3 8.4 %copy-start.5 = (f32[128]{0:T(128)S(1)}, f32[128]{0:T(128)}, u32[]{:S(2)}) copy-start(f32[128]{0:T(128)} %param.13) | copy-start | bytes 1540
  235.3 8.4 %copy-start.6 = (f32[128]{0:T(128)S(1)}, f32[128]{0:T(128)}, u32[]{:S(2)}) copy-start(f32[128]{0:T(128)} %param.12) | copy-start | bytes 1540
  241.4 2.2 copy-start.2
  244.8 4.3 %copy-start.3 = (bf16[1,16,2,8,1536]{4,3,2,1,0:T(8,128)(2,1)S(1)}, bf16[1,16,2,8,1536]{4,3,2,1,0:T(8,128)(2,1)}, u32[]{:S(2)}) copy-start(bf16[1,16,2,8,1536]{4,3,2,1,0:T(8,128)(2,1)} %copy.65) | copy-start | bytes 2359300
Sparse Core Ops, SparseCore 0:
  9.2 63.7 all-gather.5
  74.8 59.3 all-gather.7
  136.0 59.3 all-gather.3
where the time goes:
time: 274 us; the launch traced here: 273 us
  waiting for transfers between devices  183 us (67%)
  matrix products  24 us (9%)
  starting transfers between devices  20.1 us (7%)
  blocking collectives  15.6 us (6%)
  between operations  13.3 us (5%)
  local copies, waits for them, and re-layouts  12.7 us (5%)
  other arithmetic  5.24 us (2%)
    all_gather x1, waiting for transfers between devices, project(): lax.all_gather(w_query, ('dp', 'fsdp'), axis=1, tiled=True)  62.6 us
    all_gather x1, waiting for transfers between devices, project(): lax.all_gather(w_value, ('dp', 'fsdp'), axis=1, tiled=True)  53.3 us
    all_gather x1, waiting for transfers between devices, project(): lax.all_gather(w_key, ('dp', 'fsdp'), axis=1, tiled=True)  45.9 us
    dot_general x3, matrix products, apply_columns(): jnp.dot(flat, columns, preferred_element_type=jnp.float32)  19 us
    all_to_all x1, blocking collectives, shards(): lax.all_to_all(output, 'seq', split_axis=1, concat_axis=2, tiled=True)  15.6 us
    all_to_all x1, waiting for transfers between devices, shards(): lax.all_to_all(key_local, 'seq', split_axis=2, concat_axis=1, tiled=True)  12.5 us
    all_to_all x1, starting transfers between devices, shards(): lax.all_to_all(query_local, 'seq', split_axis=2, concat_axis=1, tiled=True)  7.26 us
    all_to_all x1, starting transfers between devices, shards(): lax.all_to_all(key_local, 'seq', split_axis=2, concat_axis=1, tiled=True)  7.26 us
  transfers between devices with their start and end apart: 6, of which 5 were waited for; matrix products, arithmetic and copies ran while one was open for 12% of the time, Pallas kernels for 0%

commit v1 on v0

v1 whole, which is shorter than its diff:
```python
import jax
import jax.numpy as jnp
from jax import lax
from jax.experimental import pallas as pl
from jax.experimental.pallas import tpu as pltpu
from jax.sharding import PartitionSpec as P

AXES = ("dp", "seq", "fsdp")
SHIFTS = (0, 1, 3, 2)


def place(x, y, z, core):
    return ((z // 4) * 16 + x * 4 + y) * 8 + (z % 4) * 2 + core


def every_place():
    return [(x, y, z, c) for x in range(4) for y in range(4) for z in range(8) for c in range(2)]


def scatter_perm(shift):
    pairs = []
    for x in range(4):
        for y in range(4):
            j = (x + y) % 4
            for a in range(2):
                for c in range(2):
                    z = 2 * j + a
                    pairs.append((place(x, y, z, c), place(x, y, (z + 2 * shift) % 8, c)))
    return pairs


def line_perm(shift):
    pairs = []
    for x, y, z, c in every_place():
        to = ((x + shift) % 4, y) if c == 0 else (x, (y + shift) % 4)
        pairs.append((place(x, y, z, c), place(to[0], to[1], z, c)))
    return pairs


def norm_kernel(video_ref, gain_ref, out_ref):
    values = video_ref[0].astype(jnp.float32)
    average = jnp.mean(values, axis=-1, keepdims=True)
    centred = values - average
    spread = jnp.mean(centred * centred, axis=-1, keepdims=True)
    normed = centred * lax.rsqrt(spread + 1e-06) * gain_ref[...][None]
    for s in range(out_ref.shape[0]):
        part = [normed[f, 8 * s : 8 * s + 8] for f in range(2)]
        out_ref[s] = jnp.concatenate(part, axis=0).astype(jnp.bfloat16)


def layer_normed(video, gain):
    d = video.shape[-1]
    steps = 4
    return pl.pallas_call(
        norm_kernel,
        grid=(steps,),
        in_specs=[
            pl.BlockSpec((1, 2, 128 // steps, d), lambda i: (0, 0, i, 0)),
            pl.BlockSpec((1, d), lambda i: (0, 0)),
        ],
        out_specs=pl.BlockSpec((16 // steps, 16, d), lambda i: (i, 0, 0)),
        out_shape=jax.ShapeDtypeStruct((16, 16, d), jnp.bfloat16),
        compiler_params=pltpu.CompilerParams(vmem_limit_bytes=40 * 2**20),
        name="norm_rows",
    )(video, gain.reshape(1, d))


NT = (((1,), (1,)), ((), ()))


def attend_kernel(group_ref, r0, r1, r2, r3, w_ref, qg_ref, kg_ref, out_ref, rows, weights, acc):
    t = pl.program_id(0)
    for i, ref in enumerate((r0, r1, r2, r3)):
        rows[256 * i : 256 * i + 256, :] = ref[...]
    for m in range(3):
        for blk in range(4):
            at = 384 * m + 96 * blk
            weights[at : at + 96, :] = w_ref[0, blk, 96 * m : 96 * m + 96, :]
    product = lax.dot_general(rows[...], weights[...], NT, preferred_element_type=jnp.float32)

    @pl.when(t == 0)
    def _():
        acc[...] = product

    @pl.when(t > 0)
    def _():
        acc[...] += product

    @pl.when(t == pl.num_programs(0) - 1)
    def _():
        gains = qg_ref[...] * kg_ref[...] * (128.0**-0.5)
        row_patch = lax.broadcasted_iota(jnp.int32, (256, 256), 0) % 8
        col_patch = lax.broadcasted_iota(jnp.int32, (256, 256), 1) % 8
        same = row_patch == col_patch
        for i in range(4):
            for h in range(3):
                part = acc[256 * i : 256 * i + 256, :]
                q_rows = part[:, 128 * h : 128 * h + 128].astype(jnp.bfloat16)
                k = part[:, 384 + 128 * h : 512 + 128 * h].astype(jnp.bfloat16).astype(jnp.float32)
                v = part[:, 768 + 128 * h : 896 + 128 * h].astype(jnp.bfloat16)
                q = q_rows.astype(jnp.float32)
                q_scale = lax.rsqrt(jnp.mean(q * q, axis=-1, keepdims=True) + 1e-06)
                k_scale = lax.rsqrt(jnp.mean(k * k, axis=-1, keepdims=True) + 1e-06)
                k_unit = (k * k_scale * gains).astype(jnp.bfloat16)
                scores = lax.dot_general(q_rows, k_unit, NT, preferred_element_type=jnp.float32)
                exps = jnp.where(same, jnp.exp(scores * q_scale), 0.0)
                probs = (exps / jnp.sum(exps, axis=-1, keepdims=True)).astype(jnp.bfloat16)
                out = jnp.dot(probs, v, preferred_element_type=jnp.float32).astype(jnp.bfloat16)
                out_ref[:, 16 * i : 16 * i + 16, 128 * h : 128 * h + 128] = out.reshape(16, 16, 128)


def attend(pieces, gathered, group, query_gain, key_gain):
    d = pieces[0].shape[-1]
    quarter = d // 4
    spec = pl.BlockSpec((256, quarter), lambda t, g: (0, (t - g[0] + 4) % 4))
    gain_spec = pl.BlockSpec((1, 128), lambda t, g: (0, 0))
    return pl.pallas_call(
        attend_kernel,
        grid_spec=pltpu.PrefetchScalarGridSpec(
            num_scalar_prefetch=1,
            grid=(4,),
            in_specs=[spec] * 4
            + [pl.BlockSpec((1, 4, 288, quarter), lambda t, g: (t, 0, 0, 0)), gain_spec, gain_spec],
            out_specs=pl.BlockSpec((16, 64, 384), lambda t, g: (0, 0, 0)),
            scratch_shapes=[
                pltpu.VMEM((1024, quarter), jnp.bfloat16),
                pltpu.VMEM((1152, quarter), jnp.bfloat16),
                pltpu.VMEM((1024, 1152), jnp.float32),
            ],
        ),
        out_shape=jax.ShapeDtypeStruct((16, 64, 384), jnp.bfloat16),
        compiler_params=pltpu.CompilerParams(vmem_limit_bytes=50 * 2**20),
        name="project_attend",
    )(group, *pieces, gathered, query_gain.reshape(1, 128), key_gain.reshape(1, 128))


def sources(core):
    found = {}
    for x in range(4):
        for y in range(4):
            for piece, shift in enumerate(SHIFTS):
                s = ((x - shift) % 4) * 4 + y if core == 0 else x * 4 + (y - shift) % 4
                found[s, (x + y) % 4] = (4 * x + y, piece)
    return found


def assemble_kernel(core_ref, recv_ref, out_ref):
    for core in range(2):

        @pl.when(core_ref[0] == core)
        def _(found=sources(core)):
            for s in range(0, 16, 2):
                for j in range(4):
                    src, piece = found[s, j]
                    low = recv_ref[src, 16 * piece : 16 * piece + 16, :].astype(jnp.float32)
                    src, piece = found[s + 1, j]
                    high = recv_ref[src, 16 * piece : 16 * piece + 16, :].astype(jnp.float32)
                    for f in range(2):
                        both = jnp.concatenate([low[8 * f : 8 * f + 8], high[8 * f : 8 * f + 8]], axis=0)
                        out_ref[0, f, 8 * s : 8 * s + 16, 384 * j : 384 * j + 384] = both.astype(jnp.bfloat16)


def assemble(received, core):
    return pl.pallas_call(
        assemble_kernel,
        in_specs=[pl.BlockSpec(memory_space=pltpu.SMEM), pl.BlockSpec(memory_space=pltpu.VMEM)],
        out_specs=pl.BlockSpec(memory_space=pltpu.VMEM),
        out_shape=jax.ShapeDtypeStruct((1, 2, 128, 1536), jnp.bfloat16),
        compiler_params=pltpu.CompilerParams(vmem_limit_bytes=40 * 2**20),
        name="assemble_heads",
    )(core, received)


def shards(video, norm_gain, w_query, w_key, w_value, query_gain, key_gain):
    seq = lax.axis_index("seq")
    fsdp = lax.axis_index("fsdp")
    pair = lax.axis_index("dp") * 2 + fsdp // 4
    core = (fsdp % 2).astype(jnp.int32).reshape(1)
    group = (seq // 4 + seq % 4) % 4
    d = video.shape[-1]
    quarter = d // 4

    columns = [w.T for w in (w_query, w_key, w_value)]
    quarters = [
        jnp.concatenate([c[:, quarter * r : quarter * (r + 1)] for c in columns], axis=0) for r in range(4)
    ]
    with jax.named_scope("scatter"):
        mine = [quarters[0]] + [lax.ppermute(quarters[r], AXES, scatter_perm(r)) for r in (1, 3, 2)]
    part = lax.select_n((pair - group + 4) % 4, mine[0], mine[1], mine[3], mine[2])
    gathered = lax.all_gather(part, ("dp", "fsdp"), axis=0, tiled=True)
    gathered = gathered.reshape(4, 4, 288, quarter)

    normed = layer_normed(video, norm_gain)
    with jax.named_scope("rows_home"):
        home = lax.all_to_all(normed, "seq", split_axis=0, concat_axis=0, tiled=True).reshape(256, d)
    with jax.named_scope("rows_line"):
        pieces = [home] + [lax.ppermute(home, AXES, line_perm(s)) for s in SHIFTS[1:]]
    output = attend(pieces, gathered, group.astype(jnp.int32).reshape(1), query_gain, key_gain)
    with jax.named_scope("heads_back"):
        received = lax.all_to_all(output, "seq", split_axis=0, concat_axis=0, tiled=True)
    return assemble(received, core)


def solution(mesh):
    in_specs = (
        P(("dp", "fsdp"), "seq", None, None),
        P(),
        P(None, ("dp", "fsdp")),
        P(None, ("dp", "fsdp")),
        P(None, ("dp", "fsdp")),
        P(),
        P(),
    )
    out_specs = P(("dp", "fsdp"), "seq", None, None)
    return jax.shard_map(shards, mesh=mesh, in_specs=in_specs, out_specs=out_specs, check_vma=False)
```

time: 274 us -> 161 us (0.59)
  waiting for transfers between devices: 183 us -> 82.4 us
  matrix products: 24 us -> 0 us
  Pallas kernels: 0 us -> 17.8 us
  blocking collectives: 15.6 us -> 28.2 us
  local copies, waits for them, and re-layouts: 12.7 us -> 2.87 us
  starting transfers between devices: 20.1 us -> 13.5 us
  other arithmetic: 5.24 us -> 2.24 us
    all_gather x3 -> x1, waiting for transfers between devices: 162 us -> 0.01 us  [shards(): gathered = lax.all_gather(part, ('dp', 'fsdp'), axis=0, tiled=True)]
    ppermute x0 -> x6, waiting for transfers between devices: none -> 71.4 us  [the longest x3 37 us: shards(): lax.ppermute(quarters[r], AXES, scatter_perm(r))]
    dot_general x5 -> x0, matrix products: 24 us -> none  [the longest x3 19 us: apply_columns(): jnp.dot(flat, columns, preferred_element_type=jnp.float32)]
    pallas_call x0 -> x3, Pallas kernels: none -> 17.8 us  [the longest x1 15.4 us: attend(): pl.pallas_call(attend_kernel, grid_spec=pltpu.PrefetchScalarGridSpec(num_...]
    all_to_all x3 -> x1, starting transfers between devices: 20 us -> 5.89 us  [shards(): lax.all_to_all(output, 'seq', split_axis=0, concat_axis=0, tiled=True)]
    all_to_all x1, blocking collectives: 15.6 us -> 28.2 us  [shards(): lax.all_to_all(normed, 'seq', split_axis=0, concat_axis=0, tiled=True)]
    all_to_all x3 -> x1, waiting for transfers between devices: 18.6 us -> 11 us  [shards(): lax.all_to_all(output, 'seq', split_axis=0, concat_axis=0, tiled=True)]
    ppermute x0 -> x6, starting transfers between devices: none -> 7.64 us  [the longest x3 4.27 us: shards(): lax.ppermute(quarters[r], AXES, scatter_perm(r))]
  transfers between devices with their start and end apart: 6 -> 8, of which waited for: 5 -> 4; matrix products, arithmetic and copies ran while one was open for 12% -> 0% of each run, Pallas kernels for 0% -> 1%
where the time goes in v1:
time: 161 us
  waiting for transfers between devices  82.4 us (51%)
  blocking collectives  28.2 us (18%)
  Pallas kernels  17.8 us (11%)
  between operations  13.6 us (8%)
  starting transfers between devices  13.5 us (8%)
  local copies, waits for them, and re-layouts  2.87 us (2%)
  other arithmetic  2.24 us (1%)
    ppermute x3, waiting for transfers between devices, shards(): lax.ppermute(quarters[r], AXES, scatter_perm(r))  37 us
    ppermute x3, waiting for transfers between devices, shards(): lax.ppermute(home, AXES, line_perm(s))  34.4 us
    all_to_all x1, blocking collectives, shards(): lax.all_to_all(normed, 'seq', split_axis=0, concat_axis=0, tiled=True)  28.2 us
    pallas_call x1, Pallas kernels, attend(): pl.pallas_call(attend_kernel, grid_spec=pltpu.PrefetchScalarGridSpec(num_...  15.4 us
    all_to_all x1, waiting for transfers between devices, shards(): lax.all_to_all(output, 'seq', split_axis=0, concat_axis=0, tiled=True)  11 us
    all_to_all x1, starting transfers between devices, shards(): lax.all_to_all(output, 'seq', split_axis=0, concat_axis=0, tiled=True)  5.89 us
    ppermute x3, starting transfers between devices, shards(): lax.ppermute(quarters[r], AXES, scatter_perm(r))  4.27 us
    ppermute x3, starting transfers between devices, shards(): lax.ppermute(home, AXES, line_perm(s))  3.37 us
  transfers between devices with their start and end apart: 8, of which 4 were waited for; matrix products, arithmetic and copies ran while one was open for 0% of the time, Pallas kernels for 1%

profile of v1, /device:TPU:8, one launch (start us, length us, event | category | flops | bytes accessed | tf_op | source)
XLA Modules:
  0.0 160.6 jit_solution(1119206348274306701)
XLA Ops:
  6.5 0.0 copy-start.7
  6.5 0.0 copy-start.6
  6.5 0.0 all-gather.2.cloned.1.call-start
  6.5 1.3 fusion.3
  7.8 0.1 copy-done.7
  7.9 0.2 copy-done.6
  8.1 0.1 fusion.1
  8.2 1.4 collective-permute-start.3
  9.7 1.4 collective-permute-start.4
  11.1 0.0 copy-start
  11.1 0.0 copy-start.1
  11.1 1.4 collective-permute-start.5
  12.6 0.0 collective-permute-done.3
  12.6 0.0 collective-permute-done.4
  12.7 37.0 %collective-permute-done.5 = bf16[288,768]{1,0:T(8,128)(2,1)} collective-permute-done((bf16[288,768]{1,0:T(8,128)(2,1)S(1)}, bf16[288,768]{1,0:T(8,128)(2,1)}, u32[]{:S(2)}, u32[]{:S(2)}) %collective-permute-start.5) | collective-permute-done | bytes 442400 | tf_op jit(solution)/shard_map/scatter/ppermute | solution.py:188
  49.6 2.1 %fusion = bf16[288,768]{1,0:T(8,128)(2,1)} fusion(bf16[288,768]{1,0:T(8,128)(2,1)} %collective-permute-done.3, bf16[96,768]{1,0:T(8,128)(2,1)S(1)} %get-tuple-element.16, bf16[96,768]{1,0:T(8,128)(2,1)S(1)} %get-tuple-element.17, bf16[96,768]{1,0:T(8,128)(2,1)S(1)} %get-tuple-element.8, bf16[288,768]{1,0:T(8,128)(2,1)} %collective-permute-done.4, ...), kind=kLoop, calls=%fused_computation.1 | loop fusion | flops 1990656 | bytes 2211843 | tf_op jit(solution)/shard_map/select_n | solution.py:189
  51.8 0.0 all-gather.2.cloned.1.call-update
  51.8 0.0 copy-done
  51.8 0.0 copy-done.1
  51.8 1.5 norm_rows.1
  53.3 0.0 copy-start.2
  53.3 0.0 copy-start.3
  53.3 28.2 %all_to_all.10 = bf16[16,16,3072]{2,1,0:T(8,128)(2,1)S(1)} all-to-all(bf16[16,16,3072]{2,1,0:T(8,128)(2,1)S(1)} %norm_rows.1), channel_id=1, replica_groups=mesh['dp'=2,'seq'=16,'fsdp'=8] {'seq'}, dimensions={0} | all-to-all | bytes 3145728 | tf_op jit(solution)/shard_map/rows_home/all_to_all | solution.py:195
  81.5 1.3 collective-permute-start.2
  82.9 1.6 collective-permute-start.1
  84.4 0.4 collective-permute-start
  84.9 18.7 %collective-permute-done.2.r3 = bf16[256,3072]{1,0:T(8,128)(2,1)S(1)} collective-permute-done((bf16[256,3072]{1,0:T(8,128)(2,1)S(1)}, bf16[256,3072]{1,0:T(8,128)(2,1)S(1)}, u32[]{:S(2)}, u32[]{:S(2)}) %collective-permute-start.2) | collective-permute-done | bytes 1572896 | tf_op jit(solution)/shard_map/rows_line/ppermute | solution.py:197
  103.5 0.0 copy-start.4
  103.6 15.8 %collective-permute-done.1.r2 = bf16[256,3072]{1,0:T(8,128)(2,1)S(1)} collective-permute-done((bf16[256,3072]{1,0:T(8,128)(2,1)S(1)}, bf16[256,3072]{1,0:T(8,128)(2,1)S(1)}, u32[]{:S(2)}, u32[]{:S(2)}) %collective-permute-start.1) | collective-permute-done | bytes 1572896 | tf_op jit(solution)/shard_map/rows_line/ppermute | solution.py:197
  119.3 0.0 copy-done.4
  119.3 0.0 copy-start.5
  119.3 1.2 copy-done.5
  120.6 0.0 collective-permute-done.r1
  120.6 0.0 all-gather.2.cloned.1.call-done
  120.6 0.0 copy-done.2
  120.6 0.0 copy-done.3
  120.6 15.4 %project_attend.1 = bf16[16,64,384]{2,1,0:T(8,128)(2,1)} custom-call(s32[1]{0:T(128)} %bitcast.1.group_ref, bf16[256,3072]{1,0:T(8,128)(2,1)S(1)} %bitcast.13, bf16[256,3072]{1,0:T(8,128)(2,1)S(1)} %collective-permute-done.r1, bf16[256,3072]{1,0:T(8,128)(2,1)} %copy-done.5, bf16[256,3072]{1,0:T(8,128)(2,1)} %copy-done.4, bf16[4,4,288,768]{3,2,1,0:T(8,128)(2,1)} %bitcast.17, ...), custom_call_target="tpu_custom_call" | custom-call | tf_op jit(solution)/shard_map/project_attend/pallas_call | solution.py:117
  136.0 5.9 %all-to-all-start.1 = ((bf16[16,64,384]{2,1,0:T(8,128)(2,1)}), bf16[16,64,384]{2,1,0:T(8,128)(2,1)S(1)}, u32[]{:S(2)}, u32[]{:S(2)}) async-start(bf16[16,64,384]{2,1,0:T(8,128)(2,1)} %project_attend.1), calls=%async_computation.1 | async-start | bytes 1572864 | tf_op jit(solution)/shard_map/heads_back/all_to_all | solution.py:200
  141.8 11.0 %all-to-all-done.1.recv_ref = bf16[16,64,384]{2,1,0:T(8,128)(2,1)S(1)} async-done(((bf16[16,64,384]{2,1,0:T(8,128)(2,1)}), bf16[16,64,384]{2,1,0:T(8,128)(2,1)S(1)}, u32[]{:S(2)}, u32[]{:S(2)}) %all-to-all-start.1) | async-done | bytes 786464 | tf_op jit(solution)/shard_map/heads_back/all_to_all | solution.py:200
  152.8 1.0 assemble_heads.1
  (3 shorter events, 0.1 us)
Async XLA Ops:
  6.5 1.4 copy-start.7
  6.5 1.5 copy-start.6
  6.5 114.0 %all-gather.2.cloned.1.call-start = ((), (), s32[]{:S(2)}) async-start(), calls=%async_computation.2 | async-start | bytes 7520256 | tf_op jit(solution)/shard_map/all_gather | solution.py:190
  8.2 4.4 %collective-permute-start.3 = (bf16[288,768]{1,0:T(8,128)(2,1)S(1)}, bf16[288,768]{1,0:T(8,128)(2,1)}, u32[]{:S(2)}, u32[]{:S(2)}) collective-permute-start(bf16[288,768]{1,0:T(8,128)(2,1)S(1)} %pad_maximum_fusion), channel_id=1, source_target_pairs={{0,4},{1,5},{2,6},{3,7},{12,136},{13,137},{14,138},{15,139},{144,1... | collective-permute-start | bytes 1327112 | tf_op jit(solution)/shard_map/scatter/ppermute | solution.py:188
  9.7 3.0 %collective-permute-start.4 = (bf16[288,768]{1,0:T(8,128)(2,1)S(1)}, bf16[288,768]{1,0:T(8,128)(2,1)}, u32[]{:S(2)}, u32[]{:S(2)}) collective-permute-start(bf16[288,768]{1,0:T(8,128)(2,1)S(1)} %pad_maximum_fusion.1), channel_id=1, source_target_pairs={{0,128},{1,129},{2,130},{3,131},{12,140},{13,141},{14,142},{15,143... | collective-permute-start | bytes 1327112 | tf_op jit(solution)/shard_map/scatter/ppermute | solution.py:188
  11.1 40.7 %copy-start = (bf16[1,2,128,3072]{3,2,1,0:T(8,128)(2,1)S(1)}, bf16[1,2,128,3072]{3,2,1,0:T(8,128)(2,1)}, u32[]{:S(2)}) copy-start(bf16[1,2,128,3072]{3,2,1,0:T(8,128)(2,1)} %video_ref.1) | copy-start | bytes 4718596
  11.1 40.7 %copy-start.1 = (f32[3072]{0:T(1024)S(1)}, f32[3072]{0:T(1024)}, u32[]{:S(2)}) copy-start(f32[3072]{0:T(1024)} %param.8) | copy-start | bytes 36868
  11.1 38.5 %collective-permute-start.5 = (bf16[288,768]{1,0:T(8,128)(2,1)S(1)}, bf16[288,768]{1,0:T(8,128)(2,1)}, u32[]{:S(2)}, u32[]{:S(2)}) collective-permute-start(bf16[288,768]{1,0:T(8,128)(2,1)S(1)} %pad_maximum_fusion.2), channel_id=1, source_target_pairs={{0,132},{1,133},{2,134},{3,135},{12,8},{13,9},{14,10},{15,11},{144... | collective-permute-start | bytes 1327112 | tf_op jit(solution)/shard_map/scatter/ppermute | solution.py:188
  53.3 67.3 %copy-start.2 = (f32[128]{0:T(128)S(1)}, f32[128]{0:T(128)}, u32[]{:S(2)}) copy-start(f32[128]{0:T(128)} %param.12) | copy-start | bytes 1540
  53.3 67.3 %copy-start.3 = (f32[128]{0:T(128)S(1)}, f32[128]{0:T(128)}, u32[]{:S(2)}) copy-start(f32[128]{0:T(128)} %param.13) | copy-start | bytes 1540
  81.5 22.0 %collective-permute-start.2 = (bf16[256,3072]{1,0:T(8,128)(2,1)S(1)}, bf16[256,3072]{1,0:T(8,128)(2,1)S(1)}, u32[]{:S(2)}, u32[]{:S(2)}) collective-permute-start(bf16[256,3072]{1,0:T(8,128)(2,1)S(1)} %bitcast.10), channel_id=1, source_target_pairs={{0,64},{1,17},{2,66},{3,19},{4,68},{5,21},{6,70},{7,23},{128,192},... | collective-permute-start | bytes 4718600 | tf_op jit(solution)/shard_map/rows_line/ppermute | solution.py:197
  82.9 36.4 %collective-permute-start.1 = (bf16[256,3072]{1,0:T(8,128)(2,1)S(1)}, bf16[256,3072]{1,0:T(8,128)(2,1)S(1)}, u32[]{:S(2)}, u32[]{:S(2)}) collective-permute-start(bf16[256,3072]{1,0:T(8,128)(2,1)S(1)} %bitcast.11), channel_id=1, source_target_pairs={{0,96},{1,25},{2,98},{3,27},{4,100},{5,29},{6,102},{7,31},{128,224... | collective-permute-start | bytes 4718600 | tf_op jit(solution)/shard_map/rows_line/ppermute | solution.py:197
  84.4 36.1 %collective-permute-start = (bf16[256,3072]{1,0:T(8,128)(2,1)S(1)}, bf16[256,3072]{1,0:T(8,128)(2,1)S(1)}, u32[]{:S(2)}, u32[]{:S(2)}) collective-permute-start(bf16[256,3072]{1,0:T(8,128)(2,1)S(1)} %bitcast.12), channel_id=1, source_target_pairs={{0,32},{1,9},{2,34},{3,11},{4,36},{5,13},{6,38},{7,15},{128,160},{... | collective-permute-start | bytes 4718600 | tf_op jit(solution)/shard_map/rows_line/ppermute | solution.py:197
  103.5 15.8 %copy-start.4 = (bf16[256,3072]{1,0:T(8,128)(2,1)}, bf16[256,3072]{1,0:T(8,128)(2,1)S(1)}, u32[]{:S(2)}) copy-start(bf16[256,3072]{1,0:T(8,128)(2,1)S(1)} %collective-permute-done.2.r3) | copy-start | bytes 4718596
  119.3 1.2 copy-start.5
  136.0 16.9 %all-to-all-start.1 = ((bf16[16,64,384]{2,1,0:T(8,128)(2,1)}), bf16[16,64,384]{2,1,0:T(8,128)(2,1)S(1)}, u32[]{:S(2)}, u32[]{:S(2)}) async-start(bf16[16,64,384]{2,1,0:T(8,128)(2,1)} %project_attend.1), calls=%async_computation.1 | async-start | bytes 1572864 | tf_op jit(solution)/shard_map/heads_back/all_to_all | solution.py:200
Sparse Core Ops, SparseCore 0:
  51.9 48.0 all-gather.1

commit v2 on v1

--- a/solution.py
+++ b/solution.py
@@ -186,13 +186,14 @@
     ]
     with jax.named_scope("scatter"):
         mine = [quarters[0]] + [lax.ppermute(quarters[r], AXES, scatter_perm(r)) for r in (1, 3, 2)]
+    normed = layer_normed(video, norm_gain)
+    with jax.named_scope("rows_home"):
+        home = lax.all_to_all(normed, "seq", split_axis=0, concat_axis=0, tiled=True).reshape(256, d)
+    mine, home = lax.optimization_barrier((mine, home))
     part = lax.select_n((pair - group + 4) % 4, mine[0], mine[1], mine[3], mine[2])
     gathered = lax.all_gather(part, ("dp", "fsdp"), axis=0, tiled=True)
     gathered = gathered.reshape(4, 4, 288, quarter)
 
-    normed = layer_normed(video, norm_gain)
-    with jax.named_scope("rows_home"):
-        home = lax.all_to_all(normed, "seq", split_axis=0, concat_axis=0, tiled=True).reshape(256, d)
     with jax.named_scope("rows_line"):
         pieces = [home] + [lax.ppermute(home, AXES, line_perm(s)) for s in SHIFTS[1:]]
     output = attend(pieces, gathered, group.astype(jnp.int32).reshape(1), query_gain, key_gain)

time: 161 us -> 155 us (0.963)
  blocking collectives: 28.2 us -> 0 us
  waiting for transfers between devices: 82.4 us -> 93 us
  starting transfers between devices: 13.5 us -> 21.2 us
  local copies, waits for them, and re-layouts: 2.87 us -> 4.63 us
    all_to_all x1 -> x0, blocking collectives: 28.2 us -> none  [shards(): lax.all_to_all(normed, 'seq', split_axis=0, concat_axis=0, tiled=True)]
    all_gather x1, waiting for transfers between devices: 0.01 us -> 8.61 us  [shards(): gathered = lax.all_gather(part, ('dp', 'fsdp'), axis=0, tiled=True)]
    all_to_all x0 -> x1, starting transfers between devices: none -> 7.52 us  [shards(): lax.all_to_all(normed, 'seq', split_axis=0, concat_axis=0, tiled=True)]
    all_to_all x1, waiting for transfers between devices: 11 us -> 13.7 us  [shards(): lax.all_to_all(output, 'seq', split_axis=0, concat_axis=0, tiled=True)]
    unnamed x16, local copies, waits for them, and re-layouts: 1.54 us -> 3.37 us
    ppermute x3, waiting for transfers between devices: 37 us -> 35.3 us  [shards(): lax.ppermute(quarters[r], AXES, scatter_perm(r))]
  transfers between devices with their start and end apart: 8 -> 9, of which waited for: 4 -> 6; matrix products, arithmetic and copies ran while one was open for 0% -> 2% of each run, Pallas kernels for 1% -> 0%
where the time goes in v2:
time: 155 us
  waiting for transfers between devices  93 us (60%)
  starting transfers between devices  21.2 us (14%)
  Pallas kernels  18.9 us (12%)
  between operations  13.5 us (9%)
  local copies, waits for them, and re-layouts  4.63 us (3%)
  other arithmetic  3.64 us (2%)
    ppermute x3, waiting for transfers between devices, shards(): lax.ppermute(home, AXES, line_perm(s))  35.4 us
    ppermute x3, waiting for transfers between devices, shards(): lax.ppermute(quarters[r], AXES, scatter_perm(r))  35.3 us
    pallas_call x1, Pallas kernels, attend(): pl.pallas_call(attend_kernel, grid_spec=pltpu.PrefetchScalarGridSpec(num_...  15.3 us
    all_to_all x1, waiting for transfers between devices, shards(): lax.all_to_all(output, 'seq', split_axis=0, concat_axis=0, tiled=True)  13.7 us
    all_gather x1, waiting for transfers between devices, shards(): gathered = lax.all_gather(part, ('dp', 'fsdp'), axis=0, tiled=True)  8.61 us
    all_to_all x1, starting transfers between devices, shards(): lax.all_to_all(normed, 'seq', split_axis=0, concat_axis=0, tiled=True)  7.52 us
    all_to_all x1, starting transfers between devices, shards(): lax.all_to_all(output, 'seq', split_axis=0, concat_axis=0, tiled=True)  7.26 us
    ppermute x3, starting transfers between devices, shards(): lax.ppermute(quarters[r], AXES, scatter_perm(r))  4.18 us
  transfers between devices with their start and end apart: 9, of which 6 were waited for; matrix products, arithmetic and copies ran while one was open for 2% of the time, Pallas kernels for 0%

profile of v2, /device:TPU:8, one launch (start us, length us, event | category | flops | bytes accessed | tf_op | source)
XLA Modules:
  0.0 154.8 jit_solution(14048247149416092235)
XLA Ops:
  6.5 0.0 copy-start
  6.5 1.4 copy-done
  7.9 0.0 copy-start.1
  7.9 0.7 copy-done.1
  8.7 2.6 %norm_rows.1 = bf16[16,16,3072]{2,1,0:T(8,128)(2,1)} custom-call(bf16[1,2,128,3072]{3,2,1,0:T(8,128)(2,1)S(1)} %copy-done, f32[1,3072]{1,0:T(1,128)S(1)} %bitcast.14), custom_call_target="tpu_custom_call" | custom-call | tf_op jit(solution)/shard_map/norm_rows/pallas_call | solution.py:54
  11.2 0.0 copy-start.6
  11.2 0.0 copy-start.7
  11.2 7.5 %all-to-all-start = ((bf16[16,16,3072]{2,1,0:T(8,128)(2,1)}), bf16[16,16,3072]{2,1,0:T(8,128)(2,1)S(1)}, u32[]{:S(2)}, u32[]{:S(2)}) async-start(bf16[16,16,3072]{2,1,0:T(8,128)(2,1)} %norm_rows.1), calls=%async_computation | async-start | bytes 3145728 | tf_op jit(solution)/shard_map/rows_home/all_to_all | solution.py:191
  18.8 0.0 all-gather.2.cloned.1.call-start
  18.8 0.0 copy-done.6
  18.9 0.0 copy-done.7
  18.9 1.2 fusion
  20.1 1.5 collective-permute-start
  21.6 0.8 pad_maximum_fusion.2
  22.4 1.3 collective-permute-start.1
  23.7 0.8 pad_maximum_fusion.3
  24.5 1.4 collective-permute-start.2
  25.9 0.0 copy-start.2
  25.9 0.0 copy-start.3
  26.0 0.0 collective-permute-done
  26.0 35.3 %collective-permute-done.1 = bf16[288,768]{1,0:T(8,128)(2,1)} collective-permute-done((bf16[288,768]{1,0:T(8,128)(2,1)}, bf16[288,768]{1,0:T(8,128)(2,1)}, u32[]{:S(2)}, u32[]{:S(2)}) %collective-permute-start.1) | collective-permute-done | bytes 442400 | tf_op jit(solution)/shard_map/scatter/ppermute | solution.py:188
  61.3 0.0 collective-permute-done.2
  61.3 0.0 all-to-all-done
  61.3 2.0 %select_select_fusion = bf16[288,768]{1,0:T(8,128)(2,1)} fusion(bf16[288,768]{1,0:T(8,128)(2,1)} %collective-permute-done.2, bf16[288,768]{1,0:T(8,128)(2,1)} %collective-permute-done.1, bf16[288,768]{1,0:T(8,128)(2,1)S(1)} %pad_maximum_fusion, bf16[288,768]{1,0:T(8,128)(2,1)} %collective-permute-done, pred[]{:T(512)S(6)} %select_n.64, pred[]{:T(512)S(6)} %select_n.61, ...), kind=kLoop, calls=%fused_computation.4 | loop fusion | flops 663552 | bytes 2211843 | tf_op jit(solution)/shard_map/select_n | solution.py:193
  63.3 0.0 all-gather.2.cloned.1.call-update
  63.3 0.1 collective-permute-start.5
  63.4 0.1 collective-permute-start.4
  63.5 2.0 %collective-permute-start.3 = (bf16[256,3072]{1,0:T(8,128)(2,1)S(1)}, bf16[256,3072]{1,0:T(8,128)(2,1)S(1)}, u32[]{:S(2)}, u32[]{:S(2)}) collective-permute-start(bf16[256,3072]{1,0:T(8,128)(2,1)S(1)} %bitcast.12), channel_id=1, source_target_pairs={{0,32},{1,9},{2,34},{3,11},{4,36},{5,13},{6,38},{7,15},{128,160},{... | collective-permute-start | bytes 4718600 | tf_op jit(solution)/shard_map/rows_line/ppermute | solution.py:198
  65.5 19.9 %collective-permute-done.5.r3 = bf16[256,3072]{1,0:T(8,128)(2,1)S(1)} collective-permute-done((bf16[256,3072]{1,0:T(8,128)(2,1)S(1)}, bf16[256,3072]{1,0:T(8,128)(2,1)S(1)}, u32[]{:S(2)}, u32[]{:S(2)}) %collective-permute-start.5) | collective-permute-done | bytes 1572896 | tf_op jit(solution)/shard_map/rows_line/ppermute | solution.py:198
  85.4 0.0 copy-start.4
  85.4 14.1 %collective-permute-done.4.r2 = bf16[256,3072]{1,0:T(8,128)(2,1)S(1)} collective-permute-done((bf16[256,3072]{1,0:T(8,128)(2,1)S(1)}, bf16[256,3072]{1,0:T(8,128)(2,1)S(1)}, u32[]{:S(2)}, u32[]{:S(2)}) %collective-permute-start.4) | collective-permute-done | bytes 1572896 | tf_op jit(solution)/shard_map/rows_line/ppermute | solution.py:198
  99.5 0.0 copy-done.4
  99.5 0.0 copy-start.5
  99.5 1.2 copy-done.5
  100.8 1.4 collective-permute-done.3.r1
  102.2 8.6 %all-gather.2.cloned.1.call-done = bf16[4608,768]{1,0:T(8,128)(2,1)} async-done(((bf16[288,768]{1,0:T(8,128)(2,1)}), bf16[4608,768]{1,0:T(8,128)(2,1)}) %all-gather.2.cloned.1.call-update) | async-done | bytes 7077904 | tf_op jit(solution)/shard_map/all_gather | solution.py:194
  110.8 0.0 copy-done.2
  110.8 0.0 copy-done.3
  110.8 15.3 %project_attend.1 = bf16[16,64,384]{2,1,0:T(8,128)(2,1)} custom-call(s32[1]{0:T(128)} %bitcast.1.group_ref, bf16[256,3072]{1,0:T(8,128)(2,1)S(1)} %bitcast.13, bf16[256,3072]{1,0:T(8,128)(2,1)S(1)} %collective-permute-done.3.r1, bf16[256,3072]{1,0:T(8,128)(2,1)} %copy-done.5, bf16[256,3072]{1,0:T(8,128)(2,1)} %copy-done.4, ...), custom_call_target="tpu_custom_call" | custom-call | tf_op jit(solution)/shard_map/project_attend/pallas_call | solution.py:117
  126.1 7.3 %all-to-all-start.1 = ((bf16[16,64,384]{2,1,0:T(8,128)(2,1)}), bf16[16,64,384]{2,1,0:T(8,128)(2,1)S(1)}, u32[]{:S(2)}, u32[]{:S(2)}) async-start(bf16[16,64,384]{2,1,0:T(8,128)(2,1)} %project_attend.1), calls=%async_computation.1 | async-start | bytes 1572864 | tf_op jit(solution)/shard_map/heads_back/all_to_all | solution.py:201
  133.4 13.7 %all-to-all-done.1.recv_ref = bf16[16,64,384]{2,1,0:T(8,128)(2,1)S(1)} async-done(((bf16[16,64,384]{2,1,0:T(8,128)(2,1)}), bf16[16,64,384]{2,1,0:T(8,128)(2,1)S(1)}, u32[]{:S(2)}, u32[]{:S(2)}) %all-to-all-start.1) | async-done | bytes 786464 | tf_op jit(solution)/shard_map/heads_back/all_to_all | solution.py:201
  147.0 1.0 assemble_heads.1
  (3 shorter events, 0.1 us)
Async XLA Ops:
  6.5 1.4 copy-start
  7.9 0.7 copy-start.1
  11.2 7.6 %copy-start.6 = (bf16[3072,96]{0,1:T(8,128)(2,1)S(1)}, bf16[3072,96]{0,1:T(8,128)(2,1)}, u32[]{:S(2)}) copy-start(bf16[3072,96]{0,1:T(8,128)(2,1)} %param.11) | copy-start | bytes 1769476
  11.2 7.6 %copy-start.7 = (bf16[3072,96]{0,1:T(8,128)(2,1)S(1)}, bf16[3072,96]{0,1:T(8,128)(2,1)}, u32[]{:S(2)}) copy-start(bf16[3072,96]{0,1:T(8,128)(2,1)} %param.9) | copy-start | bytes 1769476
  11.2 50.0 %all-to-all-start = ((bf16[16,16,3072]{2,1,0:T(8,128)(2,1)}), bf16[16,16,3072]{2,1,0:T(8,128)(2,1)S(1)}, u32[]{:S(2)}, u32[]{:S(2)}) async-start(bf16[16,16,3072]{2,1,0:T(8,128)(2,1)} %norm_rows.1), calls=%async_computation | async-start | bytes 3145728 | tf_op jit(solution)/shard_map/rows_home/all_to_all | solution.py:191
  18.8 92.0 %all-gather.2.cloned.1.call-start = ((), (), s32[]{:S(2)}) async-start(), calls=%async_computation.2 | async-start | bytes 7520256 | tf_op jit(solution)/shard_map/all_gather | solution.py:194
  20.1 5.8 %collective-permute-start = (bf16[288,768]{1,0:T(8,128)(2,1)S(1)}, bf16[288,768]{1,0:T(8,128)(2,1)}, u32[]{:S(2)}, u32[]{:S(2)}) collective-permute-start(bf16[288,768]{1,0:T(8,128)(2,1)S(1)} %pad_maximum_fusion.1), channel_id=1, source_target_pairs={{0,4},{1,5},{2,6},{3,7},{12,136},{13,137},{14,138},{15,139},{144,1... | collective-permute-start | bytes 1327112 | tf_op jit(solution)/shard_map/scatter/ppermute | solution.py:188
  22.4 38.9 %collective-permute-start.1 = (bf16[288,768]{1,0:T(8,128)(2,1)}, bf16[288,768]{1,0:T(8,128)(2,1)}, u32[]{:S(2)}, u32[]{:S(2)}) collective-permute-start(bf16[288,768]{1,0:T(8,128)(2,1)} %pad_maximum_fusion.2), channel_id=1, source_target_pairs={{0,132},{1,133},{2,134},{3,135},{12,8},{13,9},{14,10},{15,11},{144... | collective-permute-start | bytes 1327112 | tf_op jit(solution)/shard_map/scatter/ppermute | solution.py:188
  24.5 36.8 %collective-permute-start.2 = (bf16[288,768]{1,0:T(8,128)(2,1)}, bf16[288,768]{1,0:T(8,128)(2,1)}, u32[]{:S(2)}, u32[]{:S(2)}) collective-permute-start(bf16[288,768]{1,0:T(8,128)(2,1)} %pad_maximum_fusion.3), channel_id=1, source_target_pairs={{0,128},{1,129},{2,130},{3,131},{12,140},{13,141},{14,142},{15,143... | collective-permute-start | bytes 1327112 | tf_op jit(solution)/shard_map/scatter/ppermute | solution.py:188
  25.9 84.8 %copy-start.2 = (f32[128]{0:T(128)S(1)}, f32[128]{0:T(128)}, u32[]{:S(2)}) copy-start(f32[128]{0:T(128)} %param.12) | copy-start | bytes 1540
  25.9 84.8 %copy-start.3 = (f32[128]{0:T(128)S(1)}, f32[128]{0:T(128)}, u32[]{:S(2)}) copy-start(f32[128]{0:T(128)} %param.13) | copy-start | bytes 1540
  63.3 22.1 %collective-permute-start.5 = (bf16[256,3072]{1,0:T(8,128)(2,1)S(1)}, bf16[256,3072]{1,0:T(8,128)(2,1)S(1)}, u32[]{:S(2)}, u32[]{:S(2)}) collective-permute-start(bf16[256,3072]{1,0:T(8,128)(2,1)S(1)} %bitcast.10), channel_id=1, source_target_pairs={{0,64},{1,17},{2,66},{3,19},{4,68},{5,21},{6,70},{7,23},{128,192},... | collective-permute-start | bytes 4718600 | tf_op jit(solution)/shard_map/rows_line/ppermute | solution.py:198
  63.4 36.1 %collective-permute-start.4 = (bf16[256,3072]{1,0:T(8,128)(2,1)S(1)}, bf16[256,3072]{1,0:T(8,128)(2,1)S(1)}, u32[]{:S(2)}, u32[]{:S(2)}) collective-permute-start(bf16[256,3072]{1,0:T(8,128)(2,1)S(1)} %bitcast.11), channel_id=1, source_target_pairs={{0,96},{1,25},{2,98},{3,27},{4,100},{5,29},{6,102},{7,31},{128,224... | collective-permute-start | bytes 4718600 | tf_op jit(solution)/shard_map/rows_line/ppermute | solution.py:198
  63.5 38.7 %collective-permute-start.3 = (bf16[256,3072]{1,0:T(8,128)(2,1)S(1)}, bf16[256,3072]{1,0:T(8,128)(2,1)S(1)}, u32[]{:S(2)}, u32[]{:S(2)}) collective-permute-start(bf16[256,3072]{1,0:T(8,128)(2,1)S(1)} %bitcast.12), channel_id=1, source_target_pairs={{0,32},{1,9},{2,34},{3,11},{4,36},{5,13},{6,38},{7,15},{128,160},{... | collective-permute-start | bytes 4718600 | tf_op jit(solution)/shard_map/rows_line/ppermute | solution.py:198
  85.4 14.1 %copy-start.4 = (bf16[256,3072]{1,0:T(8,128)(2,1)}, bf16[256,3072]{1,0:T(8,128)(2,1)S(1)}, u32[]{:S(2)}) copy-start(bf16[256,3072]{1,0:T(8,128)(2,1)S(1)} %collective-permute-done.5.r3) | copy-start | bytes 4718596
  99.5 1.2 copy-start.5
  126.1 20.9 %all-to-all-start.1 = ((bf16[16,64,384]{2,1,0:T(8,128)(2,1)}), bf16[16,64,384]{2,1,0:T(8,128)(2,1)S(1)}, u32[]{:S(2)}, u32[]{:S(2)}) async-start(bf16[16,64,384]{2,1,0:T(8,128)(2,1)} %project_attend.1), calls=%async_computation.1 | async-start | bytes 1572864 | tf_op jit(solution)/shard_map/heads_back/all_to_all | solution.py:201
Sparse Core Ops, SparseCore 0:
  63.4 47.3 all-gather.1

commit v3 on v2

--- a/solution.py
+++ b/solution.py
@@ -22,10 +22,11 @@
     for x in range(4):
         for y in range(4):
             j = (x + y) % 4
+            origin = (x + 2) % 4 if shift == 2 else x
             for a in range(2):
                 for c in range(2):
                     z = 2 * j + a
-                    pairs.append((place(x, y, z, c), place(x, y, (z + 2 * shift) % 8, c)))
+                    pairs.append((place(origin, y, z, c), place(x, y, (z + 2 * shift) % 8, c)))
     return pairs
 
 

time: 155 us -> 147 us (0.948)
  waiting for transfers between devices: 93 us -> 84.3 us
    ppermute x3, waiting for transfers between devices: 35.3 us -> 25.8 us  [shards(): lax.ppermute(quarters[r], AXES, scatter_perm(r))]
where the time goes in v3:
time: 147 us; the launch traced here: 146 us
  waiting for transfers between devices  84.3 us (57%)
  starting transfers between devices  21.2 us (14%)
  Pallas kernels  18.9 us (13%)
  between operations  13.5 us (9%)
  local copies, waits for them, and re-layouts  4.63 us (3%)
  other arithmetic  3.64 us (2%)
    ppermute x3, waiting for transfers between devices, shards(): lax.ppermute(home, AXES, line_perm(s))  35.4 us
    ppermute x3, waiting for transfers between devices, shards(): lax.ppermute(quarters[r], AXES, scatter_perm(r))  25.8 us
    pallas_call x1, Pallas kernels, attend(): pl.pallas_call(attend_kernel, grid_spec=pltpu.PrefetchScalarGridSpec(num_...  15.3 us
    all_to_all x1, waiting for transfers between devices, shards(): lax.all_to_all(output, 'seq', split_axis=0, concat_axis=0, tiled=True)  13.7 us
    all_gather x1, waiting for transfers between devices, shards(): gathered = lax.all_gather(part, ('dp', 'fsdp'), axis=0, tiled=True)  9.33 us
    all_to_all x1, starting transfers between devices, shards(): lax.all_to_all(normed, 'seq', split_axis=0, concat_axis=0, tiled=True)  7.52 us
    all_to_all x1, starting transfers between devices, shards(): lax.all_to_all(output, 'seq', split_axis=0, concat_axis=0, tiled=True)  7.26 us
    ppermute x3, starting transfers between devices, shards(): lax.ppermute(quarters[r], AXES, scatter_perm(r))  4.18 us
  transfers between devices with their start and end apart: 9, of which 6 were waited for; matrix products, arithmetic and copies ran while one was open for 2% of the time, Pallas kernels for 0%

profile of v3, /device:TPU:8, one launch (start us, length us, event | category | flops | bytes accessed | tf_op | source)
XLA Modules:
  0.0 146.1 jit_solution(557053879482168771)
XLA Ops:
  6.5 0.0 copy-start
  6.5 1.4 copy-done
  7.9 0.0 copy-start.1
  7.9 0.7 copy-done.1
  8.7 2.6 %norm_rows.1 = bf16[16,16,3072]{2,1,0:T(8,128)(2,1)} custom-call(bf16[1,2,128,3072]{3,2,1,0:T(8,128)(2,1)S(1)} %copy-done, f32[1,3072]{1,0:T(1,128)S(1)} %bitcast.14), custom_call_target="tpu_custom_call" | custom-call | tf_op jit(solution)/shard_map/norm_rows/pallas_call | solution.py:55
  11.2 0.0 copy-start.6
  11.2 0.0 copy-start.7
  11.2 7.5 %all-to-all-start = ((bf16[16,16,3072]{2,1,0:T(8,128)(2,1)}), bf16[16,16,3072]{2,1,0:T(8,128)(2,1)S(1)}, u32[]{:S(2)}, u32[]{:S(2)}) async-start(bf16[16,16,3072]{2,1,0:T(8,128)(2,1)} %norm_rows.1), calls=%async_computation | async-start | bytes 3145728 | tf_op jit(solution)/shard_map/rows_home/all_to_all | solution.py:192
  18.8 0.0 all-gather.2.cloned.1.call-start
  18.8 0.0 copy-done.6
  18.9 0.0 copy-done.7
  18.9 1.2 fusion
  20.1 1.5 %collective-permute-start = (bf16[288,768]{1,0:T(8,128)(2,1)S(1)}, bf16[288,768]{1,0:T(8,128)(2,1)}, u32[]{:S(2)}, u32[]{:S(2)}) collective-permute-start(bf16[288,768]{1,0:T(8,128)(2,1)S(1)} %pad_maximum_fusion.1), channel_id=1, source_target_pairs={{0,4},{1,5},{2,6},{3,7},{12,136},{13,137},{14,138},{15,139},{144,1... | collective-permute-start | bytes 1327112 | tf_op jit(solution)/shard_map/scatter/ppermute | solution.py:189
  21.6 0.8 pad_maximum_fusion.2
  22.4 1.3 collective-permute-start.1
  23.7 0.8 pad_maximum_fusion.3
  24.5 1.4 collective-permute-start.2
  25.9 0.0 copy-start.2
  25.9 0.0 copy-start.3
  26.0 0.0 collective-permute-done
  26.0 25.8 %collective-permute-done.1 = bf16[288,768]{1,0:T(8,128)(2,1)} collective-permute-done((bf16[288,768]{1,0:T(8,128)(2,1)}, bf16[288,768]{1,0:T(8,128)(2,1)}, u32[]{:S(2)}, u32[]{:S(2)}) %collective-permute-start.1) | collective-permute-done | bytes 442400 | tf_op jit(solution)/shard_map/scatter/ppermute | solution.py:189
  51.8 0.0 collective-permute-done.2
  51.8 0.0 all-to-all-done
  51.8 2.0 %select_select_fusion = bf16[288,768]{1,0:T(8,128)(2,1)} fusion(bf16[288,768]{1,0:T(8,128)(2,1)} %collective-permute-done.2, bf16[288,768]{1,0:T(8,128)(2,1)} %collective-permute-done.1, bf16[288,768]{1,0:T(8,128)(2,1)S(1)} %pad_maximum_fusion, bf16[288,768]{1,0:T(8,128)(2,1)} %collective-permute-done, pred[]{:T(512)S(6)} %select_n.64, pred[]{:T(512)S(6)} %select_n.61, ...), kind=kLoop, calls=%fused_computation.4 | loop fusion | flops 663552 | bytes 2211843 | tf_op jit(solution)/shard_map/select_n | solution.py:194
  53.8 0.0 all-gather.2.cloned.1.call-update
  53.8 0.1 collective-permute-start.5
  53.9 0.1 collective-permute-start.4
  54.0 2.0 %collective-permute-start.3 = (bf16[256,3072]{1,0:T(8,128)(2,1)S(1)}, bf16[256,3072]{1,0:T(8,128)(2,1)S(1)}, u32[]{:S(2)}, u32[]{:S(2)}) collective-permute-start(bf16[256,3072]{1,0:T(8,128)(2,1)S(1)} %bitcast.12), channel_id=1, source_target_pairs={{0,32},{1,9},{2,34},{3,11},{4,36},{5,13},{6,38},{7,15},{128,160},{... | collective-permute-start | bytes 4718600 | tf_op jit(solution)/shard_map/rows_line/ppermute | solution.py:199
  56.0 19.9 %collective-permute-done.5.r3 = bf16[256,3072]{1,0:T(8,128)(2,1)S(1)} collective-permute-done((bf16[256,3072]{1,0:T(8,128)(2,1)S(1)}, bf16[256,3072]{1,0:T(8,128)(2,1)S(1)}, u32[]{:S(2)}, u32[]{:S(2)}) %collective-permute-start.5) | collective-permute-done | bytes 1572896 | tf_op jit(solution)/shard_map/rows_line/ppermute | solution.py:199
  75.9 0.0 copy-start.4
  75.9 14.1 %collective-permute-done.4.r2 = bf16[256,3072]{1,0:T(8,128)(2,1)S(1)} collective-permute-done((bf16[256,3072]{1,0:T(8,128)(2,1)S(1)}, bf16[256,3072]{1,0:T(8,128)(2,1)S(1)}, u32[]{:S(2)}, u32[]{:S(2)}) %collective-permute-start.4) | collective-permute-done | bytes 1572896 | tf_op jit(solution)/shard_map/rows_line/ppermute | solution.py:199
  90.1 0.0 copy-done.4
  90.1 0.0 copy-start.5
  90.1 1.2 copy-done.5
  91.3 1.4 collective-permute-done.3.r1
  92.7 9.3 %all-gather.2.cloned.1.call-done = bf16[4608,768]{1,0:T(8,128)(2,1)} async-done(((bf16[288,768]{1,0:T(8,128)(2,1)}), bf16[4608,768]{1,0:T(8,128)(2,1)}) %all-gather.2.cloned.1.call-update) | async-done | bytes 7077904 | tf_op jit(solution)/shard_map/all_gather | solution.py:195
  102.0 0.0 copy-done.2
  102.0 0.0 copy-done.3
  102.0 15.3 %project_attend.1 = bf16[16,64,384]{2,1,0:T(8,128)(2,1)} custom-call(s32[1]{0:T(128)} %bitcast.1.group_ref, bf16[256,3072]{1,0:T(8,128)(2,1)S(1)} %bitcast.13, bf16[256,3072]{1,0:T(8,128)(2,1)S(1)} %collective-permute-done.3.r1, bf16[256,3072]{1,0:T(8,128)(2,1)} %copy-done.5, bf16[256,3072]{1,0:T(8,128)(2,1)} %copy-done.4, ...), custom_call_target="tpu_custom_call" | custom-call | tf_op jit(solution)/shard_map/project_attend/pallas_call | solution.py:118
  117.3 7.3 %all-to-all-start.1 = ((bf16[16,64,384]{2,1,0:T(8,128)(2,1)}), bf16[16,64,384]{2,1,0:T(8,128)(2,1)S(1)}, u32[]{:S(2)}, u32[]{:S(2)}) async-start(bf16[16,64,384]{2,1,0:T(8,128)(2,1)} %project_attend.1), calls=%async_computation.1 | async-start | bytes 1572864 | tf_op jit(solution)/shard_map/heads_back/all_to_all | solution.py:202
  124.6 13.7 %all-to-all-done.1.recv_ref = bf16[16,64,384]{2,1,0:T(8,128)(2,1)S(1)} async-done(((bf16[16,64,384]{2,1,0:T(8,128)(2,1)}), bf16[16,64,384]{2,1,0:T(8,128)(2,1)S(1)}, u32[]{:S(2)}, u32[]{:S(2)}) %all-to-all-start.1) | async-done | bytes 786464 | tf_op jit(solution)/shard_map/heads_back/all_to_all | solution.py:202
  138.3 1.0 assemble_heads.1
  (3 shorter events, 0.1 us)
Async XLA Ops:
  6.5 1.4 copy-start
  7.9 0.7 copy-start.1
  11.2 7.6 %copy-start.6 = (bf16[3072,96]{0,1:T(8,128)(2,1)S(1)}, bf16[3072,96]{0,1:T(8,128)(2,1)}, u32[]{:S(2)}) copy-start(bf16[3072,96]{0,1:T(8,128)(2,1)} %param.11) | copy-start | bytes 1769476
  11.2 7.6 %copy-start.7 = (bf16[3072,96]{0,1:T(8,128)(2,1)S(1)}, bf16[3072,96]{0,1:T(8,128)(2,1)}, u32[]{:S(2)}) copy-start(bf16[3072,96]{0,1:T(8,128)(2,1)} %param.9) | copy-start | bytes 1769476
  11.2 40.6 %all-to-all-start = ((bf16[16,16,3072]{2,1,0:T(8,128)(2,1)}), bf16[16,16,3072]{2,1,0:T(8,128)(2,1)S(1)}, u32[]{:S(2)}, u32[]{:S(2)}) async-start(bf16[16,16,3072]{2,1,0:T(8,128)(2,1)} %norm_rows.1), calls=%async_computation | async-start | bytes 3145728 | tf_op jit(solution)/shard_map/rows_home/all_to_all | solution.py:192
  18.8 83.2 %all-gather.2.cloned.1.call-start = ((), (), s32[]{:S(2)}) async-start(), calls=%async_computation.2 | async-start | bytes 7520256 | tf_op jit(solution)/shard_map/all_gather | solution.py:195
  20.1 5.8 %collective-permute-start = (bf16[288,768]{1,0:T(8,128)(2,1)S(1)}, bf16[288,768]{1,0:T(8,128)(2,1)}, u32[]{:S(2)}, u32[]{:S(2)}) collective-permute-start(bf16[288,768]{1,0:T(8,128)(2,1)S(1)} %pad_maximum_fusion.1), channel_id=1, source_target_pairs={{0,4},{1,5},{2,6},{3,7},{12,136},{13,137},{14,138},{15,139},{144,1... | collective-permute-start | bytes 1327112 | tf_op jit(solution)/shard_map/scatter/ppermute | solution.py:189
  22.4 29.4 %collective-permute-start.1 = (bf16[288,768]{1,0:T(8,128)(2,1)}, bf16[288,768]{1,0:T(8,128)(2,1)}, u32[]{:S(2)}, u32[]{:S(2)}) collective-permute-start(bf16[288,768]{1,0:T(8,128)(2,1)} %pad_maximum_fusion.2), channel_id=1, source_target_pairs={{0,132},{1,133},{2,134},{3,135},{12,8},{13,9},{14,10},{15,11},{144... | collective-permute-start | bytes 1327112 | tf_op jit(solution)/shard_map/scatter/ppermute | solution.py:189
  24.5 27.3 %collective-permute-start.2 = (bf16[288,768]{1,0:T(8,128)(2,1)}, bf16[288,768]{1,0:T(8,128)(2,1)}, u32[]{:S(2)}, u32[]{:S(2)}) collective-permute-start(bf16[288,768]{1,0:T(8,128)(2,1)} %pad_maximum_fusion.3), channel_id=1, source_target_pairs={{64,128},{65,129},{66,130},{67,131},{76,140},{77,141},{78,142},{79... | collective-permute-start | bytes 1327112 | tf_op jit(solution)/shard_map/scatter/ppermute | solution.py:189
  25.9 76.1 %copy-start.2 = (f32[128]{0:T(128)S(1)}, f32[128]{0:T(128)}, u32[]{:S(2)}) copy-start(f32[128]{0:T(128)} %param.12) | copy-start | bytes 1540
  25.9 76.1 %copy-start.3 = (f32[128]{0:T(128)S(1)}, f32[128]{0:T(128)}, u32[]{:S(2)}) copy-start(f32[128]{0:T(128)} %param.13) | copy-start | bytes 1540
  53.8 22.1 %collective-permute-start.5 = (bf16[256,3072]{1,0:T(8,128)(2,1)S(1)}, bf16[256,3072]{1,0:T(8,128)(2,1)S(1)}, u32[]{:S(2)}, u32[]{:S(2)}) collective-permute-start(bf16[256,3072]{1,0:T(8,128)(2,1)S(1)} %bitcast.10), channel_id=1, source_target_pairs={{0,64},{1,17},{2,66},{3,19},{4,68},{5,21},{6,70},{7,23},{128,192},... | collective-permute-start | bytes 4718600 | tf_op jit(solution)/shard_map/rows_line/ppermute | solution.py:199
  53.9 36.1 %collective-permute-start.4 = (bf16[256,3072]{1,0:T(8,128)(2,1)S(1)}, bf16[256,3072]{1,0:T(8,128)(2,1)S(1)}, u32[]{:S(2)}, u32[]{:S(2)}) collective-permute-start(bf16[256,3072]{1,0:T(8,128)(2,1)S(1)} %bitcast.11), channel_id=1, source_target_pairs={{0,96},{1,25},{2,98},{3,27},{4,100},{5,29},{6,102},{7,31},{128,224... | collective-permute-start | bytes 4718600 | tf_op jit(solution)/shard_map/rows_line/ppermute | solution.py:199
  54.0 38.7 %collective-permute-start.3 = (bf16[256,3072]{1,0:T(8,128)(2,1)S(1)}, bf16[256,3072]{1,0:T(8,128)(2,1)S(1)}, u32[]{:S(2)}, u32[]{:S(2)}) collective-permute-start(bf16[256,3072]{1,0:T(8,128)(2,1)S(1)} %bitcast.12), channel_id=1, source_target_pairs={{0,32},{1,9},{2,34},{3,11},{4,36},{5,13},{6,38},{7,15},{128,160},{... | collective-permute-start | bytes 4718600 | tf_op jit(solution)/shard_map/rows_line/ppermute | solution.py:199
  75.9 14.1 %copy-start.4 = (bf16[256,3072]{1,0:T(8,128)(2,1)}, bf16[256,3072]{1,0:T(8,128)(2,1)S(1)}, u32[]{:S(2)}) copy-start(bf16[256,3072]{1,0:T(8,128)(2,1)S(1)} %collective-permute-done.5.r3) | copy-start | bytes 4718596
  90.1 1.2 copy-start.5
  117.3 20.9 %all-to-all-start.1 = ((bf16[16,64,384]{2,1,0:T(8,128)(2,1)}), bf16[16,64,384]{2,1,0:T(8,128)(2,1)S(1)}, u32[]{:S(2)}, u32[]{:S(2)}) async-start(bf16[16,64,384]{2,1,0:T(8,128)(2,1)} %project_attend.1), calls=%async_computation.1 | async-start | bytes 1572864 | tf_op jit(solution)/shard_map/heads_back/all_to_all | solution.py:202
Sparse Core Ops, SparseCore 0:
  53.9 48.0 all-gather.1

commit v4 on v3

--- a/solution.py
+++ b/solution.py
@@ -38,6 +38,51 @@
     return pairs
 
 
+def ring_perm(step):
+    return [(place(x, y, z, c), place(x, y, (z + step) % 8, c)) for x, y, z, c in every_place()]
+
+
+def swap_perm():
+    return [(place(x, y, z, c), place(x, y, z, 1 - c)) for x, y, z, c in every_place()]
+
+
+def pack_kernel(wq, wk, wv, q0, q1, q2, q3, columns, packed, sems, out_sems):
+    fetches = [pltpu.make_async_copy(w, columns.at[m], sems.at[m]) for m, w in enumerate((wq, wk, wv))]
+    for copy in fetches:
+        copy.start()
+    for copy in fetches:
+        copy.wait()
+    height, quarter = columns.shape[1], packed.shape[2]
+    stores = []
+    for r, out in ((1, q1), (2, q2), (3, q3), (0, q0)):
+        for m in range(3):
+            packed[r, height * m : height * (m + 1), :] = columns[m, :, quarter * r : quarter * (r + 1)]
+        store = pltpu.make_async_copy(packed.at[r], out, out_sems.at[r])
+        store.start()
+        stores.append(store)
+    for store in stores:
+        store.wait()
+
+
+def pack(columns):
+    height, d = columns[0].shape
+    anywhere = pl.BlockSpec(memory_space=pl.ANY)
+    return pl.pallas_call(
+        pack_kernel,
+        in_specs=[anywhere] * 3,
+        out_specs=[anywhere] * 4,
+        out_shape=[jax.ShapeDtypeStruct((3 * height, d // 4), jnp.bfloat16)] * 4,
+        scratch_shapes=[
+            pltpu.VMEM((3, height, d), jnp.bfloat16),
+            pltpu.VMEM((4, 3 * height, d // 4), jnp.bfloat16),
+            pltpu.SemaphoreType.DMA((3,)),
+            pltpu.SemaphoreType.DMA((4,)),
+        ],
+        compiler_params=pltpu.CompilerParams(vmem_limit_bytes=58 * 2**20),
+        name="pack_weights",
+    )(*columns)
+
+
 def norm_kernel(video_ref, gain_ref, out_ref):
     values = video_ref[0].astype(jnp.float32)
     average = jnp.mean(values, axis=-1, keepdims=True)
@@ -61,44 +106,147 @@
         ],
         out_specs=pl.BlockSpec((16 // steps, 16, d), lambda i: (i, 0, 0)),
         out_shape=jax.ShapeDtypeStruct((16, 16, d), jnp.bfloat16),
-        compiler_params=pltpu.CompilerParams(vmem_limit_bytes=40 * 2**20),
+        compiler_params=pltpu.CompilerParams(vmem_limit_bytes=16 * 2**20),
         name="norm_rows",
     )(video, gain.reshape(1, d))
 
 
+def choose_kernel(where, q0, q1, q2, q3, out_ref):
+    quarter = (where[0] // 2 - where[1] + 4) % 4
+    for r, ref in enumerate((q0, q1, q2, q3)):
+
+        @pl.when(quarter == r)
+        def _(ref=ref):
+            out_ref[...] = ref[...]
+
+
+def choose(where, parts):
+    vmem = pl.BlockSpec(memory_space=pltpu.VMEM)
+    return pl.pallas_call(
+        choose_kernel,
+        in_specs=[pl.BlockSpec(memory_space=pltpu.SMEM)] + [vmem] * 4,
+        out_specs=vmem,
+        out_shape=jax.ShapeDtypeStruct(parts[0].shape, parts[0].dtype),
+        compiler_params=pltpu.CompilerParams(vmem_limit_bytes=8 * 2**20),
+        name="choose_quarter",
+    )(where, *parts)
+
+
+def halve_kernel(up, down, up_half, down_half):
+    width = up_half.shape[1]
+    up_half[...] = up[:, :width]
+    down_half[...] = down[:, width:]
+
+
+def halve(up, down):
+    vmem = pl.BlockSpec(memory_space=pltpu.VMEM)
+    half = jax.ShapeDtypeStruct((up.shape[0], up.shape[1] // 2), up.dtype)
+    return pl.pallas_call(
+        halve_kernel,
+        in_specs=[vmem] * 2,
+        out_specs=[vmem] * 2,
+        out_shape=[half, half],
+        compiler_params=pltpu.CompilerParams(vmem_limit_bytes=8 * 2**20),
+        name="halve",
+    )(up, down)
+
+
 NT = (((1,), (1,)), ((), ()))
 
 
-def attend_kernel(group_ref, r0, r1, r2, r3, w_ref, qg_ref, kg_ref, out_ref, rows, weights, acc):
-    t = pl.program_id(0)
+def stack_kernel(r0, r1, r2, r3, out_ref):
     for i, ref in enumerate((r0, r1, r2, r3)):
-        rows[256 * i : 256 * i + 256, :] = ref[...]
+        out_ref[256 * i : 256 * i + 256, :] = ref[...]
+
+
+def stack(pieces):
+    vmem = pl.BlockSpec(memory_space=pltpu.VMEM)
+    rows, d = pieces[0].shape
+    return pl.pallas_call(
+        stack_kernel,
+        in_specs=[vmem] * 4,
+        out_specs=vmem,
+        out_shape=jax.ShapeDtypeStruct((4 * rows, d), jnp.bfloat16),
+        compiler_params=pltpu.CompilerParams(vmem_limit_bytes=16 * 2**20),
+        name="stack_rows",
+    )(*pieces)
+
+
+def add_products(where, rows, weights, turn, offset, own, other, total, first):
+    z = (where[0] + offset + 8) % 8
+    r = (z // 2 - where[1] + 4) % 4
+    quarter = weights.shape[-1]
+    for core, parts in ((where[2], own), (1 - where[2], other)):
+        at = 0
+        for ref in parts:
+            width = ref.shape[1]
+            for m in range(3):
+                for g in range(3):
+                    to = pl.multiple_of((z % 2 * 128 + core * 96 + 32 * g) % 192, 32)
+                    low = 96 * m + 32 * g
+                    weights[turn, m, pl.ds(to, 32), at : at + width] = ref[low : low + 32, :]
+            at += width
     for m in range(3):
-        for blk in range(4):
-            at = 384 * m + 96 * blk
-            weights[at : at + 96, :] = w_ref[0, blk, 96 * m : 96 * m + 96, :]
-    product = lax.dot_general(rows[...], weights[...], NT, preferred_element_type=jnp.float32)
-
-    @pl.when(t == 0)
-    def _():
-        acc[...] = product
-
-    @pl.when(t > 0)
-    def _():
-        acc[...] += product
-
-    @pl.when(t == pl.num_programs(0) - 1)
+        weights[turn, m, 192:, :] = jnp.zeros((64, quarter), jnp.bfloat16)
+    product = lax.dot_general(
+        rows[:, pl.ds(pl.multiple_of(r * quarter, 128), quarter)],
+        weights[turn].reshape(768, quarter),
+        NT,
+        preferred_element_type=jnp.float32,
+    )
+    if first:
+        total[z % 2] = product
+    else:
+        total[z % 2] = total[z % 2] + product
+
+
+def project_kernel(offsets, where, rows, *refs):
+    pieces, total, weights = refs[: 2 * len(offsets)], refs[-2], refs[-1]
+    for turn, offset in enumerate(offsets):
+        own, other = [[pieces[2 * turn + side]] for side in range(2)]
+        add_products(where, rows, weights, turn, offset, own, other, total, offset in (0, -1))
+
+
+def project(where, rows, offsets, pieces, before=()):
+    vmem = pl.BlockSpec(memory_space=pltpu.VMEM)
+    quarter = rows.shape[1] // 4
+    return pl.pallas_call(
+        lambda *refs: project_kernel(offsets, *refs),
+        in_specs=[pl.BlockSpec(memory_space=pltpu.SMEM)] + [vmem] * (1 + len(pieces) + len(before)),
+        out_specs=vmem,
+        out_shape=jax.ShapeDtypeStruct((2, rows.shape[0], 768), jnp.float32),
+        scratch_shapes=[pltpu.VMEM((len(offsets), 3, 256, quarter), jnp.bfloat16)],
+        input_output_aliases={2 + len(pieces): 0} if before else {},
+        compiler_params=pltpu.CompilerParams(vmem_limit_bytes=20 * 2**20),
+        name="project",
+    )(where, rows, *pieces, *before)
+
+
+def head_columns(total, rows, m, h):
+    at = 256 * m
+    if h == 0:
+        return total[0, rows, at : at + 128]
+    if h == 2:
+        return total[1, rows, at : at + 128]
+    return jnp.concatenate([total[half, rows, at + 128 : at + 192] for half in range(2)], axis=-1)
+
+
+def attend_kernel(where, rows, fh, fho, bh, bho, qg_ref, kg_ref, before, out_ref, weights, total):
+    total[...] = before[...]
+    add_products(where, rows, weights, 0, 4, [fh, bh], [fho, bho], total, False)
+
+    @pl.when(where[0] >= 0)
     def _():
         gains = qg_ref[...] * kg_ref[...] * (128.0**-0.5)
         row_patch = lax.broadcasted_iota(jnp.int32, (256, 256), 0) % 8
         col_patch = lax.broadcasted_iota(jnp.int32, (256, 256), 1) % 8
         same = row_patch == col_patch
         for i in range(4):
+            part = slice(256 * i, 256 * i + 256)
             for h in range(3):
-                part = acc[256 * i : 256 * i + 256, :]
-                q_rows = part[:, 128 * h : 128 * h + 128].astype(jnp.bfloat16)
-                k = part[:, 384 + 128 * h : 512 + 128 * h].astype(jnp.bfloat16).astype(jnp.float32)
-                v = part[:, 768 + 128 * h : 896 + 128 * h].astype(jnp.bfloat16)
+                q_rows = head_columns(total, part, 0, h).astype(jnp.bfloat16)
+                k = head_columns(total, part, 1, h).astype(jnp.bfloat16).astype(jnp.float32)
+                v = head_columns(total, part, 2, h).astype(jnp.bfloat16)
                 q = q_rows.astype(jnp.float32)
                 q_scale = lax.rsqrt(jnp.mean(q * q, axis=-1, keepdims=True) + 1e-06)
                 k_scale = lax.rsqrt(jnp.mean(k * k, axis=-1, keepdims=True) + 1e-06)
@@ -110,29 +258,21 @@
                 out_ref[:, 16 * i : 16 * i + 16, 128 * h : 128 * h + 128] = out.reshape(16, 16, 128)
 
 
-def attend(pieces, gathered, group, query_gain, key_gain):
-    d = pieces[0].shape[-1]
-    quarter = d // 4
-    spec = pl.BlockSpec((256, quarter), lambda t, g: (0, (t - g[0] + 4) % 4))
-    gain_spec = pl.BlockSpec((1, 128), lambda t, g: (0, 0))
+def attend(where, rows, pieces, query_gain, key_gain, before):
+    vmem = pl.BlockSpec(memory_space=pltpu.VMEM)
+    quarter = rows.shape[1] // 4
     return pl.pallas_call(
         attend_kernel,
-        grid_spec=pltpu.PrefetchScalarGridSpec(
-            num_scalar_prefetch=1,
-            grid=(4,),
-            in_specs=[spec] * 4
-            + [pl.BlockSpec((1, 4, 288, quarter), lambda t, g: (t, 0, 0, 0)), gain_spec, gain_spec],
-            out_specs=pl.BlockSpec((16, 64, 384), lambda t, g: (0, 0, 0)),
-            scratch_shapes=[
-                pltpu.VMEM((1024, quarter), jnp.bfloat16),
-                pltpu.VMEM((1152, quarter), jnp.bfloat16),
-                pltpu.VMEM((1024, 1152), jnp.float32),
-            ],
-        ),
+        in_specs=[pl.BlockSpec(memory_space=pltpu.SMEM)] + [vmem] * (4 + len(pieces)),
+        out_specs=vmem,
+        scratch_shapes=[
+            pltpu.VMEM((1, 3, 256, quarter), jnp.bfloat16),
+            pltpu.VMEM((2, rows.shape[0], 768), jnp.float32),
+        ],
         out_shape=jax.ShapeDtypeStruct((16, 64, 384), jnp.bfloat16),
-        compiler_params=pltpu.CompilerParams(vmem_limit_bytes=50 * 2**20),
+        compiler_params=pltpu.CompilerParams(vmem_limit_bytes=28 * 2**20),
         name="project_attend",
-    )(group, *pieces, gathered, query_gain.reshape(1, 128), key_gain.reshape(1, 128))
+    )(where, rows, *pieces, query_gain.reshape(1, 128), key_gain.reshape(1, 128), before)
 
 
 def sources(core):
@@ -175,29 +315,43 @@
 def shards(video, norm_gain, w_query, w_key, w_value, query_gain, key_gain):
     seq = lax.axis_index("seq")
     fsdp = lax.axis_index("fsdp")
-    pair = lax.axis_index("dp") * 2 + fsdp // 4
+    z = lax.axis_index("dp") * 4 + fsdp // 2
     core = (fsdp % 2).astype(jnp.int32).reshape(1)
     group = (seq // 4 + seq % 4) % 4
+    where = jnp.stack([z, group, fsdp % 2]).astype(jnp.int32)
     d = video.shape[-1]
     quarter = d // 4
 
-    columns = [w.T for w in (w_query, w_key, w_value)]
-    quarters = [
-        jnp.concatenate([c[:, quarter * r : quarter * (r + 1)] for c in columns], axis=0) for r in range(4)
-    ]
+    quarters = pack([w.T for w in (w_query, w_key, w_value)])
     with jax.named_scope("scatter"):
-        mine = [quarters[0]] + [lax.ppermute(quarters[r], AXES, scatter_perm(r)) for r in (1, 3, 2)]
+        far, one, three = [lax.ppermute(quarters[r], AXES, scatter_perm(r)) for r in (2, 1, 3)]
+    part = choose(where, [quarters[0], one, far, three])
+
     normed = layer_normed(video, norm_gain)
     with jax.named_scope("rows_home"):
         home = lax.all_to_all(normed, "seq", split_axis=0, concat_axis=0, tiled=True).reshape(256, d)
-    mine, home = lax.optimization_barrier((mine, home))
-    part = lax.select_n((pair - group + 4) % 4, mine[0], mine[1], mine[3], mine[2])
-    gathered = lax.all_gather(part, ("dp", "fsdp"), axis=0, tiled=True)
-    gathered = gathered.reshape(4, 4, 288, quarter)
-
     with jax.named_scope("rows_line"):
-        pieces = [home] + [lax.ppermute(home, AXES, line_perm(s)) for s in SHIFTS[1:]]
-    output = attend(pieces, gathered, group.astype(jnp.int32).reshape(1), query_gain, key_gain)
+        rows = stack([home] + [lax.ppermute(home, AXES, line_perm(s)) for s in SHIFTS[1:]])
+
+    def swapped(piece):
+        with jax.named_scope("swap"):
+            return piece, lax.ppermute(piece, AXES, swap_perm())
+
+    with jax.named_scope("ring"):
+        ups, downs = [part], [part]
+        for _ in range(3):
+            ups.append(lax.ppermute(ups[-1], AXES, ring_perm(1)))
+            downs.append(lax.ppermute(downs[-1], AXES, ring_perm(-1)))
+        ups[3], downs[3], rows = lax.optimization_barrier((ups[3], downs[3], rows))
+        up_half, down_half = halve(ups[3], downs[3])
+        up_half = lax.ppermute(up_half, AXES, ring_perm(1))
+        down_half = lax.ppermute(down_half, AXES, ring_perm(-1))
+    early = swapped(part) + swapped(ups[1]) + swapped(downs[1]) + swapped(ups[2]) + swapped(downs[2])
+    total = project(where, rows, (0, -1, 1, -2, 2), early)
+    total = project(where, rows, (-3, 3), swapped(ups[3]) + swapped(downs[3]), (total,))
+    up_half, down_half, total = lax.optimization_barrier((up_half, down_half, total))
+    late = swapped(up_half) + swapped(down_half)
+    output = attend(where, rows, late, query_gain, key_gain, total)
     with jax.named_scope("heads_back"):
         received = lax.all_to_all(output, "seq", split_axis=0, concat_axis=0, tiled=True)
     return assemble(received, core)

time: 147 us -> 133 us (0.905)
  waiting for transfers between devices: 84.3 us -> 50.7 us
  blocking collectives: 0 us -> 21.3 us
  between operations: 13.5 us -> 0.15 us
  starting transfers between devices: 21.2 us -> 30.6 us
  Pallas kernels: 18.9 us -> 25.4 us
  other arithmetic: 3.64 us -> 0.08 us
  local copies, waits for them, and re-layouts: 4.63 us -> 3.14 us
    ppermute x3, waiting for transfers between devices: 35.4 us -> 0.01 us  [shards(): lax.ppermute(home, AXES, line_perm(s))]
    ppermute x0 -> x17, waiting for transfers between devices: none -> 25.6 us  [the longest x3 23.3 us: shards(): ups.append(lax.ppermute(ups[-1], AXES, ring_perm(1)))]
    ppermute x3, waiting for transfers between devices: 25.8 us -> 4.22 us  [shards(): lax.ppermute(quarters[r], AXES, scatter_perm(r))]
    all_to_all x0 -> x1, blocking collectives: none -> 21.3 us  [shards(): lax.all_to_all(output, 'seq', split_axis=0, concat_axis=0, tiled=True)]
    all_to_all x1, waiting for transfers between devices: 0.01 us -> 20.9 us  [shards(): lax.all_to_all(normed, 'seq', split_axis=0, concat_axis=0, tiled=True)]
    ppermute x0 -> x17, starting transfers between devices: none -> 16.1 us  [the longest x3 10.6 us: shards(): downs.append(lax.ppermute(downs[-1], AXES, ring_perm(-1)))]
    all_to_all x1 -> x0, waiting for transfers between devices: 13.7 us -> none  [shards(): lax.all_to_all(output, 'seq', split_axis=0, concat_axis=0, tiled=True)]
    all_gather x1 -> x0, waiting for transfers between devices: 9.33 us -> none  [shards(): gathered = lax.all_gather(part, ('dp', 'fsdp'), axis=0, tiled=True)]
  transfers between devices with their start and end apart: 9 -> 24, of which waited for: 6 -> 10; matrix products, arithmetic and copies ran while one was open for 2% -> 0% of each run, Pallas kernels for 0% -> 12%
where the time goes in v4:
time: 133 us; the launch traced here: 131 us
  waiting for transfers between devices  50.7 us (38%)
  starting transfers between devices  30.6 us (23%)
  Pallas kernels  25.4 us (19%)
  blocking collectives  21.3 us (16%)
  local copies, waits for them, and re-layouts  3.14 us (2%)
    ppermute x3, waiting for transfers between devices, shards(): ups.append(lax.ppermute(ups[-1], AXES, ring_perm(1)))  23.3 us
    all_to_all x1, blocking collectives, shards(): lax.all_to_all(output, 'seq', split_axis=0, concat_axis=0, tiled=True)  21.3 us
    all_to_all x1, waiting for transfers between devices, shards(): lax.all_to_all(normed, 'seq', split_axis=0, concat_axis=0, tiled=True)  20.9 us
    pallas_call x2, Pallas kernels, project(): pl.pallas_call(lambda *refs: project_kernel(offsets, *refs), in_specs=[pl...  11.4 us
    ppermute x3, starting transfers between devices, shards(): downs.append(lax.ppermute(downs[-1], AXES, ring_perm(-1)))  10.6 us
    all_to_all x1, starting transfers between devices, shards(): lax.all_to_all(normed, 'seq', split_axis=0, concat_axis=0, tiled=True)  7.39 us
    pallas_call x1, Pallas kernels, attend(): pl.pallas_call(attend_kernel, in_specs=[pl.BlockSpec(memory_space=pltpu.S...  5.95 us
    ppermute x3, waiting for transfers between devices, shards(): lax.ppermute(quarters[r], AXES, scatter_perm(r))  4.22 us
  transfers between devices with their start and end apart: 24, of which 10 were waited for; matrix products, arithmetic and copies ran while one was open for 0% of the time, Pallas kernels for 12%

profile of v4, /device:TPU:8, one launch (start us, length us, event | category | flops | bytes accessed | tf_op | source)
XLA Modules:
  0.0 131.4 jit_solution(14769474624024380313)
XLA Ops:
  0.0 1.4 %copy-done = bf16[1,2,128,3072]{3,2,1,0:T(8,128)(2,1)S(1)} copy-done((bf16[1,2,128,3072]{3,2,1,0:T(8,128)(2,1)S(1)}, bf16[1,2,128,3072]{3,2,1,0:T(8,128)(2,1)}, u32[]{:S(2)}) %copy-start) | copy-done | bytes 1572888
  1.4 0.7 copy-done.2
  2.1 2.6 %norm_rows.1 = bf16[16,16,3072]{2,1,0:T(8,128)(2,1)} custom-call(bf16[1,2,128,3072]{3,2,1,0:T(8,128)(2,1)S(1)} %copy-done, f32[1,3072]{1,0:T(1,128)S(1)} %bitcast.14), custom_call_target="tpu_custom_call" | custom-call | tf_op jit(solution)/shard_map/norm_rows/pallas_call | solution.py:100
  4.7 7.4 %all-to-all-start = ((bf16[16,16,3072]{2,1,0:T(8,128)(2,1)}), bf16[16,16,3072]{2,1,0:T(8,128)(2,1)S(1)}, u32[]{:S(2)}, u32[]{:S(2)}) async-start(bf16[16,16,3072]{2,1,0:T(8,128)(2,1)} %norm_rows.1), calls=%async_computation | async-start | bytes 3145728 | tf_op jit(solution)/shard_map/rows_home/all_to_all | solution.py:332
  12.1 2.7 %pack_weights.1 = (bf16[288,768]{1,0:T(8,128)(2,1)}, bf16[288,768]{1,0:T(8,128)(2,1)}, bf16[288,768]{1,0:T(8,128)(2,1)}, bf16[288,768]{1,0:T(8,128)(2,1)}) custom-call(bf16[96,3072]{1,0:T(8,128)(2,1)} %bitcast.17, bf16[96,3072]{1,0:T(8,128)(2,1)} %bitcast.18, bf16[96,3072]{1,0:T(8,128)(2,1)} %bitcast.19), custom_call_target="tpu_custom_call" | custom-call | tf_op jit(solution)/shard_map/pack_weights/pallas_call | solution.py:70
  14.8 1.5 %collective-permute-start = (bf16[288,768]{1,0:T(8,128)(2,1)}, bf16[288,768]{1,0:T(8,128)(2,1)}, u32[]{:S(2)}, u32[]{:S(2)}) collective-permute-start(bf16[288,768]{1,0:T(8,128)(2,1)} %get-tuple-element.18), channel_id=1, source_target_pairs={{0,4},{1,5},{2,6},{3,7},{12,136},{13,137},{14,138},{15,139},{144,1... | collective-permute-start | bytes 1327112 | tf_op jit(solution)/shard_map/scatter/ppermute | solution.py:327
  16.3 1.5 %collective-permute-start.1 = (bf16[288,768]{1,0:T(8,128)(2,1)}, bf16[288,768]{1,0:T(8,128)(2,1)}, u32[]{:S(2)}, u32[]{:S(2)}) collective-permute-start(bf16[288,768]{1,0:T(8,128)(2,1)} %get-tuple-element.19), channel_id=1, source_target_pairs={{64,128},{65,129},{66,130},{67,131},{76,140},{77,141},{78,142},{79... | collective-permute-start | bytes 1327112 | tf_op jit(solution)/shard_map/scatter/ppermute | solution.py:327
  17.7 1.3 collective-permute-start.2
  19.0 20.9 %all-to-all-done = bf16[16,16,3072]{2,1,0:T(8,128)(2,1)S(1)} async-done(((bf16[16,16,3072]{2,1,0:T(8,128)(2,1)}), bf16[16,16,3072]{2,1,0:T(8,128)(2,1)S(1)}, u32[]{:S(2)}, u32[]{:S(2)}) %all-to-all-start) | async-done | bytes 1572896 | tf_op jit(solution)/shard_map/rows_home/all_to_all | solution.py:332
  39.9 1.2 collective-permute-start.10
  41.2 0.2 collective-permute-start.11
  41.4 0.0 collective-permute-done.q1
  41.4 1.4 %collective-permute-start.9 = (bf16[256,3072]{1,0:T(8,128)(2,1)S(1)}, bf16[256,3072]{1,0:T(8,128)(2,1)S(1)}, u32[]{:S(2)}, u32[]{:S(2)}) collective-permute-start(bf16[256,3072]{1,0:T(8,128)(2,1)S(1)} %bitcast.12), channel_id=1, source_target_pairs={{0,32},{1,9},{2,34},{3,11},{4,36},{5,13},{6,38},{7,15},{128,160},{... | collective-permute-start | bytes 4718600 | tf_op jit(solution)/shard_map/rows_line/ppermute | solution.py:334
  42.8 0.1 pad_add_fusion.where.refs_0_
  42.9 0.0 collective-permute-done.1.q2
  42.9 4.2 %collective-permute-done.2.q3 = bf16[288,768]{1,0:T(8,128)(2,1)} collective-permute-done((bf16[288,768]{1,0:T(8,128)(2,1)}, bf16[288,768]{1,0:T(8,128)(2,1)}, u32[]{:S(2)}, u32[]{:S(2)}) %collective-permute-start.2) | collective-permute-done | bytes 442400 | tf_op jit(solution)/shard_map/scatter/ppermute | solution.py:327
  47.1 1.0 copy-done.1
  48.1 1.3 %choose_quarter.1.refs_2_ = bf16[288,768]{1,0:T(8,128)(2,1)S(1)} custom-call(s32[3]{0:T(128)S(1)} %pad_add_fusion.where.refs_0_, bf16[288,768]{1,0:T(8,128)(2,1)S(1)} %copy-done.1, bf16[288,768]{1,0:T(8,128)(2,1)} %collective-permute-done.q1, bf16[288,768]{1,0:T(8,128)(2,1)} %collective-permute-done.1.q2, bf16[288,768]{1,0:T(8,128)(2,1)} %collective-permute-done.2.q3), custom_call_target="tpu_custom_call" | custom-call | tf_op jit(solution)/shard_map/choose_quarter/pallas_call | solution.py:125
  49.5 0.1 collective-permute-start.3
  49.6 4.1 %collective-permute-start.6 = (bf16[288,768]{1,0:T(8,128)(2,1)S(1)}, bf16[288,768]{1,0:T(8,128)(2,1)S(1)}, u32[]{:S(2)}, u32[]{:S(2)}) collective-permute-start(bf16[288,768]{1,0:T(8,128)(2,1)S(1)} %choose_quarter.1.refs_2_), channel_id=1, source_target_pairs={{0,134},{1,135},{2,0},{3,1},{4,2},{5,3},{6,4},{7,5},{128,6},{129,7... | collective-permute-start | bytes 1327112 | tf_op jit(solution)/shard_map/ring/ppermute | solution.py:344
  53.7 8.6 %collective-permute-done.3.refs_4_ = bf16[288,768]{1,0:T(8,128)(2,1)S(1)} collective-permute-done((bf16[288,768]{1,0:T(8,128)(2,1)S(1)}, bf16[288,768]{1,0:T(8,128)(2,1)S(1)}, u32[]{:S(2)}, u32[]{:S(2)}) %collective-permute-start.3) | collective-permute-done | bytes 442400 | tf_op jit(solution)/shard_map/ring/ppermute | solution.py:343
  62.3 0.0 collective-permute-start.4
  62.3 0.0 collective-permute-done.6.refs_6_
  62.4 3.2 %collective-permute-start.7 = (bf16[288,768]{1,0:T(8,128)(2,1)S(1)}, bf16[288,768]{1,0:T(8,128)(2,1)S(1)}, u32[]{:S(2)}, u32[]{:S(2)}) collective-permute-start(bf16[288,768]{1,0:T(8,128)(2,1)S(1)} %collective-permute-done.6.refs_6_), channel_id=1, source_target_pairs={{0,134},{1,135},{2,0},{3,1},{4,2},{5,3},{6,4},{7,5},{128,6},{129,7... | collective-permute-start | bytes 1327112 | tf_op jit(solution)/shard_map/ring/ppermute | solution.py:344
  65.6 7.8 %collective-permute-done.4.refs_8_ = bf16[288,768]{1,0:T(8,128)(2,1)S(1)} collective-permute-done((bf16[288,768]{1,0:T(8,128)(2,1)S(1)}, bf16[288,768]{1,0:T(8,128)(2,1)S(1)}, u32[]{:S(2)}, u32[]{:S(2)}) %collective-permute-start.4) | collective-permute-done | bytes 442400 | tf_op jit(solution)/shard_map/ring/ppermute | solution.py:343
  73.4 0.0 collective-permute-start.5
  73.4 0.0 collective-permute-done.7.refs_10_
  73.4 3.2 %collective-permute-start.8 = (bf16[288,768]{1,0:T(8,128)(2,1)S(1)}, bf16[288,768]{1,0:T(8,128)(2,1)S(1)}, u32[]{:S(2)}, u32[]{:S(2)}) collective-permute-start(bf16[288,768]{1,0:T(8,128)(2,1)S(1)} %collective-permute-done.7.refs_10_), channel_id=1, source_target_pairs={{0,134},{1,135},{2,0},{3,1},{4,2},{5,3},{6,4},{7,5},{128,6},{129,7... | collective-permute-start | bytes 1327112 | tf_op jit(solution)/shard_map/ring/ppermute | solution.py:344
  76.6 6.9 %collective-permute-done.5.up.refs_2_ = bf16[288,768]{1,0:T(8,128)(2,1)S(1)} collective-permute-done((bf16[288,768]{1,0:T(8,128)(2,1)S(1)}, bf16[288,768]{1,0:T(8,128)(2,1)S(1)}, u32[]{:S(2)}, u32[]{:S(2)}) %collective-permute-start.5) | collective-permute-done | bytes 442400 | tf_op jit(solution)/shard_map/ring/ppermute | solution.py:343
  83.5 0.0 collective-permute-start.16
  83.5 0.0 collective-permute-done.10.r2
  83.5 0.5 collective-permute-start.17
  84.0 0.0 collective-permute-done.11.r3
  84.0 0.1 collective-permute-start.18
  84.1 0.0 collective-permute-done.9.r1
  84.1 0.4 collective-permute-start.19
  84.5 0.4 stack_rows.1.refs_1_.rows
  84.9 0.0 collective-permute-done.8.down.refs_4_
  84.9 0.2 collective-permute-start.20
  85.1 0.2 collective-permute-done.16.refs_3_
  85.3 0.3 collective-permute-start.14
  85.5 0.4 collective-permute-done.17.refs_5_
  85.9 0.1 collective-permute-start.15
  86.1 0.5 collective-permute-done.18.refs_7_
  86.5 3.1 %collective-permute-start.12 = (bf16[288,384]{1,0:T(8,128)(2,1)S(1)}, bf16[288,384]{1,0:T(8,128)(2,1)S(1)}, u32[]{:S(2)}, u32[]{:S(2)}) collective-permute-start(bf16[288,384]{1,0:T(8,128)(2,1)S(1)} %get-tuple-element.24), channel_id=1, source_target_pairs={{0,2},{1,3},{2,4},{3,5},{4,6},{5,7},{6,128},{7,129},{128,130},{129... | collective-permute-start | bytes 663560 | tf_op jit(solution)/shard_map/ring/ppermute | solution.py:347
  89.7 0.0 collective-permute-done.19.refs_9_
  89.7 0.1 collective-permute-start.13
  89.8 0.0 collective-permute-done.20.refs_11_
  89.8 7.8 %project.2.refs_6_ = f32[2,1024,768]{2,1,0:T(8,128)S(1)} custom-call(s32[3]{0:T(128)S(1)} %pad_add_fusion.where.refs_0_, bf16[1024,3072]{1,0:T(8,128)(2,1)S(1)} %stack_rows.1.refs_1_.rows, bf16[288,768]{1,0:T(8,128)(2,1)S(1)} %choose_quarter.1.refs_2_, bf16[288,768]{1,0:T(8,128)(2,1)S(1)} %collective-permute-done.16.refs_3_, ...), custom_call_target="tpu_custom_call" | custom-call | tf_op jit(solution)/shard_map/project/pallas_call | solution.py:213
  97.6 0.0 copy-start.3
  97.6 0.0 copy-start.4
  97.6 0.0 collective-permute-done.14.refs_3_
  97.7 0.0 collective-permute-done.15.refs_5_
  97.7 3.6 %project.3.before = f32[2,1024,768]{2,1,0:T(8,128)S(1)} custom-call(s32[3]{0:T(128)S(1)} %pad_add_fusion.where.refs_0_, bf16[1024,3072]{1,0:T(8,128)(2,1)S(1)} %stack_rows.1.refs_1_.rows, bf16[288,768]{1,0:T(8,128)(2,1)S(1)} %collective-permute-done.5.up.refs_2_, ...), custom_call_target="tpu_custom_call", output_to_operand_aliasing={{}: (6, {})} | custom-call | tf_op jit(solution)/shard_map/project/pallas_call | solution.py:213
  101.2 0.0 collective-permute-done.12.fh
  101.3 0.0 collective-permute-done.13.bh
  101.3 0.1 collective-permute-start.21
  101.4 0.5 collective-permute-start.22
  101.9 1.0 collective-permute-done.21.fho
  102.8 0.3 collective-permute-done.22.bho
  103.1 0.0 copy-done.3
  103.2 5.9 %project_attend.1 = bf16[16,64,384]{2,1,0:T(8,128)(2,1)S(1)} custom-call(s32[3]{0:T(128)S(1)} %pad_add_fusion.where.refs_0_, bf16[1024,3072]{1,0:T(8,128)(2,1)S(1)} %stack_rows.1.refs_1_.rows, bf16[288,384]{1,0:T(8,128)(2,1)S(1)} %collective-permute-done.12.fh, bf16[288,384]{1,0:T(8,128)(2,1)S(1)} %collective-permute-done.21.fho, ...), custom_call_target="tpu_custom_call" | custom-call | tf_op jit(solution)/shard_map/project_attend/pallas_call | solution.py:264
  109.1 21.3 %all_to_all.10.recv_ref = bf16[16,64,384]{2,1,0:T(8,128)(2,1)S(1)} all-to-all(bf16[16,64,384]{2,1,0:T(8,128)(2,1)S(1)} %project_attend.1), channel_id=1, replica_groups=mesh['dp'=2,'seq'=16,'fsdp'=8] {'seq'}, dimensions={0} | all-to-all | bytes 1572864 | tf_op jit(solution)/shard_map/heads_back/all_to_all | solution.py:356
  130.4 1.0 assemble_heads.1
  (5 shorter events, 0.0 us)
Async XLA Ops:
  0.0 1.4 %copy-start = (bf16[1,2,128,3072]{3,2,1,0:T(8,128)(2,1)S(1)}, bf16[1,2,128,3072]{3,2,1,0:T(8,128)(2,1)}, u32[]{:S(2)}) copy-start(bf16[1,2,128,3072]{3,2,1,0:T(8,128)(2,1)} %video_ref.1) | copy-start | bytes 4718596
  1.4 0.7 copy-start.2
  4.7 35.2 %all-to-all-start = ((bf16[16,16,3072]{2,1,0:T(8,128)(2,1)}), bf16[16,16,3072]{2,1,0:T(8,128)(2,1)S(1)}, u32[]{:S(2)}, u32[]{:S(2)}) async-start(bf16[16,16,3072]{2,1,0:T(8,128)(2,1)} %norm_rows.1), calls=%async_computation | async-start | bytes 3145728 | tf_op jit(solution)/shard_map/rows_home/all_to_all | solution.py:332
  14.8 26.6 %collective-permute-start = (bf16[288,768]{1,0:T(8,128)(2,1)}, bf16[288,768]{1,0:T(8,128)(2,1)}, u32[]{:S(2)}, u32[]{:S(2)}) collective-permute-start(bf16[288,768]{1,0:T(8,128)(2,1)} %get-tuple-element.18), channel_id=1, source_target_pairs={{0,4},{1,5},{2,6},{3,7},{12,136},{13,137},{14,138},{15,139},{144,1... | collective-permute-start | bytes 1327112 | tf_op jit(solution)/shard_map/scatter/ppermute | solution.py:327
  16.3 26.6 %collective-permute-start.1 = (bf16[288,768]{1,0:T(8,128)(2,1)}, bf16[288,768]{1,0:T(8,128)(2,1)}, u32[]{:S(2)}, u32[]{:S(2)}) collective-permute-start(bf16[288,768]{1,0:T(8,128)(2,1)} %get-tuple-element.19), channel_id=1, source_target_pairs={{64,128},{65,129},{66,130},{67,131},{76,140},{77,141},{78,142},{79... | collective-permute-start | bytes 1327112 | tf_op jit(solution)/shard_map/scatter/ppermute | solution.py:327
  17.7 29.4 %collective-permute-start.2 = (bf16[288,768]{1,0:T(8,128)(2,1)}, bf16[288,768]{1,0:T(8,128)(2,1)}, u32[]{:S(2)}, u32[]{:S(2)}) collective-permute-start(bf16[288,768]{1,0:T(8,128)(2,1)} %get-tuple-element.20), channel_id=1, source_target_pairs={{0,132},{1,133},{2,134},{3,135},{12,8},{13,9},{14,10},{15,11},{144... | collective-permute-start | bytes 1327112 | tf_op jit(solution)/shard_map/scatter/ppermute | solution.py:327
  39.9 43.5 %collective-permute-start.10 = (bf16[256,3072]{1,0:T(8,128)(2,1)S(1)}, bf16[256,3072]{1,0:T(8,128)(2,1)S(1)}, u32[]{:S(2)}, u32[]{:S(2)}) collective-permute-start(bf16[256,3072]{1,0:T(8,128)(2,1)S(1)} %bitcast.10), channel_id=1, source_target_pairs={{0,96},{1,25},{2,98},{3,27},{4,100},{5,29},{6,102},{7,31},{128,224... | collective-permute-start | bytes 4718600 | tf_op jit(solution)/shard_map/rows_line/ppermute | solution.py:334
  41.2 42.8 %collective-permute-start.11 = (bf16[256,3072]{1,0:T(8,128)(2,1)S(1)}, bf16[256,3072]{1,0:T(8,128)(2,1)S(1)}, u32[]{:S(2)}, u32[]{:S(2)}) collective-permute-start(bf16[256,3072]{1,0:T(8,128)(2,1)S(1)} %bitcast.11), channel_id=1, source_target_pairs={{0,64},{1,17},{2,66},{3,19},{4,68},{5,21},{6,70},{7,23},{128,192},... | collective-permute-start | bytes 4718600 | tf_op jit(solution)/shard_map/rows_line/ppermute | solution.py:334
  41.4 42.7 %collective-permute-start.9 = (bf16[256,3072]{1,0:T(8,128)(2,1)S(1)}, bf16[256,3072]{1,0:T(8,128)(2,1)S(1)}, u32[]{:S(2)}, u32[]{:S(2)}) collective-permute-start(bf16[256,3072]{1,0:T(8,128)(2,1)S(1)} %bitcast.12), channel_id=1, source_target_pairs={{0,32},{1,9},{2,34},{3,11},{4,36},{5,13},{6,38},{7,15},{128,160},{... | collective-permute-start | bytes 4718600 | tf_op jit(solution)/shard_map/rows_line/ppermute | solution.py:334
  47.1 1.0 copy-start.1
  49.5 12.9 %collective-permute-start.3 = (bf16[288,768]{1,0:T(8,128)(2,1)S(1)}, bf16[288,768]{1,0:T(8,128)(2,1)S(1)}, u32[]{:S(2)}, u32[]{:S(2)}) collective-permute-start(bf16[288,768]{1,0:T(8,128)(2,1)S(1)} %choose_quarter.1.refs_2_), channel_id=1, source_target_pairs={{0,2},{1,3},{2,4},{3,5},{4,6},{5,7},{6,128},{7,129},{128,130},{129... | collective-permute-start | bytes 1327112 | tf_op jit(solution)/shard_map/ring/ppermute | solution.py:343
  49.6 12.8 %collective-permute-start.6 = (bf16[288,768]{1,0:T(8,128)(2,1)S(1)}, bf16[288,768]{1,0:T(8,128)(2,1)S(1)}, u32[]{:S(2)}, u32[]{:S(2)}) collective-permute-start(bf16[288,768]{1,0:T(8,128)(2,1)S(1)} %choose_quarter.1.refs_2_), channel_id=1, source_target_pairs={{0,134},{1,135},{2,0},{3,1},{4,2},{5,3},{6,4},{7,5},{128,6},{129,7... | collective-permute-start | bytes 1327112 | tf_op jit(solution)/shard_map/ring/ppermute | solution.py:344
  62.3 11.0 %collective-permute-start.4 = (bf16[288,768]{1,0:T(8,128)(2,1)S(1)}, bf16[288,768]{1,0:T(8,128)(2,1)S(1)}, u32[]{:S(2)}, u32[]{:S(2)}) collective-permute-start(bf16[288,768]{1,0:T(8,128)(2,1)S(1)} %collective-permute-done.3.refs_4_), channel_id=1, source_target_pairs={{0,2},{1,3},{2,4},{3,5},{4,6},{5,7},{6,128},{7,129},{128,130},{129... | collective-permute-start | bytes 1327112 | tf_op jit(solution)/shard_map/ring/ppermute | solution.py:343
  62.4 11.0 %collective-permute-start.7 = (bf16[288,768]{1,0:T(8,128)(2,1)S(1)}, bf16[288,768]{1,0:T(8,128)(2,1)S(1)}, u32[]{:S(2)}, u32[]{:S(2)}) collective-permute-start(bf16[288,768]{1,0:T(8,128)(2,1)S(1)} %collective-permute-done.6.refs_6_), channel_id=1, source_target_pairs={{0,134},{1,135},{2,0},{3,1},{4,2},{5,3},{6,4},{7,5},{128,6},{129,7... | collective-permute-start | bytes 1327112 | tf_op jit(solution)/shard_map/ring/ppermute | solution.py:344
  73.4 10.1 %collective-permute-start.5 = (bf16[288,768]{1,0:T(8,128)(2,1)S(1)}, bf16[288,768]{1,0:T(8,128)(2,1)S(1)}, u32[]{:S(2)}, u32[]{:S(2)}) collective-permute-start(bf16[288,768]{1,0:T(8,128)(2,1)S(1)} %collective-permute-done.4.refs_8_), channel_id=1, source_target_pairs={{0,2},{1,3},{2,4},{3,5},{4,6},{5,7},{6,128},{7,129},{128,130},{129... | collective-permute-start | bytes 1327112 | tf_op jit(solution)/shard_map/ring/ppermute | solution.py:343
  73.4 11.5 %collective-permute-start.8 = (bf16[288,768]{1,0:T(8,128)(2,1)S(1)}, bf16[288,768]{1,0:T(8,128)(2,1)S(1)}, u32[]{:S(2)}, u32[]{:S(2)}) collective-permute-start(bf16[288,768]{1,0:T(8,128)(2,1)S(1)} %collective-permute-done.7.refs_10_), channel_id=1, source_target_pairs={{0,134},{1,135},{2,0},{3,1},{4,2},{5,3},{6,4},{7,5},{128,6},{129,7... | collective-permute-start | bytes 1327112 | tf_op jit(solution)/shard_map/ring/ppermute | solution.py:344
  83.5 1.8 %collective-permute-start.16 = (bf16[288,768]{1,0:T(8,128)(2,1)S(1)}, bf16[288,768]{1,0:T(8,128)(2,1)S(1)}, u32[]{:S(2)}, u32[]{:S(2)}) collective-permute-start(bf16[288,768]{1,0:T(8,128)(2,1)S(1)} %choose_quarter.1.refs_2_), channel_id=1, source_target_pairs={{0,1},{1,0},{2,3},{3,2},{4,5},{5,4},{6,7},{7,6},{128,129},{129,128... | collective-permute-start | bytes 1327112 | tf_op jit(solution)/shard_map/swap/ppermute | solution.py:338
  83.5 2.4 %collective-permute-start.17 = (bf16[288,768]{1,0:T(8,128)(2,1)S(1)}, bf16[288,768]{1,0:T(8,128)(2,1)S(1)}, u32[]{:S(2)}, u32[]{:S(2)}) collective-permute-start(bf16[288,768]{1,0:T(8,128)(2,1)S(1)} %collective-permute-done.3.refs_4_), channel_id=1, source_target_pairs={{0,1},{1,0},{2,3},{3,2},{4,5},{5,4},{6,7},{7,6},{128,129},{129,128... | collective-permute-start | bytes 1327112 | tf_op jit(solution)/shard_map/swap/ppermute | solution.py:338
  84.0 2.5 %collective-permute-start.18 = (bf16[288,768]{1,0:T(8,128)(2,1)S(1)}, bf16[288,768]{1,0:T(8,128)(2,1)S(1)}, u32[]{:S(2)}, u32[]{:S(2)}) collective-permute-start(bf16[288,768]{1,0:T(8,128)(2,1)S(1)} %collective-permute-done.6.refs_6_), channel_id=1, source_target_pairs={{0,1},{1,0},{2,3},{3,2},{4,5},{5,4},{6,7},{7,6},{128,129},{129,128... | collective-permute-start | bytes 1327112 | tf_op jit(solution)/shard_map/swap/ppermute | solution.py:338
  84.1 5.6 %collective-permute-start.19 = (bf16[288,768]{1,0:T(8,128)(2,1)S(1)}, bf16[288,768]{1,0:T(8,128)(2,1)S(1)}, u32[]{:S(2)}, u32[]{:S(2)}) collective-permute-start(bf16[288,768]{1,0:T(8,128)(2,1)S(1)} %collective-permute-done.4.refs_8_), channel_id=1, source_target_pairs={{0,1},{1,0},{2,3},{3,2},{4,5},{5,4},{6,7},{7,6},{128,129},{129,128... | collective-permute-start | bytes 1327112 | tf_op jit(solution)/shard_map/swap/ppermute | solution.py:338
  84.9 4.9 %collective-permute-start.20 = (bf16[288,768]{1,0:T(8,128)(2,1)S(1)}, bf16[288,768]{1,0:T(8,128)(2,1)S(1)}, u32[]{:S(2)}, u32[]{:S(2)}) collective-permute-start(bf16[288,768]{1,0:T(8,128)(2,1)S(1)} %collective-permute-done.7.refs_10_), channel_id=1, source_target_pairs={{0,1},{1,0},{2,3},{3,2},{4,5},{5,4},{6,7},{7,6},{128,129},{129,128... | collective-permute-start | bytes 1327112 | tf_op jit(solution)/shard_map/swap/ppermute | solution.py:338
  85.3 12.4 %collective-permute-start.14 = (bf16[288,768]{1,0:T(8,128)(2,1)S(1)}, bf16[288,768]{1,0:T(8,128)(2,1)S(1)}, u32[]{:S(2)}, u32[]{:S(2)}) collective-permute-start(bf16[288,768]{1,0:T(8,128)(2,1)S(1)} %collective-permute-done.5.up.refs_2_), channel_id=1, source_target_pairs={{0,1},{1,0},{2,3},{3,2},{4,5},{5,4},{6,7},{7,6},{128,129},{129,128... | collective-permute-start | bytes 1327112 | tf_op jit(solution)/shard_map/swap/ppermute | solution.py:338
  85.9 11.8 %collective-permute-start.15 = (bf16[288,768]{1,0:T(8,128)(2,1)S(1)}, bf16[288,768]{1,0:T(8,128)(2,1)S(1)}, u32[]{:S(2)}, u32[]{:S(2)}) collective-permute-start(bf16[288,768]{1,0:T(8,128)(2,1)S(1)} %collective-permute-done.8.down.refs_4_), channel_id=1, source_target_pairs={{0,1},{1,0},{2,3},{3,2},{4,5},{5,4},{6,7},{7,6},{128,129},{129,128... | collective-permute-start | bytes 1327112 | tf_op jit(solution)/shard_map/swap/ppermute | solution.py:338
  86.5 14.7 %collective-permute-start.12 = (bf16[288,384]{1,0:T(8,128)(2,1)S(1)}, bf16[288,384]{1,0:T(8,128)(2,1)S(1)}, u32[]{:S(2)}, u32[]{:S(2)}) collective-permute-start(bf16[288,384]{1,0:T(8,128)(2,1)S(1)} %get-tuple-element.24), channel_id=1, source_target_pairs={{0,2},{1,3},{2,4},{3,5},{4,6},{5,7},{6,128},{7,129},{128,130},{129... | collective-permute-start | bytes 663560 | tf_op jit(solution)/shard_map/ring/ppermute | solution.py:347
  89.7 11.6 %collective-permute-start.13 = (bf16[288,384]{1,0:T(8,128)(2,1)S(1)}, bf16[288,384]{1,0:T(8,128)(2,1)S(1)}, u32[]{:S(2)}, u32[]{:S(2)}) collective-permute-start(bf16[288,384]{1,0:T(8,128)(2,1)S(1)} %get-tuple-element.25), channel_id=1, source_target_pairs={{0,134},{1,135},{2,0},{3,1},{4,2},{5,3},{6,4},{7,5},{128,6},{129,7... | collective-permute-start | bytes 663560 | tf_op jit(solution)/shard_map/ring/ppermute | solution.py:348
  97.6 5.5 %copy-start.3 = (f32[128]{0:T(128)S(1)}, f32[128]{0:T(128)}, u32[]{:S(2)}) copy-start(f32[128]{0:T(128)} %param.12) | copy-start | bytes 1540
  97.6 5.5 %copy-start.4 = (f32[128]{0:T(128)S(1)}, f32[128]{0:T(128)}, u32[]{:S(2)}) copy-start(f32[128]{0:T(128)} %param.13) | copy-start | bytes 1540
  101.3 1.6 %collective-permute-start.21 = (bf16[288,384]{1,0:T(8,128)(2,1)S(1)}, bf16[288,384]{1,0:T(8,128)(2,1)S(1)}, u32[]{:S(2)}, u32[]{:S(2)}) collective-permute-start(bf16[288,384]{1,0:T(8,128)(2,1)S(1)} %collective-permute-done.12.fh), channel_id=1, source_target_pairs={{0,1},{1,0},{2,3},{3,2},{4,5},{5,4},{6,7},{7,6},{128,129},{129,128... | collective-permute-start | bytes 663560 | tf_op jit(solution)/shard_map/swap/ppermute | solution.py:338
  101.4 1.8 %collective-permute-start.22 = (bf16[288,384]{1,0:T(8,128)(2,1)S(1)}, bf16[288,384]{1,0:T(8,128)(2,1)S(1)}, u32[]{:S(2)}, u32[]{:S(2)}) collective-permute-start(bf16[288,384]{1,0:T(8,128)(2,1)S(1)} %collective-permute-done.13.bh), channel_id=1, source_target_pairs={{0,1},{1,0},{2,3},{3,2},{4,5},{5,4},{6,7},{7,6},{128,129},{129,128... | collective-permute-start | bytes 663560 | tf_op jit(solution)/shard_map/swap/ppermute | solution.py:338

commit v5 on v4

v5 whole, which is shorter than its diff:
```python
import jax
import jax.numpy as jnp
from jax import lax
from jax.experimental import pallas as pl
from jax.experimental.pallas import tpu as pltpu
from jax.sharding import PartitionSpec as P

AXES = ("dp", "seq", "fsdp")
SHIFTS = (0, 1, 3, 2)


def place(x, y, z, core):
    return ((z // 4) * 16 + x * 4 + y) * 8 + (z % 4) * 2 + core


def every_place():
    return [(x, y, z, c) for x in range(4) for y in range(4) for z in range(8) for c in range(2)]


def scatter_perm(shift):
    pairs = []
    for x in range(4):
        for y in range(4):
            j = (x + y) % 4
            origin = (x + 2) % 4 if shift == 2 else x
            for a in range(2):
                for c in range(2):
                    z = 2 * j + a
                    pairs.append((place(origin, y, z, c), place(x, y, (z + 2 * shift) % 8, c)))
    return pairs


def line_perm(shift):
    pairs = []
    for x, y, z, c in every_place():
        to = ((x + shift) % 4, y) if c == 0 else (x, (y + shift) % 4)
        pairs.append((place(x, y, z, c), place(to[0], to[1], z, c)))
    return pairs


def cross_perm(shift):
    pairs = []
    for x, y, z, c in every_place():
        to = (x, (y + shift) % 4) if c == 0 else ((x + shift) % 4, y)
        pairs.append((place(x, y, z, c), place(to[0], to[1], z, c)))
    return pairs


def ring_perm(step):
    return [(place(x, y, z, c), place(x, y, (z + step) % 8, c)) for x, y, z, c in every_place()]


def swap_perm():
    return [(place(x, y, z, c), place(x, y, z, 1 - c)) for x, y, z, c in every_place()]


def prepare_kernel(where, video, wq, wk, wv, f0, f1, f2, f3, q0, q1, q2, q3, frames, columns, packed, sems, out_sems):
    cross = jnp.where(where[2] == 0, where[4], where[3])
    step, height, quarter = frames.shape[2], columns.shape[1], packed.shape[2]
    fetch_columns = [pltpu.make_async_copy(w, columns.at[m], sems.at[m]) for m, w in enumerate((wq, wk, wv))]
    fetch_frames = []
    for s in range(4):
        at = pl.multiple_of((cross + s) % 4 * step, step)
        fetch_frames.append(
            pltpu.make_async_copy(video.at[0, :, pl.ds(at, step), :], frames.at[s], sems.at[3 + s])
        )
    for copy in fetch_columns + fetch_frames:
        copy.start()
    stores = []
    for copy in fetch_columns:
        copy.wait()
    for r, out in ((2, q2), (1, q1), (3, q3), (0, q0)):
        for m in range(3):
            packed[r, height * m : height * (m + 1), :] = columns[m, :, quarter * r : quarter * (r + 1)]
        stores.append(pltpu.make_async_copy(packed.at[r], out, out_sems.at[r]))
        stores[-1].start()
    for s, out in enumerate((f0, f1, f2, f3)):
        fetch_frames[s].wait()
        stores.append(pltpu.make_async_copy(frames.at[s], out, out_sems.at[4 + s]))
        stores[-1].start()
    for store in stores:
        store.wait()


def prepare(where, video, columns):
    _, frames, patches, d = video.shape
    height = columns[0].shape[0]
    anywhere = pl.BlockSpec(memory_space=pl.ANY)
    return pl.pallas_call(
        prepare_kernel,
        in_specs=[pl.BlockSpec(memory_space=pltpu.SMEM)] + [anywhere] * 4,
        out_specs=[anywhere] * 8,
        out_shape=[jax.ShapeDtypeStruct((frames, patches // 4, d), jnp.bfloat16)] * 4
        + [jax.ShapeDtypeStruct((3 * height, d // 4), jnp.bfloat16)] * 4,
        scratch_shapes=[
            pltpu.VMEM((4, frames, patches // 4, d), jnp.bfloat16),
            pltpu.VMEM((3, height, d), jnp.bfloat16),
            pltpu.VMEM((4, 3 * height, d // 4), jnp.bfloat16),
            pltpu.SemaphoreType.DMA((7,)),
            pltpu.SemaphoreType.DMA((8,)),
        ],
        compiler_params=pltpu.CompilerParams(vmem_limit_bytes=60 * 2**20),
        name="prepare",
    )(where, video, *columns)


def norm_kernel(f0, f1, f2, f3, gain, out):
    at = 0
    for ref in (f0, f1, f2, f3):
        for f in range(ref.shape[0]):
            values = ref[f].astype(jnp.float32)
            average = jnp.mean(values, axis=-1, keepdims=True)
            centred = values - average
            spread = jnp.mean(centred * centred, axis=-1, keepdims=True)
            normed = centred * lax.rsqrt(spread + 1e-06) * gain[...]
            out[at : at + ref.shape[1], :] = normed.astype(jnp.bfloat16)
            at += ref.shape[1]


def layer_normed(blocks, gain):
    vmem = pl.BlockSpec(memory_space=pltpu.VMEM)
    frames, patches, d = blocks[0].shape
    return pl.pallas_call(
        norm_kernel,
        in_specs=[vmem] * 5,
        out_specs=vmem,
        out_shape=jax.ShapeDtypeStruct((4 * frames * patches, d), jnp.bfloat16),
        compiler_params=pltpu.CompilerParams(vmem_limit_bytes=10 * 2**20),
        name="norm_rows",
    )(*blocks, gain.reshape(1, d))


def choose_kernel(where, q0, q1, q2, q3, out_ref, sem):
    quarter = (where[0] // 2 - where[1] + 4) % 4
    for r, ref in enumerate((q0, q1, q2, q3)):

        @pl.when(quarter == r)
        def _(ref=ref):
            copy = pltpu.make_async_copy(ref, out_ref, sem)
            copy.start()
            copy.wait()


def choose(where, parts):
    anywhere = pl.BlockSpec(memory_space=pl.ANY)
    return pl.pallas_call(
        choose_kernel,
        in_specs=[pl.BlockSpec(memory_space=pltpu.SMEM)] + [anywhere] * 4,
        out_specs=anywhere,
        out_shape=jax.ShapeDtypeStruct(parts[0].shape, parts[0].dtype),
        scratch_shapes=[pltpu.SemaphoreType.DMA],
        compiler_params=pltpu.CompilerParams(vmem_limit_bytes=4 * 2**20),
        name="choose_quarter",
    )(where, *parts)


def halve_kernel(up, down, up_half, down_half):
    width = up_half.shape[1]
    up_half[...] = up[:, :width]
    down_half[...] = down[:, width:]


def halve(up, down):
    vmem = pl.BlockSpec(memory_space=pltpu.VMEM)
    half = jax.ShapeDtypeStruct((up.shape[0], up.shape[1] // 2), up.dtype)
    return pl.pallas_call(
        halve_kernel,
        in_specs=[vmem] * 2,
        out_specs=[vmem] * 2,
        out_shape=[half, half],
        compiler_params=pltpu.CompilerParams(vmem_limit_bytes=8 * 2**20),
        name="halve",
    )(up, down)


NT = (((1,), (1,)), ((), ()))


def stack_kernel(r0, r1, r2, r3, out_ref):
    for i, ref in enumerate((r0, r1, r2, r3)):
        out_ref[256 * i : 256 * i + 256, :] = ref[...]


def stack(pieces):
    vmem = pl.BlockSpec(memory_space=pltpu.VMEM)
    rows, d = pieces[0].shape
    return pl.pallas_call(
        stack_kernel,
        in_specs=[vmem] * 4,
        out_specs=vmem,
        out_shape=jax.ShapeDtypeStruct((4 * rows, d), jnp.bfloat16),
        compiler_params=pltpu.CompilerParams(vmem_limit_bytes=16 * 2**20),
        name="stack_rows",
    )(*pieces)


def add_products(where, rows, weights, turn, offset, own, other, total, first):
    z = (where[0] + offset + 8) % 8
    r = (z // 2 - where[1] + 4) % 4
    quarter = weights.shape[-1]
    for core, parts in ((where[2], own), (1 - where[2], other)):
        at = 0
        for ref in parts:
            width = ref.shape[1]
            for m in range(3):
                for g in range(3):
                    to = pl.multiple_of((z % 2 * 128 + core * 96 + 32 * g) % 192, 32)
                    low = 96 * m + 32 * g
                    weights[turn, m, pl.ds(to, 32), at : at + width] = ref[low : low + 32, :]
            at += width
    for m in range(3):
        weights[turn, m, 192:, :] = jnp.zeros((64, quarter), jnp.bfloat16)
    product = lax.dot_general(
        rows[:, pl.ds(pl.multiple_of(r * quarter, 128), quarter)],
        weights[turn].reshape(768, quarter),
        NT,
        preferred_element_type=jnp.float32,
    )
    product = product.reshape(total.shape[1:])
    if first:
        total[z % 2] = product
    else:
        total[z % 2] = total[z % 2] + product


def project_kernel(offsets, where, rows, *refs):
    pieces, total, weights = refs[: 2 * len(offsets)], refs[-2], refs[-1]
    for turn, offset in enumerate(offsets):
        own, other = [[pieces[2 * turn + side]] for side in range(2)]
        add_products(where, rows, weights, turn, offset, own, other, total, offset in (0, -1))


def project(where, rows, offsets, pieces, before=()):
    vmem = pl.BlockSpec(memory_space=pltpu.VMEM)
    quarter = rows.shape[1] // 4
    return pl.pallas_call(
        lambda *refs: project_kernel(offsets, *refs),
        in_specs=[pl.BlockSpec(memory_space=pltpu.SMEM)] + [vmem] * (1 + len(pieces) + len(before)),
        out_specs=vmem,
        out_shape=jax.ShapeDtypeStruct((2, 32, 4, 8, 768), jnp.float32),
        scratch_shapes=[pltpu.VMEM((len(offsets), 3, 256, quarter), jnp.bfloat16)],
        input_output_aliases={2 + len(pieces): 0} if before else {},
        compiler_params=pltpu.CompilerParams(vmem_limit_bytes=20 * 2**20),
        name="project",
    )(where, rows, *pieces, *before)


def head_columns(total, g, m, h):
    at = 256 * m
    if h == 1:
        halves = [total[half, :, g, :, at + 128 : at + 192] for half in range(2)]
        return jnp.concatenate(halves, axis=-1).reshape(256, 128)
    return total[h // 2, :, g, :, at : at + 128].reshape(256, 128)


def attend_kernel(where, rows, fh, fho, bh, bho, qg_ref, kg_ref, before, out_ref, weights, total, found):
    total[...] = before[...]
    add_products(where, rows, weights, 0, 4, [fh, bh], [fho, bho], total, False)

    @pl.when(where[0] >= 0)
    def _():
        gains = qg_ref[...] * kg_ref[...] * (128.0**-0.5)
        row_patch = lax.broadcasted_iota(jnp.int32, (256, 256), 0) % 8
        col_patch = lax.broadcasted_iota(jnp.int32, (256, 256), 1) % 8
        same = row_patch == col_patch
        for g in range(4):
            for h in range(3):
                q_rows = head_columns(total, g, 0, h).astype(jnp.bfloat16)
                k = head_columns(total, g, 1, h).astype(jnp.bfloat16).astype(jnp.float32)
                v = head_columns(total, g, 2, h).astype(jnp.bfloat16)
                q = q_rows.astype(jnp.float32)
                q_scale = lax.rsqrt(jnp.mean(q * q, axis=-1, keepdims=True) + 1e-06)
                k_scale = lax.rsqrt(jnp.mean(k * k, axis=-1, keepdims=True) + 1e-06)
                k_unit = (k * k_scale * gains).astype(jnp.bfloat16)
                scores = lax.dot_general(q_rows, k_unit, NT, preferred_element_type=jnp.float32)
                exps = jnp.where(same, jnp.exp(scores * q_scale), 0.0)
                probs = (exps / jnp.sum(exps, axis=-1, keepdims=True)).astype(jnp.bfloat16)
                out = jnp.dot(probs, v, preferred_element_type=jnp.float32)
                found[:, g, :, 128 * h : 128 * h + 128] = out.reshape(32, 8, 128)
        core = where[2]
        along = jnp.where(core == 0, where[3], where[4])
        cross = jnp.where(core == 0, where[4], where[3])
        for piece, shift in enumerate(SHIFTS):
            for s in range(4):
                line, side = (along - shift + 4) % 4, (cross - s + 4) % 4
                to = jnp.where(core == 0, 4 * line + side, 4 * side + line)
                frame = 8 * piece + 2 * s
                out_ref[to] = found[frame : frame + 2].reshape(64, 384).astype(jnp.bfloat16)


def attend(where, rows, pieces, query_gain, key_gain, before):
    vmem = pl.BlockSpec(memory_space=pltpu.VMEM)
    quarter = rows.shape[1] // 4
    return pl.pallas_call(
        attend_kernel,
        in_specs=[pl.BlockSpec(memory_space=pltpu.SMEM)] + [vmem] * (4 + len(pieces)),
        out_specs=vmem,
        scratch_shapes=[
            pltpu.VMEM((1, 3, 256, quarter), jnp.bfloat16),
            pltpu.VMEM((2, 32, 4, 8, 768), jnp.float32),
            pltpu.VMEM((32, 4, 8, 384), jnp.float32),
        ],
        out_shape=jax.ShapeDtypeStruct((16, 64, 384), jnp.bfloat16),
        compiler_params=pltpu.CompilerParams(vmem_limit_bytes=30 * 2**20),
        name="project_attend",
    )(where, rows, *pieces, query_gain.reshape(1, 128), key_gain.reshape(1, 128), before)


def assemble_kernel(where, recv_ref, out_ref):
    for core in range(2):

        @pl.when(where[2] == core)
        def _(core=core):
            for x in range(4):
                for y in range(4):
                    at, j = 32 * (y if core == 0 else x), (x + y) % 4
                    for f in range(2):
                        out_ref[0, f, at : at + 32, 384 * j : 384 * j + 384] = recv_ref[
                            4 * x + y, 32 * f : 32 * f + 32, :
                        ]


def assemble(received, where):
    return pl.pallas_call(
        assemble_kernel,
        in_specs=[pl.BlockSpec(memory_space=pltpu.SMEM), pl.BlockSpec(memory_space=pltpu.VMEM)],
        out_specs=pl.BlockSpec(memory_space=pltpu.VMEM),
        out_shape=jax.ShapeDtypeStruct((1, 2, 128, 1536), jnp.bfloat16),
        compiler_params=pltpu.CompilerParams(vmem_limit_bytes=40 * 2**20),
        name="assemble_heads",
    )(where, received)


def shards(video, norm_gain, w_query, w_key, w_value, query_gain, key_gain):
    seq = lax.axis_index("seq")
    fsdp = lax.axis_index("fsdp")
    z = lax.axis_index("dp") * 4 + fsdp // 2
    group = (seq // 4 + seq % 4) % 4
    where = jnp.stack([z, group, fsdp % 2, seq // 4, seq % 4]).astype(jnp.int32)

    *blocks, q0, q1, q2, q3 = prepare(where, video, [w.T for w in (w_query, w_key, w_value)])
    with jax.named_scope("rows_cross"):
        blocks = [blocks[0]] + [lax.ppermute(blocks[s], AXES, cross_perm(s)) for s in (1, 2, 3)]
    with jax.named_scope("scatter"):
        q2, q1, q3 = [lax.ppermute(q, AXES, scatter_perm(r)) for r, q in ((2, q2), (1, q1), (3, q3))]
    part = choose(where, [q0, q1, q2, q3])

    home = layer_normed(blocks, norm_gain)
    with jax.named_scope("rows_line"):
        rows = stack([home] + [lax.ppermute(home, AXES, line_perm(s)) for s in SHIFTS[1:]])

    def swapped(piece):
        with jax.named_scope("swap"):
            return piece, lax.ppermute(piece, AXES, swap_perm())

    def onward(up, down):
        with jax.named_scope("ring"):
            return lax.ppermute(up, AXES, ring_perm(1)), lax.ppermute(down, AXES, ring_perm(-1))

    up1, down1 = onward(part, part)
    up2, down2 = onward(up1, down1)
    up3, down3 = onward(up2, down2)
    early = swapped(part) + swapped(up1) + swapped(down1) + swapped(up2) + swapped(down2)
    total = project(where, rows, (0, -1, 1, -2, 2), early)
    up3, down3, total = lax.optimization_barrier((up3, down3, total))
    up4, down4 = onward(*halve(up3, down3))
    total = project(where, rows, (-3, 3), swapped(up3) + swapped(down3), (total,))
    up4, down4, total = lax.optimization_barrier((up4, down4, total))
    output = attend(where, rows, swapped(up4) + swapped(down4), query_gain, key_gain, total)
    with jax.named_scope("heads_back"):
        received = lax.all_to_all(output, "seq", split_axis=0, concat_axis=0, tiled=True)
    return assemble(received, where)


def solution(mesh):
    in_specs = (
        P(("dp", "fsdp"), "seq", None, None),
        P(),
        P(None, ("dp", "fsdp")),
        P(None, ("dp", "fsdp")),
        P(None, ("dp", "fsdp")),
        P(),
        P(),
    )
    out_specs = P(("dp", "fsdp"), "seq", None, None)
    return jax.shard_map(shards, mesh=mesh, in_specs=in_specs, out_specs=out_specs, check_vma=False)
```

time: 133 us -> 122 us (0.917)
  waiting for transfers between devices: 50.7 us -> 41 us
  local copies, waits for them, and re-layouts: 3.14 us -> 1.68 us
    all_to_all x1 -> x0, waiting for transfers between devices: 20.9 us -> none  [shards(): lax.all_to_all(normed, 'seq', split_axis=0, concat_axis=0, tiled=True)]
    ppermute x11 -> x14, waiting for transfers between devices: 27.5 us -> 36.6 us  [the longest x4 22.3 us: onward(): lax.ppermute(up, AXES, ring_perm(1))]
    all_to_all x1 -> x0, starting transfers between devices: 7.39 us -> none  [shards(): lax.all_to_all(normed, 'seq', split_axis=0, concat_axis=0, tiled=True)]
    ppermute x3, starting transfers between devices: 2.87 us -> 7.4 us  [shards(): lax.ppermute(home, AXES, line_perm(s))]
    ppermute x11 -> x14, starting transfers between devices: 18.1 us -> 21.6 us  [the longest x4 10.4 us: onward(): lax.ppermute(down, AXES, ring_perm(-1))]
    unnamed x10 -> x12, local copies, waits for them, and re-layouts: 3.14 us -> 1.01 us
    ppermute x9, waiting for transfers between devices: 2.28 us -> 4.35 us  [swapped(): return (piece, lax.ppermute(piece, AXES, swap_perm()))]
  transfers between devices with their start and end apart: 24 -> 26, of which waited for: 10 -> 14; matrix products, arithmetic and copies ran while one was open for 0% -> 0% of each run, Pallas kernels for 12% -> 11%
where the time goes in v5:
time: 122 us; the launch traced here: 120 us
  waiting for transfers between devices  41 us (34%)
  starting transfers between devices  30.8 us (25%)
  Pallas kernels  25 us (20%)
  blocking collectives  21.5 us (18%)
  local copies, waits for them, and re-layouts  1.68 us (1%)
    ppermute x4, waiting for transfers between devices, onward(): lax.ppermute(up, AXES, ring_perm(1))  22.3 us
    all_to_all x1, blocking collectives, shards(): lax.all_to_all(output, 'seq', split_axis=0, concat_axis=0, tiled=True)  21.5 us
    pallas_call x2, Pallas kernels, project(): pl.pallas_call(lambda *refs: project_kernel(offsets, *refs), in_specs=[pl...  11.4 us
    ppermute x4, starting transfers between devices, onward(): lax.ppermute(down, AXES, ring_perm(-1))  10.4 us
    ppermute x3, starting transfers between devices, shards(): lax.ppermute(home, AXES, line_perm(s))  7.4 us
    ppermute x3, waiting for transfers between devices, shards(): lax.ppermute(q, AXES, scatter_perm(r))  7.36 us
    ppermute x3, starting transfers between devices, shards(): lax.ppermute(blocks[s], AXES, cross_perm(s))  6.79 us
    ppermute x3, waiting for transfers between devices, shards(): lax.ppermute(blocks[s], AXES, cross_perm(s))  6.68 us
  transfers between devices with their start and end apart: 26, of which 14 were waited for; matrix products, arithmetic and copies ran while one was open for 0% of the time, Pallas kernels for 11%

profile of v5, /device:TPU:8, one launch (start us, length us, event | category | flops | bytes accessed | tf_op | source)
XLA Modules:
  0.0 120.2 jit_solution(8988325817607430495)
XLA Ops:
  0.0 0.7 stack.23.where.refs_0_
  0.7 4.1 %prepare.1 = (bf16[2,32,3072]{2,1,0:T(8,128)(2,1)}, bf16[2,32,3072]{2,1,0:T(8,128)(2,1)}, bf16[2,32,3072]{2,1,0:T(8,128)(2,1)}, bf16[2,32,3072]{2,1,0:T(8,128)(2...) custom-call(s32[5]{0:T(128)} %stack.23.where.refs_0_, ...), custom_call_target="tpu_custom_call" | custom-call | tf_op jit(solution)/shard_map/prepare/pallas_call | solution.py:89
  4.8 1.7 %collective-permute-start = (bf16[2,32,3072]{2,1,0:T(8,128)(2,1)}, bf16[2,32,3072]{2,1,0:T(8,128)(2,1)S(1)}, u32[]{:S(2)}, u32[]{:S(2)}) collective-permute-start(bf16[2,32,3072]{2,1,0:T(8,128)(2,1)} %get-tuple-element.22), channel_id=1, source_target_pairs={{0,8},{1,33},{2,10},{3,35},{4,12},{5,37},{6,14},{7,39},{128,136},{... | collective-permute-start | bytes 1179656 | tf_op jit(solution)/shard_map/rows_cross/ppermute | solution.py:343
  6.4 0.7 collective-permute-start.6
  7.1 3.4 %collective-permute-start.1 = (bf16[2,32,3072]{2,1,0:T(8,128)(2,1)}, bf16[2,32,3072]{2,1,0:T(8,128)(2,1)S(1)}, u32[]{:S(2)}, u32[]{:S(2)}) collective-permute-start(bf16[2,32,3072]{2,1,0:T(8,128)(2,1)} %get-tuple-element.23), channel_id=1, source_target_pairs={{0,16},{1,65},{2,18},{3,67},{4,20},{5,69},{6,22},{7,71},{128,144},... | collective-permute-start | bytes 1179656 | tf_op jit(solution)/shard_map/rows_cross/ppermute | solution.py:343
  10.5 1.8 %collective-permute-start.2 = (bf16[2,32,3072]{2,1,0:T(8,128)(2,1)}, bf16[2,32,3072]{2,1,0:T(8,128)(2,1)S(1)}, u32[]{:S(2)}, u32[]{:S(2)}) collective-permute-start(bf16[2,32,3072]{2,1,0:T(8,128)(2,1)} %get-tuple-element.24), channel_id=1, source_target_pairs={{0,24},{1,97},{2,26},{3,99},{4,28},{5,101},{6,30},{7,103},{128,152... | collective-permute-start | bytes 1179656 | tf_op jit(solution)/shard_map/rows_cross/ppermute | solution.py:343
  12.3 0.7 collective-permute-start.7
  12.9 0.1 collective-permute-done.f1
  13.0 1.3 %collective-permute-start.8 = (bf16[288,768]{1,0:T(8,128)(2,1)}, bf16[288,768]{1,0:T(8,128)(2,1)S(1)}, u32[]{:S(2)}, u32[]{:S(2)}) collective-permute-start(bf16[288,768]{1,0:T(8,128)(2,1)} %get-tuple-element.28), channel_id=1, source_target_pairs={{0,132},{1,133},{2,134},{3,135},{12,8},{13,9},{14,10},{15,11},{144... | collective-permute-start | bytes 1327112 | tf_op jit(solution)/shard_map/scatter/ppermute | solution.py:345
  14.3 2.5 %collective-permute-done.1.f2 = bf16[2,32,3072]{2,1,0:T(8,128)(2,1)S(1)} collective-permute-done((bf16[2,32,3072]{2,1,0:T(8,128)(2,1)}, bf16[2,32,3072]{2,1,0:T(8,128)(2,1)S(1)}, u32[]{:S(2)}, u32[]{:S(2)}) %collective-permute-start.1) | collective-permute-done | bytes 393248 | tf_op jit(solution)/shard_map/rows_cross/ppermute | solution.py:343
  16.8 4.1 %collective-permute-done.2.f3 = bf16[2,32,3072]{2,1,0:T(8,128)(2,1)S(1)} collective-permute-done((bf16[2,32,3072]{2,1,0:T(8,128)(2,1)}, bf16[2,32,3072]{2,1,0:T(8,128)(2,1)S(1)}, u32[]{:S(2)}, u32[]{:S(2)}) %collective-permute-start.2) | collective-permute-done | bytes 393248 | tf_op jit(solution)/shard_map/rows_cross/ppermute | solution.py:343
  20.9 0.0 copy-done.3
  20.9 1.0 copy-done.1
  21.9 1.0 norm_rows.1.r0
  23.0 3.5 %collective-permute-start.3 = (bf16[256,3072]{1,0:T(8,128)(2,1)S(1)}, bf16[256,3072]{1,0:T(8,128)(2,1)S(1)}, u32[]{:S(2)}, u32[]{:S(2)}) collective-permute-start(bf16[256,3072]{1,0:T(8,128)(2,1)S(1)} %norm_rows.1.r0), channel_id=1, source_target_pairs={{0,32},{1,9},{2,34},{3,11},{4,36},{5,13},{6,38},{7,15},{128,160},{... | collective-permute-start | bytes 4718600 | tf_op jit(solution)/shard_map/rows_line/ppermute | solution.py:350
  26.5 2.5 %collective-permute-start.4 = (bf16[256,3072]{1,0:T(8,128)(2,1)S(1)}, bf16[256,3072]{1,0:T(8,128)(2,1)S(1)}, u32[]{:S(2)}, u32[]{:S(2)}) collective-permute-start(bf16[256,3072]{1,0:T(8,128)(2,1)S(1)} %norm_rows.1.r0), channel_id=1, source_target_pairs={{0,96},{1,25},{2,98},{3,27},{4,100},{5,29},{6,102},{7,31},{128,224... | collective-permute-start | bytes 4718600 | tf_op jit(solution)/shard_map/rows_line/ppermute | solution.py:350
  29.0 0.0 collective-permute-done.6.q1
  29.0 1.4 %collective-permute-start.5 = (bf16[256,3072]{1,0:T(8,128)(2,1)S(1)}, bf16[256,3072]{1,0:T(8,128)(2,1)S(1)}, u32[]{:S(2)}, u32[]{:S(2)}) collective-permute-start(bf16[256,3072]{1,0:T(8,128)(2,1)S(1)} %norm_rows.1.r0), channel_id=1, source_target_pairs={{0,64},{1,17},{2,66},{3,19},{4,68},{5,21},{6,70},{7,23},{128,192},... | collective-permute-start | bytes 4718600 | tf_op jit(solution)/shard_map/rows_line/ppermute | solution.py:350
  30.4 0.0 collective-permute-done.7.q2
  30.4 7.4 %collective-permute-done.8.q3 = bf16[288,768]{1,0:T(8,128)(2,1)S(1)} collective-permute-done((bf16[288,768]{1,0:T(8,128)(2,1)}, bf16[288,768]{1,0:T(8,128)(2,1)S(1)}, u32[]{:S(2)}, u32[]{:S(2)}) %collective-permute-start.8) | collective-permute-done | bytes 442400 | tf_op jit(solution)/shard_map/scatter/ppermute | solution.py:345
  37.7 0.8 choose_quarter.1.refs_2_
  38.6 0.1 collective-permute-start.9
  38.7 3.2 %collective-permute-start.12 = (bf16[288,768]{1,0:T(8,128)(2,1)S(1)}, bf16[288,768]{1,0:T(8,128)(2,1)S(1)}, u32[]{:S(2)}, u32[]{:S(2)}) collective-permute-start(bf16[288,768]{1,0:T(8,128)(2,1)S(1)} %choose_quarter.1.refs_2_), channel_id=1, source_target_pairs={{0,134},{1,135},{2,0},{3,1},{4,2},{5,3},{6,4},{7,5},{128,6},{129,7... | collective-permute-start | bytes 1327112 | tf_op jit(solution)/shard_map/ring/ppermute | solution.py:358
  41.9 8.8 %collective-permute-done.9.refs_4_ = bf16[288,768]{1,0:T(8,128)(2,1)S(1)} collective-permute-done((bf16[288,768]{1,0:T(8,128)(2,1)S(1)}, bf16[288,768]{1,0:T(8,128)(2,1)S(1)}, u32[]{:S(2)}, u32[]{:S(2)}) %collective-permute-start.9) | collective-permute-done | bytes 442400 | tf_op jit(solution)/shard_map/ring/ppermute | solution.py:358
  50.7 0.0 collective-permute-start.15
  50.7 0.0 collective-permute-done.12.refs_6_
  50.7 0.0 collective-permute-start.10
  50.7 1.8 %collective-permute-done.15.refs_3_ = bf16[288,768]{1,0:T(8,128)(2,1)S(1)} collective-permute-done((bf16[288,768]{1,0:T(8,128)(2,1)S(1)}, bf16[288,768]{1,0:T(8,128)(2,1)S(1)}, u32[]{:S(2)}, u32[]{:S(2)}) %collective-permute-start.15) | collective-permute-done | bytes 442400 | tf_op jit(solution)/shard_map/swap/ppermute | solution.py:354
  52.5 1.5 %collective-permute-start.13 = (bf16[288,768]{1,0:T(8,128)(2,1)S(1)}, bf16[288,768]{1,0:T(8,128)(2,1)S(1)}, u32[]{:S(2)}, u32[]{:S(2)}) collective-permute-start(bf16[288,768]{1,0:T(8,128)(2,1)S(1)} %collective-permute-done.12.refs_6_), channel_id=1, source_target_pairs={{0,134},{1,135},{2,0},{3,1},{4,2},{5,3},{6,4},{7,5},{128,6},{129,7... | collective-permute-start | bytes 1327112 | tf_op jit(solution)/shard_map/ring/ppermute | solution.py:358
  54.0 10.5 %collective-permute-done.10.refs_8_ = bf16[288,768]{1,0:T(8,128)(2,1)S(1)} collective-permute-done((bf16[288,768]{1,0:T(8,128)(2,1)S(1)}, bf16[288,768]{1,0:T(8,128)(2,1)S(1)}, u32[]{:S(2)}, u32[]{:S(2)}) %collective-permute-start.10) | collective-permute-done | bytes 442400 | tf_op jit(solution)/shard_map/ring/ppermute | solution.py:358
  64.5 0.0 collective-permute-start.16
  64.5 0.2 collective-permute-done.13.refs_10_
  64.7 0.3 collective-permute-start.17
  65.0 1.3 %collective-permute-done.16.refs_5_ = bf16[288,768]{1,0:T(8,128)(2,1)S(1)} collective-permute-done((bf16[288,768]{1,0:T(8,128)(2,1)S(1)}, bf16[288,768]{1,0:T(8,128)(2,1)S(1)}, u32[]{:S(2)}, u32[]{:S(2)}) %collective-permute-start.16) | collective-permute-done | bytes 442400 | tf_op jit(solution)/shard_map/swap/ppermute | solution.py:354
  66.3 0.1 collective-permute-start.18
  66.4 0.0 collective-permute-done.3.r1
  66.4 0.4 collective-permute-start.19
  66.8 0.0 collective-permute-done.4.r2
  66.8 0.0 collective-permute-start.11
  66.8 0.0 collective-permute-done.5.r3
  66.8 4.1 %collective-permute-start.14 = (bf16[288,768]{1,0:T(8,128)(2,1)S(1)}, bf16[288,768]{1,0:T(8,128)(2,1)S(1)}, u32[]{:S(2)}, u32[]{:S(2)}) collective-permute-start(bf16[288,768]{1,0:T(8,128)(2,1)S(1)} %collective-permute-done.13.refs_10_), channel_id=1, source_target_pairs={{0,134},{1,135},{2,0},{3,1},{4,2},{5,3},{6,4},{7,5},{128,6},{129,7... | collective-permute-start | bytes 1327112 | tf_op jit(solution)/shard_map/ring/ppermute | solution.py:358
  70.9 0.4 stack_rows.1.refs_1_.rows
  71.3 0.0 collective-permute-done.17.refs_7_
  71.3 0.0 collective-permute-done.18.refs_9_
  71.3 0.0 collective-permute-done.19.refs_11_
  71.4 7.8 %project.2.refs_6_ = f32[2,32,4,8,768]{4,3,2,1,0:T(8,128)S(1)} custom-call(s32[5]{0:T(128)S(1)} %copy-done.2, bf16[1024,3072]{1,0:T(8,128)(2,1)S(1)} %stack_rows.1.refs_1_.rows, bf16[288,768]{1,0:T(8,128)(2,1)S(1)} %choose_quarter.1.refs_2_, bf16[288,768]{1,0:T(8,128)(2,1)S(1)} %collective-permute-done.15.refs_3_, ...), custom_call_target="tpu_custom_call" | custom-call | tf_op jit(solution)/shard_map/project/pallas_call | solution.py:236
  79.2 1.2 collective-permute-done.11.up.refs_2_
  80.4 0.0 collective-permute-done.14.down.refs_4_
  80.4 0.0 collective-permute-start.22
  80.4 0.5 collective-permute-start.23
  80.9 1.7 %collective-permute-start.20 = (bf16[288,384]{1,0:T(8,128)(2,1)S(1)}, bf16[288,384]{1,0:T(8,128)(2,1)S(1)}, u32[]{:S(2)}, u32[]{:S(2)}) collective-permute-start(bf16[288,384]{1,0:T(8,128)(2,1)S(1)} %get-tuple-element.31), channel_id=1, source_target_pairs={{0,2},{1,3},{2,4},{3,5},{4,6},{5,7},{6,128},{7,129},{128,130},{129... | collective-permute-start | bytes 663560 | tf_op jit(solution)/shard_map/ring/ppermute | solution.py:358
  82.6 1.6 %collective-permute-start.21 = (bf16[288,384]{1,0:T(8,128)(2,1)S(1)}, bf16[288,384]{1,0:T(8,128)(2,1)S(1)}, u32[]{:S(2)}, u32[]{:S(2)}) collective-permute-start(bf16[288,384]{1,0:T(8,128)(2,1)S(1)} %get-tuple-element.32), channel_id=1, source_target_pairs={{0,134},{1,135},{2,0},{3,1},{4,2},{5,3},{6,4},{7,5},{128,6},{129,7... | collective-permute-start | bytes 663560 | tf_op jit(solution)/shard_map/ring/ppermute | solution.py:358
  84.2 0.0 collective-permute-done.22.refs_3_
  84.3 0.0 collective-permute-done.23.refs_5_
  84.3 3.6 %project.3.before = f32[2,32,4,8,768]{4,3,2,1,0:T(8,128)S(1)} custom-call(s32[5]{0:T(128)S(1)} %copy-done.2, bf16[1024,3072]{1,0:T(8,128)(2,1)S(1)} %stack_rows.1.refs_1_.rows, bf16[288,768]{1,0:T(8,128)(2,1)S(1)} %collective-permute-done.11.up.refs_2_, bf16[288,768]{1,0:T(8,128)(2,1)S(1)} %collective-permute-done.22.refs_3_, ...), custom_call_target="tpu_custom_call", output_to_operand_aliasing={{}: (6, {})} | custom-call | tf_op jit(solution)/shard_map/project/pallas_call | solution.py:236
  87.8 1.7 %collective-permute-done.20.fh = bf16[288,384]{1,0:T(8,128)(2,1)S(1)} collective-permute-done((bf16[288,384]{1,0:T(8,128)(2,1)S(1)}, bf16[288,384]{1,0:T(8,128)(2,1)S(1)}, u32[]{:S(2)}, u32[]{:S(2)}) %collective-permute-start.20) | collective-permute-done | bytes 221216 | tf_op jit(solution)/shard_map/ring/ppermute | solution.py:358
  89.6 0.1 collective-permute-done.21.bh
  89.7 0.0 collective-permute-start.24
  89.7 0.5 collective-permute-start.25
  90.2 1.0 collective-permute-done.24.fho
  91.1 0.3 collective-permute-done.25.bho
  91.5 5.7 %project_attend.1 = bf16[16,64,384]{2,1,0:T(8,128)(2,1)S(1)} custom-call(s32[5]{0:T(128)S(1)} %copy-done.2, bf16[1024,3072]{1,0:T(8,128)(2,1)S(1)} %stack_rows.1.refs_1_.rows, bf16[288,384]{1,0:T(8,128)(2,1)S(1)} %collective-permute-done.20.fh, bf16[288,384]{1,0:T(8,128)(2,1)S(1)} %collective-permute-done.24.fho, ...), custom_call_target="tpu_custom_call" | custom-call | tf_op jit(solution)/shard_map/project_attend/pallas_call | solution.py:294
  97.2 21.5 %all_to_all.5.recv_ref = bf16[16,64,384]{2,1,0:T(8,128)(2,1)S(1)} all-to-all(bf16[16,64,384]{2,1,0:T(8,128)(2,1)S(1)} %project_attend.1), channel_id=1, replica_groups=mesh['dp'=2,'seq'=16,'fsdp'=8] {'seq'}, dimensions={0} | all-to-all | bytes 1572864 | tf_op jit(solution)/shard_map/heads_back/all_to_all | solution.py:371
  118.7 1.5 %assemble_heads.1 = bf16[1,2,128,1536]{3,2,1,0:T(8,128)(2,1)} custom-call(s32[5]{0:T(128)S(1)} %copy-done.2, bf16[16,64,384]{2,1,0:T(8,128)(2,1)S(1)} %all_to_all.5.recv_ref), custom_call_target="tpu_custom_call" | custom-call | tf_op jit(solution)/shard_map/assemble_heads/pallas_call | solution.py:324
  (11 shorter events, 0.1 us)
Async XLA Ops:
  0.7 20.2 %copy-start.3 = (f32[3072]{0:T(1024)S(1)}, f32[3072]{0:T(1024)}, u32[]{:S(2)}) copy-start(f32[3072]{0:T(1024)} %param.8) | copy-start | bytes 36868
  4.8 8.2 %collective-permute-start = (bf16[2,32,3072]{2,1,0:T(8,128)(2,1)}, bf16[2,32,3072]{2,1,0:T(8,128)(2,1)S(1)}, u32[]{:S(2)}, u32[]{:S(2)}) collective-permute-start(bf16[2,32,3072]{2,1,0:T(8,128)(2,1)} %get-tuple-element.22), channel_id=1, source_target_pairs={{0,8},{1,33},{2,10},{3,35},{4,12},{5,37},{6,14},{7,39},{128,136},{... | collective-permute-start | bytes 1179656 | tf_op jit(solution)/shard_map/rows_cross/ppermute | solution.py:343
  6.4 22.6 %collective-permute-start.6 = (bf16[288,768]{1,0:T(8,128)(2,1)}, bf16[288,768]{1,0:T(8,128)(2,1)S(1)}, u32[]{:S(2)}, u32[]{:S(2)}) collective-permute-start(bf16[288,768]{1,0:T(8,128)(2,1)} %get-tuple-element.26), channel_id=1, source_target_pairs={{0,4},{1,5},{2,6},{3,7},{12,136},{13,137},{14,138},{15,139},{144,1... | collective-permute-start | bytes 1327112 | tf_op jit(solution)/shard_map/scatter/ppermute | solution.py:345
  7.1 9.7 %collective-permute-start.1 = (bf16[2,32,3072]{2,1,0:T(8,128)(2,1)}, bf16[2,32,3072]{2,1,0:T(8,128)(2,1)S(1)}, u32[]{:S(2)}, u32[]{:S(2)}) collective-permute-start(bf16[2,32,3072]{2,1,0:T(8,128)(2,1)} %get-tuple-element.23), channel_id=1, source_target_pairs={{0,16},{1,65},{2,18},{3,67},{4,20},{5,69},{6,22},{7,71},{128,144},... | collective-permute-start | bytes 1179656 | tf_op jit(solution)/shard_map/rows_cross/ppermute | solution.py:343
  10.5 10.4 %collective-permute-start.2 = (bf16[2,32,3072]{2,1,0:T(8,128)(2,1)}, bf16[2,32,3072]{2,1,0:T(8,128)(2,1)S(1)}, u32[]{:S(2)}, u32[]{:S(2)}) collective-permute-start(bf16[2,32,3072]{2,1,0:T(8,128)(2,1)} %get-tuple-element.24), channel_id=1, source_target_pairs={{0,24},{1,97},{2,26},{3,99},{4,28},{5,101},{6,30},{7,103},{128,152... | collective-permute-start | bytes 1179656 | tf_op jit(solution)/shard_map/rows_cross/ppermute | solution.py:343
  12.3 18.1 %collective-permute-start.7 = (bf16[288,768]{1,0:T(8,128)(2,1)}, bf16[288,768]{1,0:T(8,128)(2,1)S(1)}, u32[]{:S(2)}, u32[]{:S(2)}) collective-permute-start(bf16[288,768]{1,0:T(8,128)(2,1)} %get-tuple-element.27), channel_id=1, source_target_pairs={{64,128},{65,129},{66,130},{67,131},{76,140},{77,141},{78,142},{79... | collective-permute-start | bytes 1327112 | tf_op jit(solution)/shard_map/scatter/ppermute | solution.py:345
  13.0 24.7 %collective-permute-start.8 = (bf16[288,768]{1,0:T(8,128)(2,1)}, bf16[288,768]{1,0:T(8,128)(2,1)S(1)}, u32[]{:S(2)}, u32[]{:S(2)}) collective-permute-start(bf16[288,768]{1,0:T(8,128)(2,1)} %get-tuple-element.28), channel_id=1, source_target_pairs={{0,132},{1,133},{2,134},{3,135},{12,8},{13,9},{14,10},{15,11},{144... | collective-permute-start | bytes 1327112 | tf_op jit(solution)/shard_map/scatter/ppermute | solution.py:345
  20.9 1.0 copy-start.1
  21.9 15.8 %copy-start = (bf16[288,768]{1,0:T(8,128)(2,1)S(1)}, bf16[288,768]{1,0:T(8,128)(2,1)}, u32[]{:S(2)}) copy-start(bf16[288,768]{1,0:T(8,128)(2,1)} %get-tuple-element.25.q0) | copy-start | bytes 1327108
  21.9 15.8 %copy-start.2 = (s32[5]{0:T(128)S(1)}, s32[5]{0:T(128)}, u32[]{:S(2)}) copy-start(s32[5]{0:T(128)} %stack.23.where.refs_0_) | copy-start | bytes 64
  23.0 43.5 %collective-permute-start.3 = (bf16[256,3072]{1,0:T(8,128)(2,1)S(1)}, bf16[256,3072]{1,0:T(8,128)(2,1)S(1)}, u32[]{:S(2)}, u32[]{:S(2)}) collective-permute-start(bf16[256,3072]{1,0:T(8,128)(2,1)S(1)} %norm_rows.1.r0), channel_id=1, source_target_pairs={{0,32},{1,9},{2,34},{3,11},{4,36},{5,13},{6,38},{7,15},{128,160},{... | collective-permute-start | bytes 4718600 | tf_op jit(solution)/shard_map/rows_line/ppermute | solution.py:350
  26.5 40.4 %collective-permute-start.4 = (bf16[256,3072]{1,0:T(8,128)(2,1)S(1)}, bf16[256,3072]{1,0:T(8,128)(2,1)S(1)}, u32[]{:S(2)}, u32[]{:S(2)}) collective-permute-start(bf16[256,3072]{1,0:T(8,128)(2,1)S(1)} %norm_rows.1.r0), channel_id=1, source_target_pairs={{0,96},{1,25},{2,98},{3,27},{4,100},{5,29},{6,102},{7,31},{128,224... | collective-permute-start | bytes 4718600 | tf_op jit(solution)/shard_map/rows_line/ppermute | solution.py:350
  29.0 37.8 %collective-permute-start.5 = (bf16[256,3072]{1,0:T(8,128)(2,1)S(1)}, bf16[256,3072]{1,0:T(8,128)(2,1)S(1)}, u32[]{:S(2)}, u32[]{:S(2)}) collective-permute-start(bf16[256,3072]{1,0:T(8,128)(2,1)S(1)} %norm_rows.1.r0), channel_id=1, source_target_pairs={{0,64},{1,17},{2,66},{3,19},{4,68},{5,21},{6,70},{7,23},{128,192},... | collective-permute-start | bytes 4718600 | tf_op jit(solution)/shard_map/rows_line/ppermute | solution.py:350
  38.6 12.2 %collective-permute-start.9 = (bf16[288,768]{1,0:T(8,128)(2,1)S(1)}, bf16[288,768]{1,0:T(8,128)(2,1)S(1)}, u32[]{:S(2)}, u32[]{:S(2)}) collective-permute-start(bf16[288,768]{1,0:T(8,128)(2,1)S(1)} %choose_quarter.1.refs_2_), channel_id=1, source_target_pairs={{0,2},{1,3},{2,4},{3,5},{4,6},{5,7},{6,128},{7,129},{128,130},{129... | collective-permute-start | bytes 1327112 | tf_op jit(solution)/shard_map/ring/ppermute | solution.py:358
  38.7 12.1 %collective-permute-start.12 = (bf16[288,768]{1,0:T(8,128)(2,1)S(1)}, bf16[288,768]{1,0:T(8,128)(2,1)S(1)}, u32[]{:S(2)}, u32[]{:S(2)}) collective-permute-start(bf16[288,768]{1,0:T(8,128)(2,1)S(1)} %choose_quarter.1.refs_2_), channel_id=1, source_target_pairs={{0,134},{1,135},{2,0},{3,1},{4,2},{5,3},{6,4},{7,5},{128,6},{129,7... | collective-permute-start | bytes 1327112 | tf_op jit(solution)/shard_map/ring/ppermute | solution.py:358
  50.7 1.8 %collective-permute-start.15 = (bf16[288,768]{1,0:T(8,128)(2,1)S(1)}, bf16[288,768]{1,0:T(8,128)(2,1)S(1)}, u32[]{:S(2)}, u32[]{:S(2)}) collective-permute-start(bf16[288,768]{1,0:T(8,128)(2,1)S(1)} %choose_quarter.1.refs_2_), channel_id=1, source_target_pairs={{0,1},{1,0},{2,3},{3,2},{4,5},{5,4},{6,7},{7,6},{128,129},{129,128... | collective-permute-start | bytes 1327112 | tf_op jit(solution)/shard_map/swap/ppermute | solution.py:354
  50.7 13.8 %collective-permute-start.10 = (bf16[288,768]{1,0:T(8,128)(2,1)S(1)}, bf16[288,768]{1,0:T(8,128)(2,1)S(1)}, u32[]{:S(2)}, u32[]{:S(2)}) collective-permute-start(bf16[288,768]{1,0:T(8,128)(2,1)S(1)} %collective-permute-done.9.refs_4_), channel_id=1, source_target_pairs={{0,2},{1,3},{2,4},{3,5},{4,6},{5,7},{6,128},{7,129},{128,130},{129... | collective-permute-start | bytes 1327112 | tf_op jit(solution)/shard_map/ring/ppermute | solution.py:358
  52.5 12.2 %collective-permute-start.13 = (bf16[288,768]{1,0:T(8,128)(2,1)S(1)}, bf16[288,768]{1,0:T(8,128)(2,1)S(1)}, u32[]{:S(2)}, u32[]{:S(2)}) collective-permute-start(bf16[288,768]{1,0:T(8,128)(2,1)S(1)} %collective-permute-done.12.refs_6_), channel_id=1, source_target_pairs={{0,134},{1,135},{2,0},{3,1},{4,2},{5,3},{6,4},{7,5},{128,6},{129,7... | collective-permute-start | bytes 1327112 | tf_op jit(solution)/shard_map/ring/ppermute | solution.py:358
  64.5 1.8 %collective-permute-start.16 = (bf16[288,768]{1,0:T(8,128)(2,1)S(1)}, bf16[288,768]{1,0:T(8,128)(2,1)S(1)}, u32[]{:S(2)}, u32[]{:S(2)}) collective-permute-start(bf16[288,768]{1,0:T(8,128)(2,1)S(1)} %collective-permute-done.9.refs_4_), channel_id=1, source_target_pairs={{0,1},{1,0},{2,3},{3,2},{4,5},{5,4},{6,7},{7,6},{128,129},{129,128... | collective-permute-start | bytes 1327112 | tf_op jit(solution)/shard_map/swap/ppermute | solution.py:354
  64.7 6.6 %collective-permute-start.17 = (bf16[288,768]{1,0:T(8,128)(2,1)S(1)}, bf16[288,768]{1,0:T(8,128)(2,1)S(1)}, u32[]{:S(2)}, u32[]{:S(2)}) collective-permute-start(bf16[288,768]{1,0:T(8,128)(2,1)S(1)} %collective-permute-done.12.refs_6_), channel_id=1, source_target_pairs={{0,1},{1,0},{2,3},{3,2},{4,5},{5,4},{6,7},{7,6},{128,129},{129,128... | collective-permute-start | bytes 1327112 | tf_op jit(solution)/shard_map/swap/ppermute | solution.py:354
  66.3 5.0 %collective-permute-start.18 = (bf16[288,768]{1,0:T(8,128)(2,1)S(1)}, bf16[288,768]{1,0:T(8,128)(2,1)S(1)}, u32[]{:S(2)}, u32[]{:S(2)}) collective-permute-start(bf16[288,768]{1,0:T(8,128)(2,1)S(1)} %collective-permute-done.10.refs_8_), channel_id=1, source_target_pairs={{0,1},{1,0},{2,3},{3,2},{4,5},{5,4},{6,7},{7,6},{128,129},{129,128... | collective-permute-start | bytes 1327112 | tf_op jit(solution)/shard_map/swap/ppermute | solution.py:354
  66.4 4.9 %collective-permute-start.19 = (bf16[288,768]{1,0:T(8,128)(2,1)S(1)}, bf16[288,768]{1,0:T(8,128)(2,1)S(1)}, u32[]{:S(2)}, u32[]{:S(2)}) collective-permute-start(bf16[288,768]{1,0:T(8,128)(2,1)S(1)} %collective-permute-done.13.refs_10_), channel_id=1, source_target_pairs={{0,1},{1,0},{2,3},{3,2},{4,5},{5,4},{6,7},{7,6},{128,129},{129,128... | collective-permute-start | bytes 1327112 | tf_op jit(solution)/shard_map/swap/ppermute | solution.py:354
  66.8 13.5 %collective-permute-start.11 = (bf16[288,768]{1,0:T(8,128)(2,1)S(1)}, bf16[288,768]{1,0:T(8,128)(2,1)S(1)}, u32[]{:S(2)}, u32[]{:S(2)}) collective-permute-start(bf16[288,768]{1,0:T(8,128)(2,1)S(1)} %collective-permute-done.10.refs_8_), channel_id=1, source_target_pairs={{0,2},{1,3},{2,4},{3,5},{4,6},{5,7},{6,128},{7,129},{128,130},{129... | collective-permute-start | bytes 1327112 | tf_op jit(solution)/shard_map/ring/ppermute | solution.py:358
  66.8 13.5 %collective-permute-start.14 = (bf16[288,768]{1,0:T(8,128)(2,1)S(1)}, bf16[288,768]{1,0:T(8,128)(2,1)S(1)}, u32[]{:S(2)}, u32[]{:S(2)}) collective-permute-start(bf16[288,768]{1,0:T(8,128)(2,1)S(1)} %collective-permute-done.13.refs_10_), channel_id=1, source_target_pairs={{0,134},{1,135},{2,0},{3,1},{4,2},{5,3},{6,4},{7,5},{128,6},{129,7... | collective-permute-start | bytes 1327112 | tf_op jit(solution)/shard_map/ring/ppermute | solution.py:358
  80.4 3.9 %collective-permute-start.22 = (bf16[288,768]{1,0:T(8,128)(2,1)S(1)}, bf16[288,768]{1,0:T(8,128)(2,1)S(1)}, u32[]{:S(2)}, u32[]{:S(2)}) collective-permute-start(bf16[288,768]{1,0:T(8,128)(2,1)S(1)} %collective-permute-done.11.up.refs_2_), channel_id=1, source_target_pairs={{0,1},{1,0},{2,3},{3,2},{4,5},{5,4},{6,7},{7,6},{128,129},{129,128... | collective-permute-start | bytes 1327112 | tf_op jit(solution)/shard_map/swap/ppermute | solution.py:354
  80.4 3.9 %collective-permute-start.23 = (bf16[288,768]{1,0:T(8,128)(2,1)S(1)}, bf16[288,768]{1,0:T(8,128)(2,1)S(1)}, u32[]{:S(2)}, u32[]{:S(2)}) collective-permute-start(bf16[288,768]{1,0:T(8,128)(2,1)S(1)} %collective-permute-done.14.down.refs_4_), channel_id=1, source_target_pairs={{0,1},{1,0},{2,3},{3,2},{4,5},{5,4},{6,7},{7,6},{128,129},{129,128... | collective-permute-start | bytes 1327112 | tf_op jit(solution)/shard_map/swap/ppermute | solution.py:354
  80.9 8.6 %collective-permute-start.20 = (bf16[288,384]{1,0:T(8,128)(2,1)S(1)}, bf16[288,384]{1,0:T(8,128)(2,1)S(1)}, u32[]{:S(2)}, u32[]{:S(2)}) collective-permute-start(bf16[288,384]{1,0:T(8,128)(2,1)S(1)} %get-tuple-element.31), channel_id=1, source_target_pairs={{0,2},{1,3},{2,4},{3,5},{4,6},{5,7},{6,128},{7,129},{128,130},{129... | collective-permute-start | bytes 663560 | tf_op jit(solution)/shard_map/ring/ppermute | solution.py:358
  82.6 8.9 %copy-start.4 = (f32[128]{0:T(128)S(1)}, f32[128]{0:T(128)}, u32[]{:S(2)}) copy-start(f32[128]{0:T(128)} %param.12) | copy-start | bytes 1540
  82.6 8.9 %copy-start.5 = (f32[128]{0:T(128)S(1)}, f32[128]{0:T(128)}, u32[]{:S(2)}) copy-start(f32[128]{0:T(128)} %param.13) | copy-start | bytes 1540
  82.6 7.1 %collective-permute-start.21 = (bf16[288,384]{1,0:T(8,128)(2,1)S(1)}, bf16[288,384]{1,0:T(8,128)(2,1)S(1)}, u32[]{:S(2)}, u32[]{:S(2)}) collective-permute-start(bf16[288,384]{1,0:T(8,128)(2,1)S(1)} %get-tuple-element.32), channel_id=1, source_target_pairs={{0,134},{1,135},{2,0},{3,1},{4,2},{5,3},{6,4},{7,5},{128,6},{129,7... | collective-permute-start | bytes 663560 | tf_op jit(solution)/shard_map/ring/ppermute | solution.py:358
  89.7 1.5 %collective-permute-start.24 = (bf16[288,384]{1,0:T(8,128)(2,1)S(1)}, bf16[288,384]{1,0:T(8,128)(2,1)S(1)}, u32[]{:S(2)}, u32[]{:S(2)}) collective-permute-start(bf16[288,384]{1,0:T(8,128)(2,1)S(1)} %collective-permute-done.20.fh), channel_id=1, source_target_pairs={{0,1},{1,0},{2,3},{3,2},{4,5},{5,4},{6,7},{7,6},{128,129},{129,128... | collective-permute-start | bytes 663560 | tf_op jit(solution)/shard_map/swap/ppermute | solution.py:354
  89.7 1.8 %collective-permute-start.25 = (bf16[288,384]{1,0:T(8,128)(2,1)S(1)}, bf16[288,384]{1,0:T(8,128)(2,1)S(1)}, u32[]{:S(2)}, u32[]{:S(2)}) collective-permute-start(bf16[288,384]{1,0:T(8,128)(2,1)S(1)} %collective-permute-done.21.bh), channel_id=1, source_target_pairs={{0,1},{1,0},{2,3},{3,2},{4,5},{5,4},{6,7},{7,6},{128,129},{129,128... | collective-permute-start | bytes 663560 | tf_op jit(solution)/shard_map/swap/ppermute | solution.py:354

commit v6 on v5

--- a/solution.py
+++ b/solution.py
@@ -7,6 +7,7 @@
 
 AXES = ("dp", "seq", "fsdp")
 SHIFTS = (0, 1, 3, 2)
+CHOOSE_COST = 9_000_000_000
 
 
 def place(x, y, z, core):
@@ -48,6 +49,14 @@
 
 def ring_perm(step):
     return [(place(x, y, z, c), place(x, y, (z + step) % 8, c)) for x, y, z, c in every_place()]
+
+
+def partner_perm(side):
+    pairs = []
+    for x, y, z, c in every_place():
+        step = side * (1 - 2 * (x % 2))
+        pairs.append((place(x, y, z, c), place((x + step) % 4, (y - step) % 4, z, c)))
+    return pairs
 
 
 def swap_perm():
@@ -71,7 +80,8 @@
         copy.wait()
     for r, out in ((2, q2), (1, q1), (3, q3), (0, q0)):
         for m in range(3):
-            packed[r, height * m : height * (m + 1), :] = columns[m, :, quarter * r : quarter * (r + 1)]
+            at = pl.multiple_of((r + 2 * where[6]) % 4 * quarter, 128)
+            packed[r, height * m : height * (m + 1), :] = columns[m, :, pl.ds(at, quarter)]
         stores.append(pltpu.make_async_copy(packed.at[r], out, out_sems.at[r]))
         stores[-1].start()
     for s, out in enumerate((f0, f1, f2, f3)):
@@ -131,7 +141,7 @@
 
 
 def choose_kernel(where, q0, q1, q2, q3, out_ref, sem):
-    quarter = (where[0] // 2 - where[1] + 4) % 4
+    quarter = (where[5] // 2 - where[1] + 4) % 4
     for r, ref in enumerate((q0, q1, q2, q3)):
 
         @pl.when(quarter == r)
@@ -149,28 +159,10 @@
         out_specs=anywhere,
         out_shape=jax.ShapeDtypeStruct(parts[0].shape, parts[0].dtype),
         scratch_shapes=[pltpu.SemaphoreType.DMA],
+        cost_estimate=pl.CostEstimate(flops=CHOOSE_COST, bytes_accessed=2**20, transcendentals=0),
         compiler_params=pltpu.CompilerParams(vmem_limit_bytes=4 * 2**20),
         name="choose_quarter",
     )(where, *parts)
-
-
-def halve_kernel(up, down, up_half, down_half):
-    width = up_half.shape[1]
-    up_half[...] = up[:, :width]
-    down_half[...] = down[:, width:]
-
-
-def halve(up, down):
-    vmem = pl.BlockSpec(memory_space=pltpu.VMEM)
-    half = jax.ShapeDtypeStruct((up.shape[0], up.shape[1] // 2), up.dtype)
-    return pl.pallas_call(
-        halve_kernel,
-        in_specs=[vmem] * 2,
-        out_specs=[vmem] * 2,
-        out_shape=[half, half],
-        compiler_params=pltpu.CompilerParams(vmem_limit_bytes=8 * 2**20),
-        name="halve",
-    )(up, down)
 
 
 NT = (((1,), (1,)), ((), ()))
@@ -198,16 +190,12 @@
     z = (where[0] + offset + 8) % 8
     r = (z // 2 - where[1] + 4) % 4
     quarter = weights.shape[-1]
-    for core, parts in ((where[2], own), (1 - where[2], other)):
-        at = 0
-        for ref in parts:
-            width = ref.shape[1]
-            for m in range(3):
-                for g in range(3):
-                    to = pl.multiple_of((z % 2 * 128 + core * 96 + 32 * g) % 192, 32)
-                    low = 96 * m + 32 * g
-                    weights[turn, m, pl.ds(to, 32), at : at + width] = ref[low : low + 32, :]
-            at += width
+    for core, ref in ((where[2], own), (1 - where[2], other)):
+        for m in range(3):
+            for g in range(3):
+                to = pl.multiple_of((z % 2 * 128 + core * 96 + 32 * g) % 192, 32)
+                low = 96 * m + 32 * g
+                weights[turn, m, pl.ds(to, 32), :] = ref[low : low + 32, :]
     for m in range(3):
         weights[turn, m, 192:, :] = jnp.zeros((64, quarter), jnp.bfloat16)
     product = lax.dot_general(
@@ -226,7 +214,7 @@
 def project_kernel(offsets, where, rows, *refs):
     pieces, total, weights = refs[: 2 * len(offsets)], refs[-2], refs[-1]
     for turn, offset in enumerate(offsets):
-        own, other = [[pieces[2 * turn + side]] for side in range(2)]
+        own, other = pieces[2 * turn], pieces[2 * turn + 1]
         add_products(where, rows, weights, turn, offset, own, other, total, offset in (0, -1))
 
 
@@ -253,9 +241,11 @@
     return total[h // 2, :, g, :, at : at + 128].reshape(256, 128)
 
 
-def attend_kernel(where, rows, fh, fho, bh, bho, qg_ref, kg_ref, before, out_ref, weights, total, found):
+def attend_kernel(where, rows, *refs):
+    pieces, (qg_ref, kg_ref, before, out_ref, weights, total, found) = refs[:6], refs[6:]
     total[...] = before[...]
-    add_products(where, rows, weights, 0, 4, [fh, bh], [fho, bho], total, False)
+    for turn, offset in enumerate((-3, 3, 4)):
+        add_products(where, rows, weights, turn, offset, pieces[2 * turn], pieces[2 * turn + 1], total, False)
 
     @pl.when(where[0] >= 0)
     def _():
@@ -296,7 +286,7 @@
         in_specs=[pl.BlockSpec(memory_space=pltpu.SMEM)] + [vmem] * (4 + len(pieces)),
         out_specs=vmem,
         scratch_shapes=[
-            pltpu.VMEM((1, 3, 256, quarter), jnp.bfloat16),
+            pltpu.VMEM((3, 3, 256, quarter), jnp.bfloat16),
             pltpu.VMEM((2, 32, 4, 8, 768), jnp.float32),
             pltpu.VMEM((32, 4, 8, 384), jnp.float32),
         ],
@@ -336,7 +326,8 @@
     fsdp = lax.axis_index("fsdp")
     z = lax.axis_index("dp") * 4 + fsdp // 2
     group = (seq // 4 + seq % 4) % 4
-    where = jnp.stack([z, group, fsdp % 2, seq // 4, seq % 4]).astype(jnp.int32)
+    turned = seq // 4 % 2
+    where = jnp.stack([(z + 4 * turned) % 8, group, fsdp % 2, seq // 4, seq % 4, z, turned]).astype(jnp.int32)
 
     *blocks, q0, q1, q2, q3 = prepare(where, video, [w.T for w in (w_query, w_key, w_value)])
     with jax.named_scope("rows_cross"):
@@ -357,16 +348,20 @@
         with jax.named_scope("ring"):
             return lax.ppermute(up, AXES, ring_perm(1)), lax.ppermute(down, AXES, ring_perm(-1))
 
+    def partners(piece, side):
+        with jax.named_scope("partner"):
+            return lax.ppermute(piece, AXES, partner_perm(side))
+
     up1, down1 = onward(part, part)
     up2, down2 = onward(up1, down1)
+    up2, down2, rows = lax.optimization_barrier((up2, down2, rows))
     up3, down3 = onward(up2, down2)
+    half_turn = partners(part, 1)
     early = swapped(part) + swapped(up1) + swapped(down1) + swapped(up2) + swapped(down2)
     total = project(where, rows, (0, -1, 1, -2, 2), early)
-    up3, down3, total = lax.optimization_barrier((up3, down3, total))
-    up4, down4 = onward(*halve(up3, down3))
-    total = project(where, rows, (-3, 3), swapped(up3) + swapped(down3), (total,))
-    up4, down4, total = lax.optimization_barrier((up4, down4, total))
-    output = attend(where, rows, swapped(up4) + swapped(down4), query_gain, key_gain, total)
+    up3, down3, half_turn, total = lax.optimization_barrier((up3, down3, half_turn, total))
+    late = swapped(up3) + swapped(down3) + swapped(half_turn)
+    output = attend(where, rows, late, query_gain, key_gain, total)
     with jax.named_scope("heads_back"):
         received = lax.all_to_all(output, "seq", split_axis=0, concat_axis=0, tiled=True)
     return assemble(received, where)

time: 122 us -> 118 us (0.967)
    ppermute x3, waiting for transfers between devices: 0.01 us -> 11.6 us  [shards(): lax.ppermute(home, AXES, line_perm(s))]
    ppermute x4 -> x3, waiting for transfers between devices: 22.3 us -> 11.2 us  [onward(): lax.ppermute(up, AXES, ring_perm(1))]
    pallas_call x2 -> x1, Pallas kernels: 11.4 us -> 7.83 us  [project(): pl.pallas_call(lambda *refs: project_kernel(offsets, *refs), in_specs=[pl...]
    pallas_call x1, Pallas kernels: 5.72 us -> 8.65 us  [attend(): pl.pallas_call(attend_kernel, in_specs=[pl.BlockSpec(memory_space=pltpu.S...]
    ppermute x9 -> x8, waiting for transfers between devices: 4.35 us -> 2.56 us  [swapped(): return (piece, lax.ppermute(piece, AXES, swap_perm()))]
    ppermute x4 -> x3, starting transfers between devices: 10.4 us -> 9.65 us  [onward(): lax.ppermute(down, AXES, ring_perm(-1))]
  transfers between devices with their start and end apart: 26 -> 24, of which waited for: 14 -> 12; matrix products, arithmetic and copies ran while one was open for 0% -> 0% of each run, Pallas kernels for 11% -> 9%
where the time goes in v6:
time: 118 us; the launch traced here: 117 us
  waiting for transfers between devices  39.8 us (34%)
  starting transfers between devices  30.6 us (26%)
  Pallas kernels  24.4 us (21%)
  blocking collectives  20.4 us (17%)
  local copies, waits for them, and re-layouts  1.62 us (1%)
    all_to_all x1, blocking collectives, shards(): lax.all_to_all(output, 'seq', split_axis=0, concat_axis=0, tiled=True)  20.4 us
    ppermute x3, waiting for transfers between devices, shards(): lax.ppermute(home, AXES, line_perm(s))  11.6 us
    ppermute x3, waiting for transfers between devices, onward(): lax.ppermute(up, AXES, ring_perm(1))  11.2 us
    ppermute x3, starting transfers between devices, onward(): lax.ppermute(down, AXES, ring_perm(-1))  9.65 us
    pallas_call x1, Pallas kernels, attend(): pl.pallas_call(attend_kernel, in_specs=[pl.BlockSpec(memory_space=pltpu.S...  8.65 us
    pallas_call x1, Pallas kernels, project(): pl.pallas_call(lambda *refs: project_kernel(offsets, *refs), in_specs=[pl...  7.83 us
    ppermute x3, starting transfers between devices, shards(): lax.ppermute(home, AXES, line_perm(s))  7.4 us
    ppermute x3, waiting for transfers between devices, shards(): lax.ppermute(q, AXES, scatter_perm(r))  7.36 us
  transfers between devices with their start and end apart: 24, of which 12 were waited for; matrix products, arithmetic and copies ran while one was open for 0% of the time, Pallas kernels for 9%

profile of v6, /device:TPU:8, one launch (start us, length us, event | category | flops | bytes accessed | tf_op | source)
XLA Modules:
  0.0 116.9 jit_solution(838577198808864494)
XLA Ops:
  0.0 0.6 stack.31.where.refs_0_
  0.6 4.1 %prepare.1 = (bf16[2,32,3072]{2,1,0:T(8,128)(2,1)}, bf16[2,32,3072]{2,1,0:T(8,128)(2,1)}, bf16[2,32,3072]{2,1,0:T(8,128)(2,1)}, bf16[2,32,3072]{2,1,0:T(8,128)(2...) custom-call(s32[7]{0:T(128)} %stack.31.where.refs_0_, ...), custom_call_target="tpu_custom_call" | custom-call | tf_op jit(solution)/shard_map/prepare/pallas_call | solution.py:99
  4.7 1.7 %collective-permute-start.7 = (bf16[2,32,3072]{2,1,0:T(8,128)(2,1)}, bf16[2,32,3072]{2,1,0:T(8,128)(2,1)S(1)}, u32[]{:S(2)}, u32[]{:S(2)}) collective-permute-start(bf16[2,32,3072]{2,1,0:T(8,128)(2,1)} %get-tuple-element.25), channel_id=1, source_target_pairs={{0,8},{1,33},{2,10},{3,35},{4,12},{5,37},{6,14},{7,39},{128,136},{... | collective-permute-start | bytes 1179656 | tf_op jit(solution)/shard_map/rows_cross/ppermute | solution.py:334
  6.4 0.7 collective-permute-start
  7.1 3.4 %collective-permute-start.8 = (bf16[2,32,3072]{2,1,0:T(8,128)(2,1)}, bf16[2,32,3072]{2,1,0:T(8,128)(2,1)S(1)}, u32[]{:S(2)}, u32[]{:S(2)}) collective-permute-start(bf16[2,32,3072]{2,1,0:T(8,128)(2,1)} %get-tuple-element.26), channel_id=1, source_target_pairs={{0,16},{1,65},{2,18},{3,67},{4,20},{5,69},{6,22},{7,71},{128,144},... | collective-permute-start | bytes 1179656 | tf_op jit(solution)/shard_map/rows_cross/ppermute | solution.py:334
  10.4 1.8 %collective-permute-start.9 = (bf16[2,32,3072]{2,1,0:T(8,128)(2,1)}, bf16[2,32,3072]{2,1,0:T(8,128)(2,1)S(1)}, u32[]{:S(2)}, u32[]{:S(2)}) collective-permute-start(bf16[2,32,3072]{2,1,0:T(8,128)(2,1)} %get-tuple-element.27), channel_id=1, source_target_pairs={{0,24},{1,97},{2,26},{3,99},{4,28},{5,101},{6,30},{7,103},{128,152... | collective-permute-start | bytes 1179656 | tf_op jit(solution)/shard_map/rows_cross/ppermute | solution.py:334
  12.2 0.7 collective-permute-start.1
  12.9 0.1 collective-permute-done.7.f1
  13.0 1.3 %collective-permute-start.2 = (bf16[288,768]{1,0:T(8,128)(2,1)}, bf16[288,768]{1,0:T(8,128)(2,1)S(1)}, u32[]{:S(2)}, u32[]{:S(2)}) collective-permute-start(bf16[288,768]{1,0:T(8,128)(2,1)} %get-tuple-element.23), channel_id=1, source_target_pairs={{0,132},{1,133},{2,134},{3,135},{12,8},{13,9},{14,10},{15,11},{144... | collective-permute-start | bytes 1327112 | tf_op jit(solution)/shard_map/scatter/ppermute | solution.py:336
  14.2 2.5 %collective-permute-done.8.f2 = bf16[2,32,3072]{2,1,0:T(8,128)(2,1)S(1)} collective-permute-done((bf16[2,32,3072]{2,1,0:T(8,128)(2,1)}, bf16[2,32,3072]{2,1,0:T(8,128)(2,1)S(1)}, u32[]{:S(2)}, u32[]{:S(2)}) %collective-permute-start.8) | collective-permute-done | bytes 393248 | tf_op jit(solution)/shard_map/rows_cross/ppermute | solution.py:334
  16.8 4.1 %collective-permute-done.9.f3 = bf16[2,32,3072]{2,1,0:T(8,128)(2,1)S(1)} collective-permute-done((bf16[2,32,3072]{2,1,0:T(8,128)(2,1)}, bf16[2,32,3072]{2,1,0:T(8,128)(2,1)S(1)}, u32[]{:S(2)}, u32[]{:S(2)}) %collective-permute-start.9) | collective-permute-done | bytes 393248 | tf_op jit(solution)/shard_map/rows_cross/ppermute | solution.py:334
  20.9 0.0 copy-done.2
  20.9 1.0 copy-done
  21.9 1.0 norm_rows.1.r0
  22.9 3.5 %collective-permute-start.10 = (bf16[256,3072]{1,0:T(8,128)(2,1)S(1)}, bf16[256,3072]{1,0:T(8,128)(2,1)S(1)}, u32[]{:S(2)}, u32[]{:S(2)}) collective-permute-start(bf16[256,3072]{1,0:T(8,128)(2,1)S(1)} %norm_rows.1.r0), channel_id=1, source_target_pairs={{0,32},{1,9},{2,34},{3,11},{4,36},{5,13},{6,38},{7,15},{128,160},{... | collective-permute-start | bytes 4718600 | tf_op jit(solution)/shard_map/rows_line/ppermute | solution.py:341
  26.4 2.5 %collective-permute-start.11 = (bf16[256,3072]{1,0:T(8,128)(2,1)S(1)}, bf16[256,3072]{1,0:T(8,128)(2,1)S(1)}, u32[]{:S(2)}, u32[]{:S(2)}) collective-permute-start(bf16[256,3072]{1,0:T(8,128)(2,1)S(1)} %norm_rows.1.r0), channel_id=1, source_target_pairs={{0,96},{1,25},{2,98},{3,27},{4,100},{5,29},{6,102},{7,31},{128,224... | collective-permute-start | bytes 4718600 | tf_op jit(solution)/shard_map/rows_line/ppermute | solution.py:341
  28.9 0.0 collective-permute-done.q1
  28.9 1.4 %collective-permute-start.12 = (bf16[256,3072]{1,0:T(8,128)(2,1)S(1)}, bf16[256,3072]{1,0:T(8,128)(2,1)S(1)}, u32[]{:S(2)}, u32[]{:S(2)}) collective-permute-start(bf16[256,3072]{1,0:T(8,128)(2,1)S(1)} %norm_rows.1.r0), channel_id=1, source_target_pairs={{0,64},{1,17},{2,66},{3,19},{4,68},{5,21},{6,70},{7,23},{128,192},... | collective-permute-start | bytes 4718600 | tf_op jit(solution)/shard_map/rows_line/ppermute | solution.py:341
  30.3 0.0 collective-permute-done.1.q2
  30.3 7.4 %collective-permute-done.2.q3 = bf16[288,768]{1,0:T(8,128)(2,1)S(1)} collective-permute-done((bf16[288,768]{1,0:T(8,128)(2,1)}, bf16[288,768]{1,0:T(8,128)(2,1)S(1)}, u32[]{:S(2)}, u32[]{:S(2)}) %collective-permute-start.2) | collective-permute-done | bytes 442400 | tf_op jit(solution)/shard_map/scatter/ppermute | solution.py:336
  37.7 0.0 copy-done.1
  37.7 0.0 copy-done.5
  37.7 0.8 choose_quarter.1.refs_2_
  38.5 0.1 collective-permute-start.3
  38.6 3.2 %collective-permute-start.5 = (bf16[288,768]{1,0:T(8,128)(2,1)S(1)}, bf16[288,768]{1,0:T(8,128)(2,1)S(1)}, u32[]{:S(2)}, u32[]{:S(2)}) collective-permute-start(bf16[288,768]{1,0:T(8,128)(2,1)S(1)} %choose_quarter.1.refs_2_), channel_id=1, source_target_pairs={{0,134},{1,135},{2,0},{3,1},{4,2},{5,3},{6,4},{7,5},{128,6},{129,7... | collective-permute-start | bytes 1327112 | tf_op jit(solution)/shard_map/ring/ppermute | solution.py:349
  41.8 8.8 %collective-permute-done.3.refs_4_ = bf16[288,768]{1,0:T(8,128)(2,1)S(1)} collective-permute-done((bf16[288,768]{1,0:T(8,128)(2,1)S(1)}, bf16[288,768]{1,0:T(8,128)(2,1)S(1)}, u32[]{:S(2)}, u32[]{:S(2)}) %collective-permute-start.3) | collective-permute-done | bytes 442400 | tf_op jit(solution)/shard_map/ring/ppermute | solution.py:349
  50.7 0.0 collective-permute-start.4
  50.7 0.0 collective-permute-done.5.refs_6_
  50.7 3.2 %collective-permute-start.6 = (bf16[288,768]{1,0:T(8,128)(2,1)S(1)}, bf16[288,768]{1,0:T(8,128)(2,1)S(1)}, u32[]{:S(2)}, u32[]{:S(2)}) collective-permute-start(bf16[288,768]{1,0:T(8,128)(2,1)S(1)} %collective-permute-done.5.refs_6_), channel_id=1, source_target_pairs={{0,134},{1,135},{2,0},{3,1},{4,2},{5,3},{6,4},{7,5},{128,6},{129,7... | collective-permute-start | bytes 1327112 | tf_op jit(solution)/shard_map/ring/ppermute | solution.py:349
  53.9 0.0 collective-permute-done.10.r1
  53.9 0.0 collective-permute-start.16
  53.9 9.8 %collective-permute-done.11.r2 = bf16[256,3072]{1,0:T(8,128)(2,1)S(1)} collective-permute-done((bf16[256,3072]{1,0:T(8,128)(2,1)S(1)}, bf16[256,3072]{1,0:T(8,128)(2,1)S(1)}, u32[]{:S(2)}, u32[]{:S(2)}) %collective-permute-start.11) | collective-permute-done | bytes 1572896 | tf_op jit(solution)/shard_map/rows_line/ppermute | solution.py:341
  63.8 0.0 collective-permute-start.17
  63.8 1.8 %collective-permute-done.12.r3 = bf16[256,3072]{1,0:T(8,128)(2,1)S(1)} collective-permute-done((bf16[256,3072]{1,0:T(8,128)(2,1)S(1)}, bf16[256,3072]{1,0:T(8,128)(2,1)S(1)}, u32[]{:S(2)}, u32[]{:S(2)}) %collective-permute-start.12) | collective-permute-done | bytes 1572896 | tf_op jit(solution)/shard_map/rows_line/ppermute | solution.py:341
  65.5 0.0 collective-permute-start.18
  65.5 0.4 stack_rows.1.refs_1_.rows
  66.0 0.0 copy-start.3
  66.0 0.0 copy-start.4
  66.0 0.0 collective-permute-done.4.refs_8_
  66.0 0.0 collective-permute-done.6.refs_10_
  66.0 0.6 collective-permute-start.19
  66.6 0.3 collective-permute-start.20
  66.9 0.0 collective-permute-done.16.refs_3_
  66.9 0.8 collective-permute-start.15
  67.7 0.0 collective-permute-done.17.refs_5_
  67.7 1.9 %collective-permute-start.13 = (bf16[288,768]{1,0:T(8,128)(2,1)S(1)}, bf16[288,768]{1,0:T(8,128)(2,1)S(1)}, u32[]{:S(2)}, u32[]{:S(2)}) collective-permute-start(bf16[288,768]{1,0:T(8,128)(2,1)S(1)} %collective-permute-done.4.refs_8_), channel_id=1, source_target_pairs={{0,2},{1,3},{2,4},{3,5},{4,6},{5,7},{6,128},{7,129},{128,130},{129... | collective-permute-start | bytes 1327112 | tf_op jit(solution)/shard_map/ring/ppermute | solution.py:349
  69.6 0.0 collective-permute-done.18.refs_7_
  69.6 3.2 %collective-permute-start.14 = (bf16[288,768]{1,0:T(8,128)(2,1)S(1)}, bf16[288,768]{1,0:T(8,128)(2,1)S(1)}, u32[]{:S(2)}, u32[]{:S(2)}) collective-permute-start(bf16[288,768]{1,0:T(8,128)(2,1)S(1)} %collective-permute-done.6.refs_10_), channel_id=1, source_target_pairs={{0,134},{1,135},{2,0},{3,1},{4,2},{5,3},{6,4},{7,5},{128,6},{129,7... | collective-permute-start | bytes 1327112 | tf_op jit(solution)/shard_map/ring/ppermute | solution.py:349
  72.8 0.0 collective-permute-done.19.refs_9_
  72.8 0.0 collective-permute-done.20.refs_11_
  72.8 7.8 %project.1.refs_8_ = f32[2,32,4,8,768]{4,3,2,1,0:T(8,128)S(1)} custom-call(s32[7]{0:T(128)S(1)} %copy-done.1, bf16[1024,3072]{1,0:T(8,128)(2,1)S(1)} %stack_rows.1.refs_1_.rows, bf16[288,768]{1,0:T(8,128)(2,1)S(1)} %choose_quarter.1.refs_2_, bf16[288,768]{1,0:T(8,128)(2,1)S(1)} %collective-permute-done.16.refs_3_, ...), custom_call_target="tpu_custom_call" | custom-call | tf_op jit(solution)/shard_map/project/pallas_call | solution.py:224
  80.6 0.0 collective-permute-done.15.refs_4_
  80.6 2.3 %collective-permute-done.13.refs_0_ = bf16[288,768]{1,0:T(8,128)(2,1)S(1)} collective-permute-done((bf16[288,768]{1,0:T(8,128)(2,1)S(1)}, bf16[288,768]{1,0:T(8,128)(2,1)S(1)}, u32[]{:S(2)}, u32[]{:S(2)}) %collective-permute-start.13) | collective-permute-done | bytes 442400 | tf_op jit(solution)/shard_map/ring/ppermute | solution.py:349
  83.0 0.4 collective-permute-done.14.refs_2_
  83.3 0.0 collective-permute-start.21
  83.3 0.5 collective-permute-start.22
  83.9 0.0 collective-permute-start.23
  83.9 1.3 %collective-permute-done.21.refs_1_ = bf16[288,768]{1,0:T(8,128)(2,1)S(1)} collective-permute-done((bf16[288,768]{1,0:T(8,128)(2,1)S(1)}, bf16[288,768]{1,0:T(8,128)(2,1)S(1)}, u32[]{:S(2)}, u32[]{:S(2)}) %collective-permute-start.21) | collective-permute-done | bytes 442400 | tf_op jit(solution)/shard_map/swap/ppermute | solution.py:345
  85.1 0.6 collective-permute-done.22.refs_3_
  85.8 0.6 collective-permute-done.23.refs_5_
  86.4 0.0 copy-done.4
  86.4 8.7 %project_attend.1 = bf16[16,64,384]{2,1,0:T(8,128)(2,1)S(1)} custom-call(s32[7]{0:T(128)S(1)} %copy-done.1, bf16[1024,3072]{1,0:T(8,128)(2,1)S(1)} %stack_rows.1.refs_1_.rows, bf16[288,768]{1,0:T(8,128)(2,1)S(1)} %collective-permute-done.13.refs_0_, bf16[288,768]{1,0:T(8,128)(2,1)S(1)} %collective-permute-done.21.refs_1_, ...), custom_call_target="tpu_custom_call" | custom-call | tf_op jit(solution)/shard_map/project_attend/pallas_call | solution.py:284
  95.1 20.4 %all_to_all.5.recv_ref = bf16[16,64,384]{2,1,0:T(8,128)(2,1)S(1)} all-to-all(bf16[16,64,384]{2,1,0:T(8,128)(2,1)S(1)} %project_attend.1), channel_id=1, replica_groups=mesh['dp'=2,'seq'=16,'fsdp'=8] {'seq'}, dimensions={0} | all-to-all | bytes 1572864 | tf_op jit(solution)/shard_map/heads_back/all_to_all | solution.py:366
  115.4 1.5 %assemble_heads.1 = bf16[1,2,128,1536]{3,2,1,0:T(8,128)(2,1)} custom-call(s32[7]{0:T(128)S(1)} %copy-done.1, bf16[16,64,384]{2,1,0:T(8,128)(2,1)S(1)} %all_to_all.5.recv_ref), custom_call_target="tpu_custom_call" | custom-call | tf_op jit(solution)/shard_map/assemble_heads/pallas_call | solution.py:314
  (5 shorter events, 0.0 us)
Async XLA Ops:
  0.6 20.3 %copy-start.2 = (f32[3072]{0:T(1024)S(1)}, f32[3072]{0:T(1024)}, u32[]{:S(2)}) copy-start(f32[3072]{0:T(1024)} %param.8) | copy-start | bytes 36868
  4.7 8.2 %collective-permute-start.7 = (bf16[2,32,3072]{2,1,0:T(8,128)(2,1)}, bf16[2,32,3072]{2,1,0:T(8,128)(2,1)S(1)}, u32[]{:S(2)}, u32[]{:S(2)}) collective-permute-start(bf16[2,32,3072]{2,1,0:T(8,128)(2,1)} %get-tuple-element.25), channel_id=1, source_target_pairs={{0,8},{1,33},{2,10},{3,35},{4,12},{5,37},{6,14},{7,39},{128,136},{... | collective-permute-start | bytes 1179656 | tf_op jit(solution)/shard_map/rows_cross/ppermute | solution.py:334
  6.4 22.6 %collective-permute-start = (bf16[288,768]{1,0:T(8,128)(2,1)}, bf16[288,768]{1,0:T(8,128)(2,1)S(1)}, u32[]{:S(2)}, u32[]{:S(2)}) collective-permute-start(bf16[288,768]{1,0:T(8,128)(2,1)} %get-tuple-element.21), channel_id=1, source_target_pairs={{0,4},{1,5},{2,6},{3,7},{12,136},{13,137},{14,138},{15,139},{144,1... | collective-permute-start | bytes 1327112 | tf_op jit(solution)/shard_map/scatter/ppermute | solution.py:336
  7.1 9.7 %collective-permute-start.8 = (bf16[2,32,3072]{2,1,0:T(8,128)(2,1)}, bf16[2,32,3072]{2,1,0:T(8,128)(2,1)S(1)}, u32[]{:S(2)}, u32[]{:S(2)}) collective-permute-start(bf16[2,32,3072]{2,1,0:T(8,128)(2,1)} %get-tuple-element.26), channel_id=1, source_target_pairs={{0,16},{1,65},{2,18},{3,67},{4,20},{5,69},{6,22},{7,71},{128,144},... | collective-permute-start | bytes 1179656 | tf_op jit(solution)/shard_map/rows_cross/ppermute | solution.py:334
  10.4 10.4 %collective-permute-start.9 = (bf16[2,32,3072]{2,1,0:T(8,128)(2,1)}, bf16[2,32,3072]{2,1,0:T(8,128)(2,1)S(1)}, u32[]{:S(2)}, u32[]{:S(2)}) collective-permute-start(bf16[2,32,3072]{2,1,0:T(8,128)(2,1)} %get-tuple-element.27), channel_id=1, source_target_pairs={{0,24},{1,97},{2,26},{3,99},{4,28},{5,101},{6,30},{7,103},{128,152... | collective-permute-start | bytes 1179656 | tf_op jit(solution)/shard_map/rows_cross/ppermute | solution.py:334
  12.2 18.1 %collective-permute-start.1 = (bf16[288,768]{1,0:T(8,128)(2,1)}, bf16[288,768]{1,0:T(8,128)(2,1)S(1)}, u32[]{:S(2)}, u32[]{:S(2)}) collective-permute-start(bf16[288,768]{1,0:T(8,128)(2,1)} %get-tuple-element.22), channel_id=1, source_target_pairs={{64,128},{65,129},{66,130},{67,131},{76,140},{77,141},{78,142},{79... | collective-permute-start | bytes 1327112 | tf_op jit(solution)/shard_map/scatter/ppermute | solution.py:336
  13.0 24.7 %collective-permute-start.2 = (bf16[288,768]{1,0:T(8,128)(2,1)}, bf16[288,768]{1,0:T(8,128)(2,1)S(1)}, u32[]{:S(2)}, u32[]{:S(2)}) collective-permute-start(bf16[288,768]{1,0:T(8,128)(2,1)} %get-tuple-element.23), channel_id=1, source_target_pairs={{0,132},{1,133},{2,134},{3,135},{12,8},{13,9},{14,10},{15,11},{144... | collective-permute-start | bytes 1327112 | tf_op jit(solution)/shard_map/scatter/ppermute | solution.py:336
  20.9 1.0 copy-start
  21.9 15.8 %copy-start.1 = (s32[7]{0:T(128)S(1)}, s32[7]{0:T(128)}, u32[]{:S(2)}) copy-start(s32[7]{0:T(128)} %stack.31.where.refs_0_) | copy-start | bytes 88
  21.9 15.8 %copy-start.5 = (bf16[288,768]{1,0:T(8,128)(2,1)S(1)}, bf16[288,768]{1,0:T(8,128)(2,1)}, u32[]{:S(2)}) copy-start(bf16[288,768]{1,0:T(8,128)(2,1)} %get-tuple-element.20.q0) | copy-start | bytes 1327108
  22.9 31.0 %collective-permute-start.10 = (bf16[256,3072]{1,0:T(8,128)(2,1)S(1)}, bf16[256,3072]{1,0:T(8,128)(2,1)S(1)}, u32[]{:S(2)}, u32[]{:S(2)}) collective-permute-start(bf16[256,3072]{1,0:T(8,128)(2,1)S(1)} %norm_rows.1.r0), channel_id=1, source_target_pairs={{0,32},{1,9},{2,34},{3,11},{4,36},{5,13},{6,38},{7,15},{128,160},{... | collective-permute-start | bytes 4718600 | tf_op jit(solution)/shard_map/rows_line/ppermute | solution.py:341
  26.4 37.3 %collective-permute-start.11 = (bf16[256,3072]{1,0:T(8,128)(2,1)S(1)}, bf16[256,3072]{1,0:T(8,128)(2,1)S(1)}, u32[]{:S(2)}, u32[]{:S(2)}) collective-permute-start(bf16[256,3072]{1,0:T(8,128)(2,1)S(1)} %norm_rows.1.r0), channel_id=1, source_target_pairs={{0,96},{1,25},{2,98},{3,27},{4,100},{5,29},{6,102},{7,31},{128,224... | collective-permute-start | bytes 4718600 | tf_op jit(solution)/shard_map/rows_line/ppermute | solution.py:341
  28.9 36.6 %collective-permute-start.12 = (bf16[256,3072]{1,0:T(8,128)(2,1)S(1)}, bf16[256,3072]{1,0:T(8,128)(2,1)S(1)}, u32[]{:S(2)}, u32[]{:S(2)}) collective-permute-start(bf16[256,3072]{1,0:T(8,128)(2,1)S(1)} %norm_rows.1.r0), channel_id=1, source_target_pairs={{0,64},{1,17},{2,66},{3,19},{4,68},{5,21},{6,70},{7,23},{128,192},... | collective-permute-start | bytes 4718600 | tf_op jit(solution)/shard_map/rows_line/ppermute | solution.py:341
  38.5 12.2 %collective-permute-start.3 = (bf16[288,768]{1,0:T(8,128)(2,1)S(1)}, bf16[288,768]{1,0:T(8,128)(2,1)S(1)}, u32[]{:S(2)}, u32[]{:S(2)}) collective-permute-start(bf16[288,768]{1,0:T(8,128)(2,1)S(1)} %choose_quarter.1.refs_2_), channel_id=1, source_target_pairs={{0,2},{1,3},{2,4},{3,5},{4,6},{5,7},{6,128},{7,129},{128,130},{129... | collective-permute-start | bytes 1327112 | tf_op jit(solution)/shard_map/ring/ppermute | solution.py:349
  38.6 12.1 %collective-permute-start.5 = (bf16[288,768]{1,0:T(8,128)(2,1)S(1)}, bf16[288,768]{1,0:T(8,128)(2,1)S(1)}, u32[]{:S(2)}, u32[]{:S(2)}) collective-permute-start(bf16[288,768]{1,0:T(8,128)(2,1)S(1)} %choose_quarter.1.refs_2_), channel_id=1, source_target_pairs={{0,134},{1,135},{2,0},{3,1},{4,2},{5,3},{6,4},{7,5},{128,6},{129,7... | collective-permute-start | bytes 1327112 | tf_op jit(solution)/shard_map/ring/ppermute | solution.py:349
  50.7 15.3 %collective-permute-start.4 = (bf16[288,768]{1,0:T(8,128)(2,1)S(1)}, bf16[288,768]{1,0:T(8,128)(2,1)S(1)}, u32[]{:S(2)}, u32[]{:S(2)}) collective-permute-start(bf16[288,768]{1,0:T(8,128)(2,1)S(1)} %collective-permute-done.3.refs_4_), channel_id=1, source_target_pairs={{0,2},{1,3},{2,4},{3,5},{4,6},{5,7},{6,128},{7,129},{128,130},{129... | collective-permute-start | bytes 1327112 | tf_op jit(solution)/shard_map/ring/ppermute | solution.py:349
  50.7 15.3 %collective-permute-start.6 = (bf16[288,768]{1,0:T(8,128)(2,1)S(1)}, bf16[288,768]{1,0:T(8,128)(2,1)S(1)}, u32[]{:S(2)}, u32[]{:S(2)}) collective-permute-start(bf16[288,768]{1,0:T(8,128)(2,1)S(1)} %collective-permute-done.5.refs_6_), channel_id=1, source_target_pairs={{0,134},{1,135},{2,0},{3,1},{4,2},{5,3},{6,4},{7,5},{128,6},{129,7... | collective-permute-start | bytes 1327112 | tf_op jit(solution)/shard_map/ring/ppermute | solution.py:349
  53.9 13.0 %collective-permute-start.16 = (bf16[288,768]{1,0:T(8,128)(2,1)S(1)}, bf16[288,768]{1,0:T(8,128)(2,1)S(1)}, u32[]{:S(2)}, u32[]{:S(2)}) collective-permute-start(bf16[288,768]{1,0:T(8,128)(2,1)S(1)} %choose_quarter.1.refs_2_), channel_id=1, source_target_pairs={{0,1},{1,0},{2,3},{3,2},{4,5},{5,4},{6,7},{7,6},{128,129},{129,128... | collective-permute-start | bytes 1327112 | tf_op jit(solution)/shard_map/swap/ppermute | solution.py:345
  63.8 3.9 %collective-permute-start.17 = (bf16[288,768]{1,0:T(8,128)(2,1)S(1)}, bf16[288,768]{1,0:T(8,128)(2,1)S(1)}, u32[]{:S(2)}, u32[]{:S(2)}) collective-permute-start(bf16[288,768]{1,0:T(8,128)(2,1)S(1)} %collective-permute-done.3.refs_4_), channel_id=1, source_target_pairs={{0,1},{1,0},{2,3},{3,2},{4,5},{5,4},{6,7},{7,6},{128,129},{129,128... | collective-permute-start | bytes 1327112 | tf_op jit(solution)/shard_map/swap/ppermute | solution.py:345
  65.5 4.0 %collective-permute-start.18 = (bf16[288,768]{1,0:T(8,128)(2,1)S(1)}, bf16[288,768]{1,0:T(8,128)(2,1)S(1)}, u32[]{:S(2)}, u32[]{:S(2)}) collective-permute-start(bf16[288,768]{1,0:T(8,128)(2,1)S(1)} %collective-permute-done.5.refs_6_), channel_id=1, source_target_pairs={{0,1},{1,0},{2,3},{3,2},{4,5},{5,4},{6,7},{7,6},{128,129},{129,128... | collective-permute-start | bytes 1327112 | tf_op jit(solution)/shard_map/swap/ppermute | solution.py:345
  66.0 20.4 %copy-start.3 = (f32[128]{0:T(128)S(1)}, f32[128]{0:T(128)}, u32[]{:S(2)}) copy-start(f32[128]{0:T(128)} %param.12) | copy-start | bytes 1540
  66.0 20.4 %copy-start.4 = (f32[128]{0:T(128)S(1)}, f32[128]{0:T(128)}, u32[]{:S(2)}) copy-start(f32[128]{0:T(128)} %param.13) | copy-start | bytes 1540
  66.0 6.8 %collective-permute-start.19 = (bf16[288,768]{1,0:T(8,128)(2,1)S(1)}, bf16[288,768]{1,0:T(8,128)(2,1)S(1)}, u32[]{:S(2)}, u32[]{:S(2)}) collective-permute-start(bf16[288,768]{1,0:T(8,128)(2,1)S(1)} %collective-permute-done.4.refs_8_), channel_id=1, source_target_pairs={{0,1},{1,0},{2,3},{3,2},{4,5},{5,4},{6,7},{7,6},{128,129},{129,128... | collective-permute-start | bytes 1327112 | tf_op jit(solution)/shard_map/swap/ppermute | solution.py:345
  66.6 6.2 %collective-permute-start.20 = (bf16[288,768]{1,0:T(8,128)(2,1)S(1)}, bf16[288,768]{1,0:T(8,128)(2,1)S(1)}, u32[]{:S(2)}, u32[]{:S(2)}) collective-permute-start(bf16[288,768]{1,0:T(8,128)(2,1)S(1)} %collective-permute-done.6.refs_10_), channel_id=1, source_target_pairs={{0,1},{1,0},{2,3},{3,2},{4,5},{5,4},{6,7},{7,6},{128,129},{129,128... | collective-permute-start | bytes 1327112 | tf_op jit(solution)/shard_map/swap/ppermute | solution.py:345
  66.9 13.7 %collective-permute-start.15 = (bf16[288,768]{1,0:T(8,128)(2,1)S(1)}, bf16[288,768]{1,0:T(8,128)(2,1)S(1)}, u32[]{:S(2)}, u32[]{:S(2)}) collective-permute-start(bf16[288,768]{1,0:T(8,128)(2,1)S(1)} %choose_quarter.1.refs_2_), channel_id=1, source_target_pairs={{0,56},{1,57},{2,58},{3,59},{4,60},{5,61},{6,62},{7,63},{128,184},... | collective-permute-start | bytes 1327112 | tf_op jit(solution)/shard_map/partner/ppermute | solution.py:353
  67.7 15.3 %collective-permute-start.13 = (bf16[288,768]{1,0:T(8,128)(2,1)S(1)}, bf16[288,768]{1,0:T(8,128)(2,1)S(1)}, u32[]{:S(2)}, u32[]{:S(2)}) collective-permute-start(bf16[288,768]{1,0:T(8,128)(2,1)S(1)} %collective-permute-done.4.refs_8_), channel_id=1, source_target_pairs={{0,2},{1,3},{2,4},{3,5},{4,6},{5,7},{6,128},{7,129},{128,130},{129... | collective-permute-start | bytes 1327112 | tf_op jit(solution)/shard_map/ring/ppermute | solution.py:349
  69.6 13.8 %collective-permute-start.14 = (bf16[288,768]{1,0:T(8,128)(2,1)S(1)}, bf16[288,768]{1,0:T(8,128)(2,1)S(1)}, u32[]{:S(2)}, u32[]{:S(2)}) collective-permute-start(bf16[288,768]{1,0:T(8,128)(2,1)S(1)} %collective-permute-done.6.refs_10_), channel_id=1, source_target_pairs={{0,134},{1,135},{2,0},{3,1},{4,2},{5,3},{6,4},{7,5},{128,6},{129,7... | collective-permute-start | bytes 1327112 | tf_op jit(solution)/shard_map/ring/ppermute | solution.py:349
  83.3 1.8 %collective-permute-start.21 = (bf16[288,768]{1,0:T(8,128)(2,1)S(1)}, bf16[288,768]{1,0:T(8,128)(2,1)S(1)}, u32[]{:S(2)}, u32[]{:S(2)}) collective-permute-start(bf16[288,768]{1,0:T(8,128)(2,1)S(1)} %collective-permute-done.13.refs_0_), channel_id=1, source_target_pairs={{0,1},{1,0},{2,3},{3,2},{4,5},{5,4},{6,7},{7,6},{128,129},{129,128... | collective-permute-start | bytes 1327112 | tf_op jit(solution)/shard_map/swap/ppermute | solution.py:345
  83.3 2.4 %collective-permute-start.22 = (bf16[288,768]{1,0:T(8,128)(2,1)S(1)}, bf16[288,768]{1,0:T(8,128)(2,1)S(1)}, u32[]{:S(2)}, u32[]{:S(2)}) collective-permute-start(bf16[288,768]{1,0:T(8,128)(2,1)S(1)} %collective-permute-done.14.refs_2_), channel_id=1, source_target_pairs={{0,1},{1,0},{2,3},{3,2},{4,5},{5,4},{6,7},{7,6},{128,129},{129,128... | collective-permute-start | bytes 1327112 | tf_op jit(solution)/shard_map/swap/ppermute | solution.py:345
  83.9 2.5 %collective-permute-start.23 = (bf16[288,768]{1,0:T(8,128)(2,1)S(1)}, bf16[288,768]{1,0:T(8,128)(2,1)S(1)}, u32[]{:S(2)}, u32[]{:S(2)}) collective-permute-start(bf16[288,768]{1,0:T(8,128)(2,1)S(1)} %collective-permute-done.15.refs_4_), channel_id=1, source_target_pairs={{0,1},{1,0},{2,3},{3,2},{4,5},{5,4},{6,7},{7,6},{128,129},{129,128... | collective-permute-start | bytes 1327112 | tf_op jit(solution)/shard_map/swap/ppermute | solution.py:345

commit v7 on v6

--- a/solution.py
+++ b/solution.py
@@ -242,9 +242,9 @@
 
 
 def attend_kernel(where, rows, *refs):
-    pieces, (qg_ref, kg_ref, before, out_ref, weights, total, found) = refs[:6], refs[6:]
+    pieces, (qg_ref, kg_ref, before, out_ref, weights, total, found) = refs[:4], refs[4:]
     total[...] = before[...]
-    for turn, offset in enumerate((-3, 3, 4)):
+    for turn, offset in enumerate((-3, 3)):
         add_products(where, rows, weights, turn, offset, pieces[2 * turn], pieces[2 * turn + 1], total, False)
 
     @pl.when(where[0] >= 0)
@@ -286,7 +286,7 @@
         in_specs=[pl.BlockSpec(memory_space=pltpu.SMEM)] + [vmem] * (4 + len(pieces)),
         out_specs=vmem,
         scratch_shapes=[
-            pltpu.VMEM((3, 3, 256, quarter), jnp.bfloat16),
+            pltpu.VMEM((2, 3, 256, quarter), jnp.bfloat16),
             pltpu.VMEM((2, 32, 4, 8, 768), jnp.float32),
             pltpu.VMEM((32, 4, 8, 384), jnp.float32),
         ],
@@ -360,7 +360,8 @@
     early = swapped(part) + swapped(up1) + swapped(down1) + swapped(up2) + swapped(down2)
     total = project(where, rows, (0, -1, 1, -2, 2), early)
     up3, down3, half_turn, total = lax.optimization_barrier((up3, down3, half_turn, total))
-    late = swapped(up3) + swapped(down3) + swapped(half_turn)
+    total = project(where, rows, (4,), swapped(half_turn), (total,))
+    late = swapped(up3) + swapped(down3)
     output = attend(where, rows, late, query_gain, key_gain, total)
     with jax.named_scope("heads_back"):
         received = lax.all_to_all(output, "seq", split_axis=0, concat_axis=0, tiled=True)

time: 118 us -> 118 us (level)
  waiting for transfers between devices: 39.8 us -> 38.5 us
    pallas_call x1 -> x2, Pallas kernels: 7.83 us -> 9.92 us  [project(): pl.pallas_call(lambda *refs: project_kernel(offsets, *refs), in_specs=[pl...]
    pallas_call x1, Pallas kernels: 8.65 us -> 7.37 us  [attend(): pl.pallas_call(attend_kernel, in_specs=[pl.BlockSpec(memory_space=pltpu.S...]
    ppermute x8, waiting for transfers between devices: 2.56 us -> 1.3 us  [swapped(): return (piece, lax.ppermute(piece, AXES, swap_perm()))]
  transfers between devices with their start and end apart: 24 -> 24, of which waited for: 12 -> 10; matrix products, arithmetic and copies ran while one was open for 0% -> 0% of each run, Pallas kernels for 9% -> 10%
where the time goes in v7:
time: 118 us; the launch traced here: 116 us
  waiting for transfers between devices  38.5 us (33%)
  starting transfers between devices  30.6 us (26%)
  Pallas kernels  25.2 us (21%)
  blocking collectives  20.4 us (17%)
  local copies, waits for them, and re-layouts  1.62 us (1%)
    all_to_all x1, blocking collectives, shards(): lax.all_to_all(output, 'seq', split_axis=0, concat_axis=0, tiled=True)  20.4 us
    ppermute x3, waiting for transfers between devices, shards(): lax.ppermute(home, AXES, line_perm(s))  11.6 us
    ppermute x3, waiting for transfers between devices, onward(): lax.ppermute(up, AXES, ring_perm(1))  11.2 us
    pallas_call x2, Pallas kernels, project(): pl.pallas_call(lambda *refs: project_kernel(offsets, *refs), in_specs=[pl...  9.92 us
    ppermute x3, starting transfers between devices, onward(): lax.ppermute(down, AXES, ring_perm(-1))  9.65 us
    ppermute x3, starting transfers between devices, shards(): lax.ppermute(home, AXES, line_perm(s))  7.4 us
    pallas_call x1, Pallas kernels, attend(): pl.pallas_call(attend_kernel, in_specs=[pl.BlockSpec(memory_space=pltpu.S...  7.37 us
    ppermute x3, waiting for transfers between devices, shards(): lax.ppermute(q, AXES, scatter_perm(r))  7.36 us
  transfers between devices with their start and end apart: 24, of which 10 were waited for; matrix products, arithmetic and copies ran while one was open for 0% of the time, Pallas kernels for 10%

profile of v7, /device:TPU:8, one launch (start us, length us, event | category | flops | bytes accessed | tf_op | source)
XLA Modules:
  0.0 116.5 jit_solution(13221093254748223018)
XLA Ops:
  0.0 0.6 stack.31.where.refs_0_
  0.6 4.1 %prepare.1 = (bf16[2,32,3072]{2,1,0:T(8,128)(2,1)}, bf16[2,32,3072]{2,1,0:T(8,128)(2,1)}, bf16[2,32,3072]{2,1,0:T(8,128)(2,1)}, bf16[2,32,3072]{2,1,0:T(8,128)(2...) custom-call(s32[7]{0:T(128)} %stack.31.where.refs_0_, ...), custom_call_target="tpu_custom_call" | custom-call | tf_op jit(solution)/shard_map/prepare/pallas_call | solution.py:99
  4.7 1.7 %collective-permute-start.7 = (bf16[2,32,3072]{2,1,0:T(8,128)(2,1)}, bf16[2,32,3072]{2,1,0:T(8,128)(2,1)S(1)}, u32[]{:S(2)}, u32[]{:S(2)}) collective-permute-start(bf16[2,32,3072]{2,1,0:T(8,128)(2,1)} %get-tuple-element.25), channel_id=1, source_target_pairs={{0,8},{1,33},{2,10},{3,35},{4,12},{5,37},{6,14},{7,39},{128,136},{... | collective-permute-start | bytes 1179656 | tf_op jit(solution)/shard_map/rows_cross/ppermute | solution.py:334
  6.4 0.7 collective-permute-start
  7.1 3.4 %collective-permute-start.8 = (bf16[2,32,3072]{2,1,0:T(8,128)(2,1)}, bf16[2,32,3072]{2,1,0:T(8,128)(2,1)S(1)}, u32[]{:S(2)}, u32[]{:S(2)}) collective-permute-start(bf16[2,32,3072]{2,1,0:T(8,128)(2,1)} %get-tuple-element.26), channel_id=1, source_target_pairs={{0,16},{1,65},{2,18},{3,67},{4,20},{5,69},{6,22},{7,71},{128,144},... | collective-permute-start | bytes 1179656 | tf_op jit(solution)/shard_map/rows_cross/ppermute | solution.py:334
  10.4 1.8 %collective-permute-start.9 = (bf16[2,32,3072]{2,1,0:T(8,128)(2,1)}, bf16[2,32,3072]{2,1,0:T(8,128)(2,1)S(1)}, u32[]{:S(2)}, u32[]{:S(2)}) collective-permute-start(bf16[2,32,3072]{2,1,0:T(8,128)(2,1)} %get-tuple-element.27), channel_id=1, source_target_pairs={{0,24},{1,97},{2,26},{3,99},{4,28},{5,101},{6,30},{7,103},{128,152... | collective-permute-start | bytes 1179656 | tf_op jit(solution)/shard_map/rows_cross/ppermute | solution.py:334
  12.2 0.7 collective-permute-start.1
  12.9 0.1 collective-permute-done.7.f1
  13.0 1.3 %collective-permute-start.2 = (bf16[288,768]{1,0:T(8,128)(2,1)}, bf16[288,768]{1,0:T(8,128)(2,1)S(1)}, u32[]{:S(2)}, u32[]{:S(2)}) collective-permute-start(bf16[288,768]{1,0:T(8,128)(2,1)} %get-tuple-element.23), channel_id=1, source_target_pairs={{0,132},{1,133},{2,134},{3,135},{12,8},{13,9},{14,10},{15,11},{144... | collective-permute-start | bytes 1327112 | tf_op jit(solution)/shard_map/scatter/ppermute | solution.py:336
  14.2 2.5 %collective-permute-done.8.f2 = bf16[2,32,3072]{2,1,0:T(8,128)(2,1)S(1)} collective-permute-done((bf16[2,32,3072]{2,1,0:T(8,128)(2,1)}, bf16[2,32,3072]{2,1,0:T(8,128)(2,1)S(1)}, u32[]{:S(2)}, u32[]{:S(2)}) %collective-permute-start.8) | collective-permute-done | bytes 393248 | tf_op jit(solution)/shard_map/rows_cross/ppermute | solution.py:334
  16.8 4.1 %collective-permute-done.9.f3 = bf16[2,32,3072]{2,1,0:T(8,128)(2,1)S(1)} collective-permute-done((bf16[2,32,3072]{2,1,0:T(8,128)(2,1)}, bf16[2,32,3072]{2,1,0:T(8,128)(2,1)S(1)}, u32[]{:S(2)}, u32[]{:S(2)}) %collective-permute-start.9) | collective-permute-done | bytes 393248 | tf_op jit(solution)/shard_map/rows_cross/ppermute | solution.py:334
  20.9 0.0 copy-done.2
  20.9 1.0 copy-done
  21.9 1.0 norm_rows.1.r0
  22.9 3.5 %collective-permute-start.10 = (bf16[256,3072]{1,0:T(8,128)(2,1)S(1)}, bf16[256,3072]{1,0:T(8,128)(2,1)S(1)}, u32[]{:S(2)}, u32[]{:S(2)}) collective-permute-start(bf16[256,3072]{1,0:T(8,128)(2,1)S(1)} %norm_rows.1.r0), channel_id=1, source_target_pairs={{0,32},{1,9},{2,34},{3,11},{4,36},{5,13},{6,38},{7,15},{128,160},{... | collective-permute-start | bytes 4718600 | tf_op jit(solution)/shard_map/rows_line/ppermute | solution.py:341
  26.4 2.5 %collective-permute-start.11 = (bf16[256,3072]{1,0:T(8,128)(2,1)S(1)}, bf16[256,3072]{1,0:T(8,128)(2,1)S(1)}, u32[]{:S(2)}, u32[]{:S(2)}) collective-permute-start(bf16[256,3072]{1,0:T(8,128)(2,1)S(1)} %norm_rows.1.r0), channel_id=1, source_target_pairs={{0,96},{1,25},{2,98},{3,27},{4,100},{5,29},{6,102},{7,31},{128,224... | collective-permute-start | bytes 4718600 | tf_op jit(solution)/shard_map/rows_line/ppermute | solution.py:341
  28.9 0.0 collective-permute-done.q1
  28.9 1.4 %collective-permute-start.12 = (bf16[256,3072]{1,0:T(8,128)(2,1)S(1)}, bf16[256,3072]{1,0:T(8,128)(2,1)S(1)}, u32[]{:S(2)}, u32[]{:S(2)}) collective-permute-start(bf16[256,3072]{1,0:T(8,128)(2,1)S(1)} %norm_rows.1.r0), channel_id=1, source_target_pairs={{0,64},{1,17},{2,66},{3,19},{4,68},{5,21},{6,70},{7,23},{128,192},... | collective-permute-start | bytes 4718600 | tf_op jit(solution)/shard_map/rows_line/ppermute | solution.py:341
  30.3 0.0 collective-permute-done.1.q2
  30.3 7.4 %collective-permute-done.2.q3 = bf16[288,768]{1,0:T(8,128)(2,1)S(1)} collective-permute-done((bf16[288,768]{1,0:T(8,128)(2,1)}, bf16[288,768]{1,0:T(8,128)(2,1)S(1)}, u32[]{:S(2)}, u32[]{:S(2)}) %collective-permute-start.2) | collective-permute-done | bytes 442400 | tf_op jit(solution)/shard_map/scatter/ppermute | solution.py:336
  37.7 0.0 copy-done.1
  37.7 0.0 copy-done.5
  37.7 0.8 choose_quarter.1.refs_2_
  38.5 0.1 collective-permute-start.3
  38.6 3.2 %collective-permute-start.5 = (bf16[288,768]{1,0:T(8,128)(2,1)S(1)}, bf16[288,768]{1,0:T(8,128)(2,1)S(1)}, u32[]{:S(2)}, u32[]{:S(2)}) collective-permute-start(bf16[288,768]{1,0:T(8,128)(2,1)S(1)} %choose_quarter.1.refs_2_), channel_id=1, source_target_pairs={{0,134},{1,135},{2,0},{3,1},{4,2},{5,3},{6,4},{7,5},{128,6},{129,7... | collective-permute-start | bytes 1327112 | tf_op jit(solution)/shard_map/ring/ppermute | solution.py:349
  41.8 8.8 %collective-permute-done.3.refs_4_ = bf16[288,768]{1,0:T(8,128)(2,1)S(1)} collective-permute-done((bf16[288,768]{1,0:T(8,128)(2,1)S(1)}, bf16[288,768]{1,0:T(8,128)(2,1)S(1)}, u32[]{:S(2)}, u32[]{:S(2)}) %collective-permute-start.3) | collective-permute-done | bytes 442400 | tf_op jit(solution)/shard_map/ring/ppermute | solution.py:349
  50.7 0.0 collective-permute-start.4
  50.7 0.0 collective-permute-done.5.refs_6_
  50.7 3.2 %collective-permute-start.6 = (bf16[288,768]{1,0:T(8,128)(2,1)S(1)}, bf16[288,768]{1,0:T(8,128)(2,1)S(1)}, u32[]{:S(2)}, u32[]{:S(2)}) collective-permute-start(bf16[288,768]{1,0:T(8,128)(2,1)S(1)} %collective-permute-done.5.refs_6_), channel_id=1, source_target_pairs={{0,134},{1,135},{2,0},{3,1},{4,2},{5,3},{6,4},{7,5},{128,6},{129,7... | collective-permute-start | bytes 1327112 | tf_op jit(solution)/shard_map/ring/ppermute | solution.py:349
  53.9 0.0 collective-permute-done.10.r1
  53.9 0.0 collective-permute-start.16
  53.9 9.8 %collective-permute-done.11.r2 = bf16[256,3072]{1,0:T(8,128)(2,1)S(1)} collective-permute-done((bf16[256,3072]{1,0:T(8,128)(2,1)S(1)}, bf16[256,3072]{1,0:T(8,128)(2,1)S(1)}, u32[]{:S(2)}, u32[]{:S(2)}) %collective-permute-start.11) | collective-permute-done | bytes 1572896 | tf_op jit(solution)/shard_map/rows_line/ppermute | solution.py:341
  63.8 0.0 collective-permute-start.17
  63.8 1.8 %collective-permute-done.12.r3 = bf16[256,3072]{1,0:T(8,128)(2,1)S(1)} collective-permute-done((bf16[256,3072]{1,0:T(8,128)(2,1)S(1)}, bf16[256,3072]{1,0:T(8,128)(2,1)S(1)}, u32[]{:S(2)}, u32[]{:S(2)}) %collective-permute-start.12) | collective-permute-done | bytes 1572896 | tf_op jit(solution)/shard_map/rows_line/ppermute | solution.py:341
  65.5 0.0 collective-permute-start.18
  65.5 0.4 stack_rows.1.refs_1_.rows
  66.0 0.0 collective-permute-done.4.refs_8_
  66.0 0.0 collective-permute-done.6.refs_10_
  66.0 0.6 collective-permute-start.19
  66.6 0.3 collective-permute-start.20
  66.9 0.0 collective-permute-done.16.refs_3_
  66.9 0.8 collective-permute-start.15
  67.6 0.0 collective-permute-done.17.refs_5_
  67.6 1.9 %collective-permute-start.13 = (bf16[288,768]{1,0:T(8,128)(2,1)S(1)}, bf16[288,768]{1,0:T(8,128)(2,1)S(1)}, u32[]{:S(2)}, u32[]{:S(2)}) collective-permute-start(bf16[288,768]{1,0:T(8,128)(2,1)S(1)} %collective-permute-done.4.refs_8_), channel_id=1, source_target_pairs={{0,2},{1,3},{2,4},{3,5},{4,6},{5,7},{6,128},{7,129},{128,130},{129... | collective-permute-start | bytes 1327112 | tf_op jit(solution)/shard_map/ring/ppermute | solution.py:349
  69.6 0.0 collective-permute-done.18.refs_7_
  69.6 3.2 %collective-permute-start.14 = (bf16[288,768]{1,0:T(8,128)(2,1)S(1)}, bf16[288,768]{1,0:T(8,128)(2,1)S(1)}, u32[]{:S(2)}, u32[]{:S(2)}) collective-permute-start(bf16[288,768]{1,0:T(8,128)(2,1)S(1)} %collective-permute-done.6.refs_10_), channel_id=1, source_target_pairs={{0,134},{1,135},{2,0},{3,1},{4,2},{5,3},{6,4},{7,5},{128,6},{129,7... | collective-permute-start | bytes 1327112 | tf_op jit(solution)/shard_map/ring/ppermute | solution.py:349
  72.7 0.0 collective-permute-done.19.refs_9_
  72.8 0.0 collective-permute-done.20.refs_11_
  72.8 7.8 %project.2.refs_4_ = f32[2,32,4,8,768]{4,3,2,1,0:T(8,128)S(1)} custom-call(s32[7]{0:T(128)S(1)} %copy-done.1, bf16[1024,3072]{1,0:T(8,128)(2,1)S(1)} %stack_rows.1.refs_1_.rows, bf16[288,768]{1,0:T(8,128)(2,1)S(1)} %choose_quarter.1.refs_2_, bf16[288,768]{1,0:T(8,128)(2,1)S(1)} %collective-permute-done.16.refs_3_, ...), custom_call_target="tpu_custom_call" | custom-call | tf_op jit(solution)/shard_map/project/pallas_call | solution.py:224
  80.6 0.0 copy-start.3
  80.6 0.0 copy-start.4
  80.6 0.0 collective-permute-done.15.refs_2_
  80.6 2.3 %collective-permute-done.13.refs_0_ = bf16[288,768]{1,0:T(8,128)(2,1)S(1)} collective-permute-done((bf16[288,768]{1,0:T(8,128)(2,1)S(1)}, bf16[288,768]{1,0:T(8,128)(2,1)S(1)}, u32[]{:S(2)}, u32[]{:S(2)}) %collective-permute-start.13) | collective-permute-done | bytes 442400 | tf_op jit(solution)/shard_map/ring/ppermute | solution.py:349
  82.9 0.4 collective-permute-done.14.refs_2_
  83.3 0.0 collective-permute-start.23
  83.3 0.5 collective-permute-start.21
  83.8 0.0 collective-permute-start.22
  83.8 1.3 %collective-permute-done.23.refs_3_ = bf16[288,768]{1,0:T(8,128)(2,1)S(1)} collective-permute-done((bf16[288,768]{1,0:T(8,128)(2,1)S(1)}, bf16[288,768]{1,0:T(8,128)(2,1)S(1)}, u32[]{:S(2)}, u32[]{:S(2)}) %collective-permute-start.23) | collective-permute-done | bytes 442400 | tf_op jit(solution)/shard_map/swap/ppermute | solution.py:345
  85.1 2.1 %project.3.refs_6_ = f32[2,32,4,8,768]{4,3,2,1,0:T(8,128)S(1)} custom-call(s32[7]{0:T(128)S(1)} %copy-done.1, bf16[1024,3072]{1,0:T(8,128)(2,1)S(1)} %stack_rows.1.refs_1_.rows, bf16[288,768]{1,0:T(8,128)(2,1)S(1)} %collective-permute-done.15.refs_2_, bf16[288,768]{1,0:T(8,128)(2,1)S(1)} %collective-permute-done.23.refs_3_, ...), custom_call_target="tpu_custom_call", output_to_operand_aliasing={{}: (4, {})} | custom-call | tf_op jit(solution)/shard_map/project/pallas_call | solution.py:224
  87.2 0.0 collective-permute-done.21.refs_1_
  87.2 0.0 collective-permute-done.22.refs_3_
  87.3 7.4 %project_attend.1 = bf16[16,64,384]{2,1,0:T(8,128)(2,1)S(1)} custom-call(s32[7]{0:T(128)S(1)} %copy-done.1, bf16[1024,3072]{1,0:T(8,128)(2,1)S(1)} %stack_rows.1.refs_1_.rows, bf16[288,768]{1,0:T(8,128)(2,1)S(1)} %collective-permute-done.13.refs_0_, bf16[288,768]{1,0:T(8,128)(2,1)S(1)} %collective-permute-done.21.refs_1_, ...), custom_call_target="tpu_custom_call" | custom-call | tf_op jit(solution)/shard_map/project_attend/pallas_call | solution.py:284
  94.6 20.4 %all_to_all.5.recv_ref = bf16[16,64,384]{2,1,0:T(8,128)(2,1)S(1)} all-to-all(bf16[16,64,384]{2,1,0:T(8,128)(2,1)S(1)} %project_attend.1), channel_id=1, replica_groups=mesh['dp'=2,'seq'=16,'fsdp'=8] {'seq'}, dimensions={0} | all-to-all | bytes 1572864 | tf_op jit(solution)/shard_map/heads_back/all_to_all | solution.py:367
  115.0 1.5 %assemble_heads.1 = bf16[1,2,128,1536]{3,2,1,0:T(8,128)(2,1)} custom-call(s32[7]{0:T(128)S(1)} %copy-done.1, bf16[16,64,384]{2,1,0:T(8,128)(2,1)S(1)} %all_to_all.5.recv_ref), custom_call_target="tpu_custom_call" | custom-call | tf_op jit(solution)/shard_map/assemble_heads/pallas_call | solution.py:314
  (6 shorter events, 0.0 us)
Async XLA Ops:
  0.6 20.3 %copy-start.2 = (f32[3072]{0:T(1024)S(1)}, f32[3072]{0:T(1024)}, u32[]{:S(2)}) copy-start(f32[3072]{0:T(1024)} %param.8) | copy-start | bytes 36868
  4.7 8.2 %collective-permute-start.7 = (bf16[2,32,3072]{2,1,0:T(8,128)(2,1)}, bf16[2,32,3072]{2,1,0:T(8,128)(2,1)S(1)}, u32[]{:S(2)}, u32[]{:S(2)}) collective-permute-start(bf16[2,32,3072]{2,1,0:T(8,128)(2,1)} %get-tuple-element.25), channel_id=1, source_target_pairs={{0,8},{1,33},{2,10},{3,35},{4,12},{5,37},{6,14},{7,39},{128,136},{... | collective-permute-start | bytes 1179656 | tf_op jit(solution)/shard_map/rows_cross/ppermute | solution.py:334
  6.4 22.6 %collective-permute-start = (bf16[288,768]{1,0:T(8,128)(2,1)}, bf16[288,768]{1,0:T(8,128)(2,1)S(1)}, u32[]{:S(2)}, u32[]{:S(2)}) collective-permute-start(bf16[288,768]{1,0:T(8,128)(2,1)} %get-tuple-element.21), channel_id=1, source_target_pairs={{0,4},{1,5},{2,6},{3,7},{12,136},{13,137},{14,138},{15,139},{144,1... | collective-permute-start | bytes 1327112 | tf_op jit(solution)/shard_map/scatter/ppermute | solution.py:336
  7.1 9.7 %collective-permute-start.8 = (bf16[2,32,3072]{2,1,0:T(8,128)(2,1)}, bf16[2,32,3072]{2,1,0:T(8,128)(2,1)S(1)}, u32[]{:S(2)}, u32[]{:S(2)}) collective-permute-start(bf16[2,32,3072]{2,1,0:T(8,128)(2,1)} %get-tuple-element.26), channel_id=1, source_target_pairs={{0,16},{1,65},{2,18},{3,67},{4,20},{5,69},{6,22},{7,71},{128,144},... | collective-permute-start | bytes 1179656 | tf_op jit(solution)/shard_map/rows_cross/ppermute | solution.py:334
  10.4 10.4 %collective-permute-start.9 = (bf16[2,32,3072]{2,1,0:T(8,128)(2,1)}, bf16[2,32,3072]{2,1,0:T(8,128)(2,1)S(1)}, u32[]{:S(2)}, u32[]{:S(2)}) collective-permute-start(bf16[2,32,3072]{2,1,0:T(8,128)(2,1)} %get-tuple-element.27), channel_id=1, source_target_pairs={{0,24},{1,97},{2,26},{3,99},{4,28},{5,101},{6,30},{7,103},{128,152... | collective-permute-start | bytes 1179656 | tf_op jit(solution)/shard_map/rows_cross/ppermute | solution.py:334
  12.2 18.1 %collective-permute-start.1 = (bf16[288,768]{1,0:T(8,128)(2,1)}, bf16[288,768]{1,0:T(8,128)(2,1)S(1)}, u32[]{:S(2)}, u32[]{:S(2)}) collective-permute-start(bf16[288,768]{1,0:T(8,128)(2,1)} %get-tuple-element.22), channel_id=1, source_target_pairs={{64,128},{65,129},{66,130},{67,131},{76,140},{77,141},{78,142},{79... | collective-permute-start | bytes 1327112 | tf_op jit(solution)/shard_map/scatter/ppermute | solution.py:336
  13.0 24.7 %collective-permute-start.2 = (bf16[288,768]{1,0:T(8,128)(2,1)}, bf16[288,768]{1,0:T(8,128)(2,1)S(1)}, u32[]{:S(2)}, u32[]{:S(2)}) collective-permute-start(bf16[288,768]{1,0:T(8,128)(2,1)} %get-tuple-element.23), channel_id=1, source_target_pairs={{0,132},{1,133},{2,134},{3,135},{12,8},{13,9},{14,10},{15,11},{144... | collective-permute-start | bytes 1327112 | tf_op jit(solution)/shard_map/scatter/ppermute | solution.py:336
  20.9 1.0 copy-start
  21.9 15.8 %copy-start.1 = (s32[7]{0:T(128)S(1)}, s32[7]{0:T(128)}, u32[]{:S(2)}) copy-start(s32[7]{0:T(128)} %stack.31.where.refs_0_) | copy-start | bytes 88
  21.9 15.8 %copy-start.5 = (bf16[288,768]{1,0:T(8,128)(2,1)S(1)}, bf16[288,768]{1,0:T(8,128)(2,1)}, u32[]{:S(2)}) copy-start(bf16[288,768]{1,0:T(8,128)(2,1)} %get-tuple-element.20.q0) | copy-start | bytes 1327108
  22.9 31.0 %collective-permute-start.10 = (bf16[256,3072]{1,0:T(8,128)(2,1)S(1)}, bf16[256,3072]{1,0:T(8,128)(2,1)S(1)}, u32[]{:S(2)}, u32[]{:S(2)}) collective-permute-start(bf16[256,3072]{1,0:T(8,128)(2,1)S(1)} %norm_rows.1.r0), channel_id=1, source_target_pairs={{0,32},{1,9},{2,34},{3,11},{4,36},{5,13},{6,38},{7,15},{128,160},{... | collective-permute-start | bytes 4718600 | tf_op jit(solution)/shard_map/rows_line/ppermute | solution.py:341
  26.4 37.3 %collective-permute-start.11 = (bf16[256,3072]{1,0:T(8,128)(2,1)S(1)}, bf16[256,3072]{1,0:T(8,128)(2,1)S(1)}, u32[]{:S(2)}, u32[]{:S(2)}) collective-permute-start(bf16[256,3072]{1,0:T(8,128)(2,1)S(1)} %norm_rows.1.r0), channel_id=1, source_target_pairs={{0,96},{1,25},{2,98},{3,27},{4,100},{5,29},{6,102},{7,31},{128,224... | collective-permute-start | bytes 4718600 | tf_op jit(solution)/shard_map/rows_line/ppermute | solution.py:341
  28.9 36.6 %collective-permute-start.12 = (bf16[256,3072]{1,0:T(8,128)(2,1)S(1)}, bf16[256,3072]{1,0:T(8,128)(2,1)S(1)}, u32[]{:S(2)}, u32[]{:S(2)}) collective-permute-start(bf16[256,3072]{1,0:T(8,128)(2,1)S(1)} %norm_rows.1.r0), channel_id=1, source_target_pairs={{0,64},{1,17},{2,66},{3,19},{4,68},{5,21},{6,70},{7,23},{128,192},... | collective-permute-start | bytes 4718600 | tf_op jit(solution)/shard_map/rows_line/ppermute | solution.py:341
  38.5 12.2 %collective-permute-start.3 = (bf16[288,768]{1,0:T(8,128)(2,1)S(1)}, bf16[288,768]{1,0:T(8,128)(2,1)S(1)}, u32[]{:S(2)}, u32[]{:S(2)}) collective-permute-start(bf16[288,768]{1,0:T(8,128)(2,1)S(1)} %choose_quarter.1.refs_2_), channel_id=1, source_target_pairs={{0,2},{1,3},{2,4},{3,5},{4,6},{5,7},{6,128},{7,129},{128,130},{129... | collective-permute-start | bytes 1327112 | tf_op jit(solution)/shard_map/ring/ppermute | solution.py:349
  38.6 12.1 %collective-permute-start.5 = (bf16[288,768]{1,0:T(8,128)(2,1)S(1)}, bf16[288,768]{1,0:T(8,128)(2,1)S(1)}, u32[]{:S(2)}, u32[]{:S(2)}) collective-permute-start(bf16[288,768]{1,0:T(8,128)(2,1)S(1)} %choose_quarter.1.refs_2_), channel_id=1, source_target_pairs={{0,134},{1,135},{2,0},{3,1},{4,2},{5,3},{6,4},{7,5},{128,6},{129,7... | collective-permute-start | bytes 1327112 | tf_op jit(solution)/shard_map/ring/ppermute | solution.py:349
  50.7 15.3 %collective-permute-start.4 = (bf16[288,768]{1,0:T(8,128)(2,1)S(1)}, bf16[288,768]{1,0:T(8,128)(2,1)S(1)}, u32[]{:S(2)}, u32[]{:S(2)}) collective-permute-start(bf16[288,768]{1,0:T(8,128)(2,1)S(1)} %collective-permute-done.3.refs_4_), channel_id=1, source_target_pairs={{0,2},{1,3},{2,4},{3,5},{4,6},{5,7},{6,128},{7,129},{128,130},{129... | collective-permute-start | bytes 1327112 | tf_op jit(solution)/shard_map/ring/ppermute | solution.py:349
  50.7 15.3 %collective-permute-start.6 = (bf16[288,768]{1,0:T(8,128)(2,1)S(1)}, bf16[288,768]{1,0:T(8,128)(2,1)S(1)}, u32[]{:S(2)}, u32[]{:S(2)}) collective-permute-start(bf16[288,768]{1,0:T(8,128)(2,1)S(1)} %collective-permute-done.5.refs_6_), channel_id=1, source_target_pairs={{0,134},{1,135},{2,0},{3,1},{4,2},{5,3},{6,4},{7,5},{128,6},{129,7... | collective-permute-start | bytes 1327112 | tf_op jit(solution)/shard_map/ring/ppermute | solution.py:349
  53.9 12.9 %collective-permute-start.16 = (bf16[288,768]{1,0:T(8,128)(2,1)S(1)}, bf16[288,768]{1,0:T(8,128)(2,1)S(1)}, u32[]{:S(2)}, u32[]{:S(2)}) collective-permute-start(bf16[288,768]{1,0:T(8,128)(2,1)S(1)} %choose_quarter.1.refs_2_), channel_id=1, source_target_pairs={{0,1},{1,0},{2,3},{3,2},{4,5},{5,4},{6,7},{7,6},{128,129},{129,128... | collective-permute-start | bytes 1327112 | tf_op jit(solution)/shard_map/swap/ppermute | solution.py:345
  63.8 3.9 %collective-permute-start.17 = (bf16[288,768]{1,0:T(8,128)(2,1)S(1)}, bf16[288,768]{1,0:T(8,128)(2,1)S(1)}, u32[]{:S(2)}, u32[]{:S(2)}) collective-permute-start(bf16[288,768]{1,0:T(8,128)(2,1)S(1)} %collective-permute-done.3.refs_4_), channel_id=1, source_target_pairs={{0,1},{1,0},{2,3},{3,2},{4,5},{5,4},{6,7},{7,6},{128,129},{129,128... | collective-permute-start | bytes 1327112 | tf_op jit(solution)/shard_map/swap/ppermute | solution.py:345
  65.5 4.0 %collective-permute-start.18 = (bf16[288,768]{1,0:T(8,128)(2,1)S(1)}, bf16[288,768]{1,0:T(8,128)(2,1)S(1)}, u32[]{:S(2)}, u32[]{:S(2)}) collective-permute-start(bf16[288,768]{1,0:T(8,128)(2,1)S(1)} %collective-permute-done.5.refs_6_), channel_id=1, source_target_pairs={{0,1},{1,0},{2,3},{3,2},{4,5},{5,4},{6,7},{7,6},{128,129},{129,128... | collective-permute-start | bytes 1327112 | tf_op jit(solution)/shard_map/swap/ppermute | solution.py:345
  66.0 6.8 %collective-permute-start.19 = (bf16[288,768]{1,0:T(8,128)(2,1)S(1)}, bf16[288,768]{1,0:T(8,128)(2,1)S(1)}, u32[]{:S(2)}, u32[]{:S(2)}) collective-permute-start(bf16[288,768]{1,0:T(8,128)(2,1)S(1)} %collective-permute-done.4.refs_8_), channel_id=1, source_target_pairs={{0,1},{1,0},{2,3},{3,2},{4,5},{5,4},{6,7},{7,6},{128,129},{129,128... | collective-permute-start | bytes 1327112 | tf_op jit(solution)/shard_map/swap/ppermute | solution.py:345
  66.6 6.2 %collective-permute-start.20 = (bf16[288,768]{1,0:T(8,128)(2,1)S(1)}, bf16[288,768]{1,0:T(8,128)(2,1)S(1)}, u32[]{:S(2)}, u32[]{:S(2)}) collective-permute-start(bf16[288,768]{1,0:T(8,128)(2,1)S(1)} %collective-permute-done.6.refs_10_), channel_id=1, source_target_pairs={{0,1},{1,0},{2,3},{3,2},{4,5},{5,4},{6,7},{7,6},{128,129},{129,128... | collective-permute-start | bytes 1327112 | tf_op jit(solution)/shard_map/swap/ppermute | solution.py:345
  66.9 13.8 %collective-permute-start.15 = (bf16[288,768]{1,0:T(8,128)(2,1)S(1)}, bf16[288,768]{1,0:T(8,128)(2,1)S(1)}, u32[]{:S(2)}, u32[]{:S(2)}) collective-permute-start(bf16[288,768]{1,0:T(8,128)(2,1)S(1)} %choose_quarter.1.refs_2_), channel_id=1, source_target_pairs={{0,56},{1,57},{2,58},{3,59},{4,60},{5,61},{6,62},{7,63},{128,184},... | collective-permute-start | bytes 1327112 | tf_op jit(solution)/shard_map/partner/ppermute | solution.py:353
  67.6 15.3 %collective-permute-start.13 = (bf16[288,768]{1,0:T(8,128)(2,1)S(1)}, bf16[288,768]{1,0:T(8,128)(2,1)S(1)}, u32[]{:S(2)}, u32[]{:S(2)}) collective-permute-start(bf16[288,768]{1,0:T(8,128)(2,1)S(1)} %collective-permute-done.4.refs_8_), channel_id=1, source_target_pairs={{0,2},{1,3},{2,4},{3,5},{4,6},{5,7},{6,128},{7,129},{128,130},{129... | collective-permute-start | bytes 1327112 | tf_op jit(solution)/shard_map/ring/ppermute | solution.py:349
  69.6 13.8 %collective-permute-start.14 = (bf16[288,768]{1,0:T(8,128)(2,1)S(1)}, bf16[288,768]{1,0:T(8,128)(2,1)S(1)}, u32[]{:S(2)}, u32[]{:S(2)}) collective-permute-start(bf16[288,768]{1,0:T(8,128)(2,1)S(1)} %collective-permute-done.6.refs_10_), channel_id=1, source_target_pairs={{0,134},{1,135},{2,0},{3,1},{4,2},{5,3},{6,4},{7,5},{128,6},{129,7... | collective-permute-start | bytes 1327112 | tf_op jit(solution)/shard_map/ring/ppermute | solution.py:349
  80.6 6.7 %copy-start.3 = (f32[128]{0:T(128)S(1)}, f32[128]{0:T(128)}, u32[]{:S(2)}) copy-start(f32[128]{0:T(128)} %param.12) | copy-start | bytes 1540
  80.6 6.7 %copy-start.4 = (f32[128]{0:T(128)S(1)}, f32[128]{0:T(128)}, u32[]{:S(2)}) copy-start(f32[128]{0:T(128)} %param.13) | copy-start | bytes 1540
  83.3 1.8 %collective-permute-start.23 = (bf16[288,768]{1,0:T(8,128)(2,1)S(1)}, bf16[288,768]{1,0:T(8,128)(2,1)S(1)}, u32[]{:S(2)}, u32[]{:S(2)}) collective-permute-start(bf16[288,768]{1,0:T(8,128)(2,1)S(1)} %collective-permute-done.15.refs_2_), channel_id=1, source_target_pairs={{0,1},{1,0},{2,3},{3,2},{4,5},{5,4},{6,7},{7,6},{128,129},{129,128... | collective-permute-start | bytes 1327112 | tf_op jit(solution)/shard_map/swap/ppermute | solution.py:345
  83.3 3.9 %collective-permute-start.21 = (bf16[288,768]{1,0:T(8,128)(2,1)S(1)}, bf16[288,768]{1,0:T(8,128)(2,1)S(1)}, u32[]{:S(2)}, u32[]{:S(2)}) collective-permute-start(bf16[288,768]{1,0:T(8,128)(2,1)S(1)} %collective-permute-done.13.refs_0_), channel_id=1, source_target_pairs={{0,1},{1,0},{2,3},{3,2},{4,5},{5,4},{6,7},{7,6},{128,129},{129,128... | collective-permute-start | bytes 1327112 | tf_op jit(solution)/shard_map/swap/ppermute | solution.py:345
  83.8 3.4 %collective-permute-start.22 = (bf16[288,768]{1,0:T(8,128)(2,1)S(1)}, bf16[288,768]{1,0:T(8,128)(2,1)S(1)}, u32[]{:S(2)}, u32[]{:S(2)}) collective-permute-start(bf16[288,768]{1,0:T(8,128)(2,1)S(1)} %collective-permute-done.14.refs_2_), channel_id=1, source_target_pairs={{0,1},{1,0},{2,3},{3,2},{4,5},{5,4},{6,7},{7,6},{128,129},{129,128... | collective-permute-start | bytes 1327112 | tf_op jit(solution)/shard_map/swap/ppermute | solution.py:345
